TPU v7x, 128 devices: a whole 4x4x4 slice. The times are simulated.
128 devices in a mesh: expert: 64 (over y, x, z), seq: 2 (over core).
Axes of the slice: x: 4, y: 4, z: 4, core: 2. Of those that a mesh axis runs over, the one named last changes fastest.
Arguments:
- out_grad: bfloat16 [16384, 7168], P(('expert', 'seq')), may hold values from -6 to 6
- route_ids: int32 [16384, 8], P('expert'), may hold values from 0 to 255, all different within a row
- route_weights: float32 [16384, 8], P('expert'), may hold values from 0.2 to 1
- gate_pre: bfloat16 [64, 768, 1024], P('expert', None, 'seq'), may hold values from -5 to 5
- up_pre: bfloat16 [64, 768, 1024], P('expert', None, 'seq'), may hold values from -5 to 5
- w_gate: bfloat16 [64, 7168, 1024], P('expert', None, 'seq'), may hold values from -0.75 to 0.75
- w_up: bfloat16 [64, 7168, 1024], P('expert', None, 'seq'), may hold values from -0.75 to 0.75
- w_down: bfloat16 [64, 1024, 7168], P('expert', 'seq'), may hold values from -0.0078125 to 0.0078125
Outputs:
- in_grad: bfloat16 [16384, 7168], P(('expert', 'seq'))
- weight_grad: bfloat16 [16384, 8], P(('expert', 'seq'))
Inputs may be any that keep to these rules, and one draw needn't show every extreme that they name: `route_ids`: each row names 8 different experts; only experts below 64 are held in this window, the others are left to other windows.
All inputs are finite; a program needn't handle non-finite values.
Results may differ from a plain program's by a relative error of at most 0.0065.
Values may be sent and summed in bfloat16 or wider, within the bound.
No kernel may reach another device: no remote copies, remote signals or barrier semaphores. Data moves between devices by JAX's collectives and lax.ppermute only.
A program may use at most 192 MiB of HBM per device.

v0:
```python
import jax
import jax.numpy as jnp
from jax import lax
from jax.sharding import PartitionSpec as P


def silu_parts(value):
    sigma = jax.nn.sigmoid(value)
    return (value * sigma, sigma * (1.0 + value * (1.0 - sigma)))


def pair_tables(group_ids, experts, capacity):
    pair_count = group_ids.shape[0]
    fanout = group_ids.shape[1]
    assigned = group_ids.reshape(-1)
    one_hot = (assigned[:, None] == jnp.arange(experts, dtype=jnp.int32)[None, :]).astype(jnp.int32)
    earlier = jnp.cumsum(one_hot, axis=0) - one_hot
    position = jnp.sum(earlier * one_hot, axis=1)
    retained = (assigned < experts) & (position < capacity)
    slot_index = jnp.where(retained, assigned * capacity + position, experts * capacity)
    owner_row = jnp.arange(assigned.shape[0], dtype=jnp.int32) // fanout
    slot_rows = (
        jnp.full((experts * capacity + 1,), pair_count, jnp.int32).at[slot_index].set(owner_row)
    )
    return (
        slot_index.reshape(pair_count, fanout),
        slot_rows[: experts * capacity].reshape(experts, capacity),
    )


def combine_rows(flat_input, flat_score, indices, weights):
    total = jnp.zeros((indices.shape[0], flat_input.shape[1]), jnp.float32)
    for column in range(indices.shape[1]):
        total = total + weights[:, column : column + 1] * flat_input[indices[:, column]].astype(
            jnp.float32
        )
    return (total, flat_score[indices])


def on_device(out_grad, route_ids, route_weights, gate_pre, up_pre, w_gate, w_up, w_down):
    n_expert = lax.axis_size("expert")
    seq_at = lax.axis_index("seq")
    local_rows = out_grad.shape[0]
    width = out_grad.shape[1]
    exp_local = w_gate.shape[0]
    experts = exp_local * n_expert
    capacity = gate_pre.shape[1] // n_expert
    slot_index, slot_rows = pair_tables(route_ids, experts, capacity)
    group_grad = lax.all_gather(out_grad, "seq", axis=0, tiled=True)
    padded_grad = jnp.concatenate([group_grad, jnp.zeros((1, width), jnp.bfloat16)], axis=0)
    outgoing = padded_grad[slot_rows]
    received = lax.all_to_all(outgoing, "expert", split_axis=0, concat_axis=1, tiled=True)
    contract = (((1,), (1,)), ((), ()))
    slot_grad = received[0]
    hidden_grad = lax.dot_general(
        slot_grad, w_down[0], contract, preferred_element_type=jnp.float32
    )
    active, slope_val = silu_parts(gate_pre[0].astype(jnp.float32))
    up_part = up_pre[0].astype(jnp.float32)
    score_parts = [jnp.sum(hidden_grad * active * up_part, axis=1)]
    gate_diff = (hidden_grad * up_part * slope_val).astype(jnp.bfloat16)
    up_diff = (hidden_grad * active).astype(jnp.bfloat16)
    input_part = lax.dot_general(gate_diff, w_gate[0], contract, preferred_element_type=jnp.float32)
    input_part = input_part + lax.dot_general(
        up_diff, w_up[0], contract, preferred_element_type=jnp.float32
    )
    input_parts = [input_part]
    input_term = lax.optimization_barrier(jnp.stack(input_parts).astype(jnp.bfloat16)).astype(
        jnp.float32
    )
    score_term = lax.optimization_barrier(jnp.stack(score_parts).astype(jnp.bfloat16)).astype(
        jnp.float32
    )
    input_sum, score_sum = (
        lax.psum(input_term.astype(jnp.bfloat16), "seq").astype(jnp.float32),
        lax.psum(score_term.astype(jnp.bfloat16), "seq").astype(jnp.float32),
    )
    back_input, back_score = (
        lax.all_to_all(
            input_sum.astype(jnp.bfloat16), "expert", split_axis=1, concat_axis=0, tiled=True
        ),
        lax.all_to_all(
            score_sum.astype(jnp.bfloat16), "expert", split_axis=1, concat_axis=0, tiled=True
        ),
    )
    flat_input = jnp.concatenate(
        [back_input.reshape(experts * capacity, width), jnp.zeros((1, width), jnp.bfloat16)], axis=0
    )
    flat_score = jnp.concatenate(
        [back_score.reshape(experts * capacity), jnp.zeros((1,), jnp.bfloat16)], axis=0
    )
    own_slots = lax.dynamic_slice_in_dim(slot_index, seq_at * local_rows, local_rows, 0)
    own_weights = lax.dynamic_slice_in_dim(route_weights, seq_at * local_rows, local_rows, 0)
    total, scores = combine_rows(flat_input, flat_score, own_slots, own_weights)
    return (total.astype(jnp.bfloat16), scores)


def solution(mesh):
    in_specs = (
        P(("expert", "seq"), None),
        P("expert", None),
        P("expert", None),
        P("expert", None, "seq"),
        P("expert", None, "seq"),
        P("expert", None, "seq"),
        P("expert", None, "seq"),
        P("expert", "seq", None),
    )
    out_specs = (P(("expert", "seq"), None), P(("expert", "seq"), None))
    return jax.shard_map(
        on_device, mesh=mesh, in_specs=in_specs, out_specs=out_specs, check_vma=False
    )
```

profile of v0, /device:TPU:1, one launch (start us, length us, event | category | flops | bytes accessed | tf_op | source)
XLA Modules:
  0.0 895.8 jit_solution(11426256836971638184)
XLA Ops:
  7.2 0.7 all-gather.2.cloned.1.call-update
  7.9 0.1 copy.41
  8.6 18.1 %reduce-window.6 = s32[64,16,128]{2,1,0:T(8,128)S(1)} reduce-window(s32[64,16,128]{2,1,0:T(8,128)S(1)} %fusion.23, s32[]{:T(128)} %constant.19.clone.1), window={size=1x1x128 pad=0_0x0_0x127_0}, to_apply=%region_0.0 | reduce-window | flops 16646144 | bytes 1048580 | tf_op jit(solution)/shard_map/reduce-window
  26.8 0.2 slice.96
  27.0 0.4 copy.52
  27.4 0.2 reduce-window.9
  27.6 0.2 broadcast_add_fusion
  27.8 0.3 fusion.22
  28.1 8.0 scatter_custom_fusion
  36.4 4.4 concatenate.9
  40.8 22.1 %gather_fusion = bf16[768,7168]{1,0:T(8,128)(2,1)} fusion(bf16[257,7168]{1,0:T(8,128)(2,1)} %concatenate.9, s32[1024]{0:T(1024)S(1)} %pad_clamp_fusion.8), kind=kCustom, calls=%fused_computation | custom fusion | bytes 22023168 | tf_op jit(solution)/shard_map/gather | solution.py:51
  63.0 15.4 %reshape.145 = bf16[64,12,7168]{2,1,0:T(8,128)(2,1)} reshape(bf16[768,7168]{1,0:T(8,128)(2,1)} %gather_fusion) | data formatting | bytes 22020096 | tf_op jit(solution)/shard_map/gather | solution.py:51
  78.4 12.3 %all-to-all-start = ((bf16[64,12,7168]{2,1,0:T(8,128)(2,1)}), bf16[64,12,7168]{2,1,0:T(8,128)(2,1)}, u32[]{:S(2)}, u32[]{:S(2)}) async-start(bf16[64,12,7168]{2,1,0:T(8,128)(2,1)} %reshape.145), calls=%async_computation | async-start | bytes 29360128 | tf_op jit(solution)/shard_map/all_to_all | solution.py:52
  90.7 0.5 all-reduce.4.cloned.1.call-start
  91.2 0.3 copy.48
  91.5 0.3 copy-done.2
  91.8 0.3 copy.47
  92.1 241.4 %all-to-all-done = bf16[64,12,7168]{2,1,0:T(8,128)(2,1)} async-done(((bf16[64,12,7168]{2,1,0:T(8,128)(2,1)}), bf16[64,12,7168]{2,1,0:T(8,128)(2,1)}, u32[]{:S(2)}, u32[]{:S(2)}) %all-to-all-start) | async-done | bytes 11010080 | tf_op jit(solution)/shard_map/all_to_all | solution.py:52
  333.5 15.9 %squeeze.8 = bf16[768,7168]{1,0:T(8,128)(2,1)} reshape(bf16[64,12,7168]{2,1,0:T(8,128)(2,1)} %all-to-all-done) | data formatting | bytes 22020096 | tf_op jit(solution)/shard_map/squeeze | solution.py:54
  349.4 11.7 %fusion.8 = (bf16[768]{0:T(1024)(128)(2,1)S(1)}, f32[768,512]{0,1:T(8,128)S(1)}) fusion(bf16[1,768,512]{1,2,0:T(8,128)(2,1)S(1)} %copy.47, bf16[1,768,512]{1,2,0:T(8,128)(2,1)S(1)} %copy.48, bf16[768,7168]{1,0:T(8,128)(2,1)} %squeeze.8, bf16[1,512,7168]{2,1,0:T(8,128)(2,1)} %param.15), kind=kOutput, calls=%fused_computation.27 | convolution fusion | flops 5640682496 | bytes 21497344 | tf_op jit(solution)/shard_map/dot_general | solution.py:55
  361.1 1.1 copy-done.4
  362.2 13.8 %fusion.2 = f32[768,7168]{1,0:T(8,128)} fusion(bf16[1,7168,512]{2,1,0:T(8,128)(2,1)} %param.13, f32[768,512]{0,1:T(8,128)S(1)} %get-tuple-element.29, bf16[1,768,512]{1,2,0:T(8,128)(2,1)S(1)} %copy.47, bf16[1,768,512]{1,2,0:T(8,128)(2,1)S(1)} %copy.48), kind=kOutput, calls=%fused_computation.15 | convolution fusion | flops 5641863168 | bytes 32505856 | tf_op jit(solution)/shard_map/dot_general | solution.py:63
  376.0 15.6 %fusion = bf16[1,768,7168]{2,1,0:T(8,128)(2,1)} fusion(f32[768,7168]{1,0:T(8,128)} %fusion.2, bf16[1,7168,512]{2,1,0:T(8,128)(2,1)} %param.14, f32[768,512]{0,1:T(8,128)} %copy-done.4, bf16[1,768,512]{1,2,0:T(8,128)(2,1)S(1)} %copy.48), kind=kOutput, calls=%fused_computation.13 | convolution fusion | flops 5650907136 | bytes 42729472 | tf_op jit(solution)/shard_map/dot_general | solution.py:64
  391.8 6.3 psum.15
  398.1 0.6 copy.50
  398.8 12.4 %all-to-all-start.2 = ((bf16[1,64,12]{2,0,1:T(2,128)(2,1)}), bf16[1,64,12]{2,0,1:T(2,128)(2,1)S(1)}, u32[]{:S(2)}, u32[]{:S(2)}) async-start(bf16[1,64,12]{2,0,1:T(2,128)(2,1)} %copy.50), calls=%async_computation.2 | async-start | bytes 65536 | tf_op jit(solution)/shard_map/all_to_all | solution.py:82
  411.2 36.2 %all-reduce.4.cloned.1.call-done = bf16[1,768,7168]{2,1,0:T(8,128)(2,1)} async-done(((bf16[1,768,7168]{2,1,0:T(8,128)(2,1)}), bf16[1,768,7168]{2,1,0:T(8,128)(2,1)}) %all-reduce.4.cloned.1.call-update) | async-done | bytes 11010064 | tf_op jit(solution)/shard_map/psum | solution.py:75
  447.4 20.0 %copy.59 = bf16[1,768,7168]{2,0,1:T(2,128)(2,1)} copy(bf16[1,768,7168]{2,1,0:T(8,128)(2,1)} %all-reduce.4.cloned.1.call-done) | data formatting | bytes 22020096 | tf_op jit(solution)/shard_map/psum | solution.py:75
  467.3 0.5 broadcast.210
  467.9 65.5 %reduce.18 = bf16[768,7168]{1,0:T(8,128)(2,1)} reduce(bf16[768,1,7168]{2,1,0:T(2,128)(2,1)} %bitcast.82, bf16[]{:T(256)} %broadcast.210), dimensions={1}, to_apply=%bitcast.78.reduce_sub_computation | reduce | bytes 22020098
  533.4 15.9 %reshape.247 = bf16[64,2,43008]{2,1,0:T(2,128)(2,1)} reshape(bf16[768,7168]{1,0:T(8,128)(2,1)} %reduce.18) | data formatting | bytes 22020096
  549.2 10.4 %all-to-all-start.1 = ((bf16[64,2,43008]{2,1,0:T(2,128)(2,1)}), bf16[64,2,43008]{2,1,0:T(2,128)(2,1)}, u32[]{:S(2)}, u32[]{:S(2)}) async-start(bf16[64,2,43008]{2,1,0:T(2,128)(2,1)} %reshape.247), calls=%async_computation.1 | async-start | bytes 22020096 | tf_op jit(solution)/shard_map/all_to_all | solution.py:79
  559.9 0.4 fusion.24
  560.6 6.8 gather_fusion.9
  567.5 0.7 copy.51
  568.1 174.3 %all-to-all-done.1 = bf16[64,2,43008]{2,1,0:T(2,128)(2,1)} async-done(((bf16[64,2,43008]{2,1,0:T(2,128)(2,1)}), bf16[64,2,43008]{2,1,0:T(2,128)(2,1)}, u32[]{:S(2)}, u32[]{:S(2)}) %all-to-all-start.1) | async-done | bytes 11010080 | tf_op jit(solution)/shard_map/all_to_all | solution.py:79
  742.4 40.5 %reshape.248 = bf16[768,1,7168]{2,1,0:T(2,128)(2,1)} reshape(bf16[64,2,43008]{2,1,0:T(2,128)(2,1)} %all-to-all-done.1) | data formatting | bytes 22020096
  782.9 12.1 %copy.58 = bf16[1,768,7168]{2,1,0:T(8,128)(2,1)S(1)} copy(bf16[1,768,7168]{2,0,1:T(2,128)(2,1)} %bitcast.83) | data formatting | bytes 22020096
  794.9 5.1 concatenate.10
  800.1 9.0 %gather_fusion.8 = bf16[128,7168]{1,0:T(8,128)(2,1)S(1)} fusion(bf16[769,7168]{1,0:T(8,128)(2,1)} %concatenate.10, s32[1024]{0:T(1024)S(1)} %get-tuple-element.30), kind=kCustom, calls=%fused_computation.8 | custom fusion | bytes 3670528 | tf_op jit(solution)/shard_map/gather | solution.py:34
  809.1 10.2 %gather_fusion.7 = bf16[128,7168]{1,0:T(8,128)(2,1)} fusion(bf16[769,7168]{1,0:T(8,128)(2,1)} %concatenate.10, s32[1024]{0:T(1024)S(1)} %get-tuple-element.31), kind=kCustom, calls=%fused_computation.7 | custom fusion | bytes 3670528 | tf_op jit(solution)/shard_map/gather | solution.py:34
  819.2 10.7 %gather_fusion.6 = bf16[128,7168]{1,0:T(8,128)(2,1)} fusion(bf16[769,7168]{1,0:T(8,128)(2,1)} %concatenate.10, s32[1024]{0:T(1024)S(1)} %get-tuple-element.32), kind=kCustom, calls=%fused_computation.6 | custom fusion | bytes 3670528 | tf_op jit(solution)/shard_map/gather | solution.py:34
  829.9 10.2 %gather_fusion.5 = bf16[128,7168]{1,0:T(8,128)(2,1)} fusion(bf16[769,7168]{1,0:T(8,128)(2,1)} %concatenate.10, s32[1024]{0:T(1024)S(1)} %get-tuple-element.33), kind=kCustom, calls=%fused_computation.5 | custom fusion | bytes 3670528 | tf_op jit(solution)/shard_map/gather | solution.py:34
  840.1 10.2 %gather_fusion.4 = bf16[128,7168]{1,0:T(8,128)(2,1)} fusion(bf16[769,7168]{1,0:T(8,128)(2,1)} %concatenate.10, s32[1024]{0:T(1024)S(1)} %get-tuple-element.34), kind=kCustom, calls=%fused_computation.4 | custom fusion | bytes 3670528 | tf_op jit(solution)/shard_map/gather | solution.py:34
  850.3 10.4 %gather_fusion.3 = bf16[128,7168]{1,0:T(8,128)(2,1)} fusion(bf16[769,7168]{1,0:T(8,128)(2,1)} %concatenate.10, s32[1024]{0:T(1024)S(1)} %get-tuple-element.35), kind=kCustom, calls=%fused_computation.3 | custom fusion | bytes 3670528 | tf_op jit(solution)/shard_map/gather | solution.py:34
  860.7 10.2 %gather_fusion.2 = bf16[128,7168]{1,0:T(8,128)(2,1)} fusion(bf16[769,7168]{1,0:T(8,128)(2,1)} %concatenate.10, s32[1024]{0:T(1024)S(1)} %get-tuple-element.36), kind=kCustom, calls=%fused_computation.2 | custom fusion | bytes 3670528 | tf_op jit(solution)/shard_map/gather | solution.py:34
  870.8 10.2 %gather_fusion.1 = bf16[128,7168]{1,0:T(8,128)(2,1)} fusion(bf16[769,7168]{1,0:T(8,128)(2,1)} %concatenate.10, s32[1024]{0:T(1024)S(1)} %get-tuple-element.37), kind=kCustom, calls=%fused_computation.1 | custom fusion | bytes 3670528 | tf_op jit(solution)/shard_map/gather | solution.py:34
  881.1 7.7 add_convert_fusion.1
  (42 shorter events, 1.6 us)
Async XLA Ops:
  7.2 552.7 %copy-start = (f32[256,8]{0,1:T(8,128)S(1)}, f32[256,8]{0,1:T(8,128)}, u32[]{:S(2)}) copy-start(f32[256,8]{0,1:T(8,128)} %param.10) | copy-start | bytes 24580
  7.2 0.7 copy-start.3
  7.2 29.2 %all-gather.2.cloned.1.call-start = ((), (), s32[]{:S(2)}) async-start(), calls=%async_computation.3 | async-start | bytes 5505024 | tf_op jit(solution)/shard_map/all_gather | solution.py:49
  78.4 12.9 %copy-start.1 = (bf16[1,768,512]{2,1,0:T(8,128)(2,1)S(1)}, bf16[1,768,512]{2,1,0:T(8,128)(2,1)}, u32[]{:S(2)}) copy-start(bf16[1,768,512]{2,1,0:T(8,128)(2,1)} %param.11) | copy-start | bytes 2359300
  78.4 255.1 %all-to-all-start = ((bf16[64,12,7168]{2,1,0:T(8,128)(2,1)}), bf16[64,12,7168]{2,1,0:T(8,128)(2,1)}, u32[]{:S(2)}, u32[]{:S(2)}) async-start(bf16[64,12,7168]{2,1,0:T(8,128)(2,1)} %reshape.145), calls=%async_computation | async-start | bytes 29360128 | tf_op jit(solution)/shard_map/all_to_all | solution.py:52
  90.7 1.1 copy-start.2
  90.7 356.7 %all-reduce.4.cloned.1.call-start = ((), (), s32[]{:S(2)}) async-start(), calls=%async_computation.4 | async-start | bytes 22020096 | tf_op jit(solution)/shard_map/psum | solution.py:75
  361.1 1.1 copy-start.4
  398.8 150.5 %all-to-all-start.2 = ((bf16[1,64,12]{2,0,1:T(2,128)(2,1)}), bf16[1,64,12]{2,0,1:T(2,128)(2,1)S(1)}, u32[]{:S(2)}, u32[]{:S(2)}) async-start(bf16[1,64,12]{2,0,1:T(2,128)(2,1)} %copy.50), calls=%async_computation.2 | async-start | bytes 65536 | tf_op jit(solution)/shard_map/all_to_all | solution.py:82
  549.2 193.2 %all-to-all-start.1 = ((bf16[64,2,43008]{2,1,0:T(2,128)(2,1)}), bf16[64,2,43008]{2,1,0:T(2,128)(2,1)}, u32[]{:S(2)}, u32[]{:S(2)}) async-start(bf16[64,2,43008]{2,1,0:T(2,128)(2,1)} %reshape.247), calls=%async_computation.1 | async-start | bytes 22020096 | tf_op jit(solution)/shard_map/all_to_all | solution.py:79
Sparse Core Ops, SparseCore 0:
  9.7 19.2 all-gather.1
  391.8 55.5 all-reduce.3
where the time goes:
time: 906 us; the launch traced here: 896 us
  waiting for transfers between devices  453 us (50%)
  local copies, waits for them, and re-layouts  253 us (28%)
  other arithmetic  92.7 us (10%)
  matrix products  41.1 us (5%)
  starting transfers between devices  35.6 us (4%)
  between operations  14.6 us (2%)
    all_to_all x1, waiting for transfers between devices, on_device(): lax.all_to_all(outgoing, 'expert', split_axis=0, concat_axis=1, tiled=True)  241 us
    all_to_all x1, waiting for transfers between devices, on_device(): lax.all_to_all(input_sum.astype(jnp.bfloat16), 'expert', split_axis=1, co...  174 us
    gather x8, local copies, waits for them, and re-layouts, combine_rows(): flat_input[indices[:, column]].astype(jnp.float32)  81 us
    unnamed x18, local copies, waits for them, and re-layouts  71.7 us
    unnamed x1, other arithmetic  65.5 us
    gather x2, local copies, waits for them, and re-layouts, on_device(): outgoing = padded_grad[slot_rows]  37.5 us
    psum x1, waiting for transfers between devices, on_device(): lax.psum(input_term.astype(jnp.bfloat16), 'seq').astype(jnp.float32)  36.2 us
    psum x1, local copies, waits for them, and re-layouts, on_device(): lax.psum(input_term.astype(jnp.bfloat16), 'seq').astype(jnp.float32)  20 us
  transfers between devices with their start and end apart: 5, of which 3 were waited for; matrix products, arithmetic and copies ran while one was open for 16% of the time, Pallas kernels for 0%

commit v1 on v0

v1 whole, which is shorter than its diff:
```python
import jax
import jax.numpy as jnp
from jax import lax
from jax.experimental import pallas as pl
from jax.experimental.pallas import tpu as pltpu
from jax.sharding import PartitionSpec as P

F32 = jnp.float32
BF16 = jnp.bfloat16
NT = (((1,), (1,)), ((), ()))
MAIN = 8
REST = 4
LIMIT = 40 * 1024 * 1024


def iota(shape, dim):
    return lax.broadcasted_iota(jnp.int32, shape, dim)


def flag(cond):
    return jnp.where(cond, 1.0, 0.0).astype(F32)


def dot(a, b):
    return jnp.dot(a, b, preferred_element_type=F32)


def params():
    return pltpu.CompilerParams(vmem_limit_bytes=LIMIT)


def swap(value):
    return lax.ppermute(value, "seq", [(0, 1), (1, 0)])


def dispatch_kernel(at_ref, ids_ref, own_ref, other_ref, out_ref, g_ref, pa_ref, pb_ref):
    step = pl.program_id(0)
    experts = out_ref.shape[0] // MAIN
    tokens = g_ref.shape[0]
    half = tokens // 2
    rows = experts * MAIN
    tile = out_ref.shape[1]
    quarter = g_ref.shape[1] // 2

    @pl.when(step == 0)
    def _():
        at = at_ref[0]
        g_ref[pl.ds(pl.multiple_of(at * half, half), half), :] = own_ref[...]
        g_ref[pl.ds(pl.multiple_of((1 - at) * half, half), half), :] = other_ref[...]
        names = iota((experts, tokens), 0)
        member = jnp.zeros((experts, tokens), F32)
        for k in range(ids_ref.shape[0]):
            member = member + flag(names == ids_ref[k : k + 1, :])
        before = flag(iota((tokens, tokens), 0) < iota((tokens, tokens), 1)).astype(BF16)
        place = dot(member.astype(BF16), before)
        place = jnp.where(member > 0.5, place, -1.0).astype(BF16)
        spread = flag(iota((rows, experts), 0) // MAIN == iota((rows, experts), 1)).astype(BF16)
        wide = dot(spread, place).astype(jnp.int32)
        row = iota((rows, tokens), 0)
        pa_ref[...] = flag(wide == row % MAIN).astype(BF16)
        rest = flag(wide == MAIN + row % REST)
        upper = (row // REST) % 2
        pb_ref[:, :tokens] = jnp.where(upper == 0, rest, 0.0).astype(BF16)
        pb_ref[:, tokens:] = jnp.where(upper == 1, rest, 0.0).astype(BF16)

    steps_a = g_ref.shape[1] // tile

    @pl.when(step < steps_a)
    def _():
        cols = pl.ds(pl.multiple_of(step * tile, 128), tile)
        out_ref[...] = dot(pa_ref[...], g_ref[:, cols]).astype(BF16)

    @pl.when(step >= steps_a)
    def _():
        low = (step - steps_a) * tile
        first = g_ref[:, pl.ds(pl.multiple_of(low, 128), tile)]
        second = g_ref[:, pl.ds(pl.multiple_of(low + quarter, 128), tile)]
        out_ref[...] = (
            dot(pb_ref[:, :tokens], first) + dot(pb_ref[:, tokens:], second)
        ).astype(BF16)


def dispatch(at, ids_t, out_grad, other, experts):
    local, width = out_grad.shape
    part = width // 2
    tile = part // 4
    rows = experts * MAIN
    return pl.pallas_call(
        dispatch_kernel,
        grid_spec=pltpu.PrefetchScalarGridSpec(
            num_scalar_prefetch=1,
            grid=(6,),
            in_specs=[
                pl.BlockSpec(ids_t.shape, lambda j, at: (0, 0)),
                pl.BlockSpec((local, part), lambda j, at: (0, at[0])),
                pl.BlockSpec((local, part), lambda j, at: (0, 0)),
            ],
            out_specs=pl.BlockSpec((rows, tile), lambda j, at: (0, j)),
            scratch_shapes=[
                pltpu.VMEM((2 * local, part), BF16),
                pltpu.VMEM((rows, 2 * local), BF16),
                pltpu.VMEM((rows, 4 * local), BF16),
            ],
        ),
        out_shape=jax.ShapeDtypeStruct((rows, 6 * tile), BF16),
        compiler_params=params(),
        cost_estimate=pl.CostEstimate(flops=2 * 10**9, bytes_accessed=8 * 10**6, transcendentals=0),
        name="dispatch",
    )(at, ids_t, out_grad, other)


def hidden_kernel(at_ref, x_ref, w_ref, out_ref):
    step = pl.program_id(0)
    tile = x_ref.shape[0]
    part = w_ref.shape[1]
    quarter = part // 2
    units = w_ref.shape[0]
    main = lax.dot_general(x_ref[:, :part], w_ref[...], NT, preferred_element_type=F32)
    out_ref[pl.ds(pl.multiple_of(step * tile, tile), tile), :] = main
    rest = x_ref[:, part:]
    low = lax.dot_general(rest, w_ref[:, :quarter], NT, preferred_element_type=F32)
    high = lax.dot_general(rest, w_ref[:, quarter:], NT, preferred_element_type=F32)
    groups = tile // 16
    low = low.reshape(groups, 2, 8, units)
    high = high.reshape(groups, 2, 8, units)
    top = iota((groups, 8, units), 1) < REST
    even = low[:, 0] + pltpu.roll(high[:, 0], REST, 1)
    odd = high[:, 1] + pltpu.roll(low[:, 1], REST, 1)
    base = x_ref.shape[0] * pl.num_programs(0)
    out_ref[pl.ds(pl.multiple_of(base + step * (tile // 2), tile // 2), tile // 2), :] = jnp.where(
        top, even, odd
    ).reshape(tile // 2, units)


def hidden(at, x, w, own):
    rows, lanes = x.shape
    units = w.shape[0]
    part = lanes // 3 * 2
    tile = 128
    return pl.pallas_call(
        hidden_kernel,
        grid_spec=pltpu.PrefetchScalarGridSpec(
            num_scalar_prefetch=1,
            grid=(rows // tile,),
            in_specs=[
                pl.BlockSpec((tile, lanes), lambda i, at: (i, 0)),
                pl.BlockSpec((units, part), (lambda i, at: (0, at[0])) if own else (lambda i, at: (0, 0))),
            ],
            out_specs=pl.BlockSpec((rows // 2 * 3, units), lambda i, at: (0, 0)),
        ),
        out_shape=jax.ShapeDtypeStruct((rows // 2 * 3, units), F32),
        compiler_params=params(),
        cost_estimate=pl.CostEstimate(
            flops=4 * rows * part * units, bytes_accessed=12 * 10**6, transcendentals=0
        ),
        name="hidden_own" if own else "hidden_other",
    )(at, x, w)


def diff_kernel(mine_ref, other_ref, gate_ref, up_ref, out_ref):
    units = mine_ref.shape[1]
    grad = mine_ref[...] + other_ref[...]
    value = gate_ref[...].astype(F32)
    up = up_ref[...].astype(F32)
    sigma = jax.nn.sigmoid(value)
    active = value * sigma
    slope = sigma * (1.0 + value * (1.0 - sigma))
    through = grad * active
    score = jnp.sum(through * up, axis=1, keepdims=True)
    out_ref[:, :units] = (grad * up * slope).astype(BF16)
    out_ref[:, units : 2 * units] = through.astype(BF16)
    out_ref[:, 2 * units :] = jnp.broadcast_to(score, (score.shape[0], 128)).astype(BF16)


def diffs(mine, other, gate, up):
    rows, units = mine.shape
    tile = 256
    spec = pl.BlockSpec((tile, units), lambda i: (i, 0))
    return pl.pallas_call(
        diff_kernel,
        grid=(rows // tile,),
        in_specs=[spec] * 4,
        out_specs=pl.BlockSpec((tile, 2 * units + 128), lambda i: (i, 0)),
        out_shape=jax.ShapeDtypeStruct((rows, 2 * units + 128), BF16),
        compiler_params=params(),
        cost_estimate=pl.CostEstimate(flops=10**7, bytes_accessed=7 * 10**6, transcendentals=rows * units),
        name="diffs",
    )(mine, other, gate, up)


def spread_rows(low, high):
    rows, lanes = low.shape
    pairs = rows // 8
    low = low.reshape(pairs, 8, lanes)
    high = high.reshape(pairs, 8, lanes)
    top = iota((pairs, 8, lanes), 1) < REST
    even = jnp.where(top, low, pltpu.roll(high, REST, 1))
    odd = jnp.where(top, pltpu.roll(low, REST, 1), high)
    return jnp.stack([even, odd], axis=1).reshape(2 * rows, lanes)


def inputs_kernel(at_ref, mine_ref, other_ref, g0, g1, u0, u1, og0, og1, ou0, ou1, out_ref):
    step = pl.program_id(0)
    last = pl.num_programs(0) - 1
    units = g0.shape[1]
    tile = g0.shape[0]
    main = out_ref.shape[0]

    @pl.when(step < last)
    def _():
        def product(g, u, og, ou):
            def one(x, w):
                return lax.dot_general(x, w[...], NT, preferred_element_type=F32)

            total = one(mine_ref[:, :units], g) + one(mine_ref[:, units : 2 * units], u)
            return total + one(other_ref[:, :units], og) + one(other_ref[:, units : 2 * units], ou)

        low = product(g0, u0, og0, ou0)
        high = product(g1, u1, og1, ou1)
        out_ref[:, :tile] = low[:main].astype(BF16)
        out_ref[:, tile : 2 * tile] = high[:main].astype(BF16)
        out_ref[:, 2 * tile :] = spread_rows(low[main:], high[main:]).astype(BF16)

    @pl.when(step == last)
    def _():
        score = mine_ref[:, 2 * units :].astype(F32) + other_ref[:, 2 * units :].astype(F32)
        rest = spread_rows(score[main:], score[main:])
        lane = iota((main, 128), 1)
        out_ref[:, :128] = jnp.where(lane == 0, score[:main], rest).astype(BF16)


def inputs(at, mine, other, w_gate, w_up, gate_other, up_other):
    rows, lanes = mine.shape
    units = w_gate.shape[1]
    part = gate_other.shape[0]
    tile = 256
    steps = part // 2 // tile
    main = rows // 3 * 2

    def own(shift):
        return pl.BlockSpec(
            (tile, units),
            lambda j, at: (at[0] * 2 * steps + shift * steps + jnp.minimum(j, steps - 1), 0),
        )

    def far(shift):
        return pl.BlockSpec(
            (tile, units), lambda j, at: (shift * steps + jnp.minimum(j, steps - 1), 0)
        )

    whole = pl.BlockSpec((rows, lanes), lambda j, at: (0, 0))
    return pl.pallas_call(
        inputs_kernel,
        grid_spec=pltpu.PrefetchScalarGridSpec(
            num_scalar_prefetch=1,
            grid=(steps + 1,),
            in_specs=[whole, whole, own(0), own(1), own(0), own(1), far(0), far(1), far(0), far(1)],
            out_specs=pl.BlockSpec((main, 3 * tile), lambda j, at: (0, j)),
        ),
        out_shape=jax.ShapeDtypeStruct((main, 3 * tile * steps + 128), BF16),
        compiler_params=params(),
        cost_estimate=pl.CostEstimate(
            flops=8 * rows * part * units, bytes_accessed=24 * 10**6, transcendentals=0
        ),
        name="inputs",
    )(at, mine, other, w_gate, w_gate, w_up, w_up, gate_other, gate_other, up_other, up_other)


def combine_kernel(at_ref, ids_ref, weight_ref, back_ref, score_ref, out_ref, grad_ref, w_ref):
    step = pl.program_id(0)
    tokens, topk = ids_ref.shape
    rows = back_ref.shape[0]
    experts = rows // MAIN
    tile = back_ref.shape[1] // 3

    @pl.when(step == 0)
    def _():
        names = iota((tokens, experts), 1)
        ids = ids_ref[...]
        weights = weight_ref[...]
        member = jnp.zeros((tokens, experts), F32)
        gate = jnp.zeros((tokens, experts), F32)
        for k in range(topk):
            hit = names == ids[:, k : k + 1]
            member = member + flag(hit)
            gate = gate + jnp.where(hit, weights[:, k : k + 1], 0.0)
        before = flag(iota((tokens, tokens), 1) < iota((tokens, tokens), 0)).astype(BF16)
        place = dot(before, member.astype(BF16))
        place = jnp.where(member > 0.5, place, -1.0).astype(BF16)
        spread = flag(iota((experts, rows), 1) // MAIN == iota((experts, rows), 0)).astype(BF16)
        wide = dot(place, spread).astype(jnp.int32)
        gate_high = gate.astype(BF16)
        gate_low = (gate - gate_high.astype(F32)).astype(BF16)
        lane = iota((tokens, rows), 1)
        in_main = wide == lane % MAIN
        in_rest = wide == MAIN + lane % REST
        upper = (lane // REST) % 2
        masks = (in_main, in_rest & (upper == 0), in_rest & (upper == 1))
        for at_part, part in enumerate((dot(gate_high, spread), dot(gate_low, spread))):
            for at_mask, mask in enumerate(masks):
                low = (2 * at_mask + at_part) * tokens
                w_ref[low : low + tokens, :] = jnp.where(mask, part, 0.0).astype(BF16)
        block = iota((rows, experts), 0) // MAIN == iota((rows, experts), 1)
        score = score_ref[...].astype(F32)
        main_score = jnp.where(block, score[:, 0:1], 0.0).astype(BF16)
        rest_score = jnp.where(block, score[:, 1:2], 0.0).astype(BF16)
        table = dot(flag(masks[0]).astype(BF16), main_score)
        table = table + dot(flag(masks[1]).astype(BF16), rest_score)
        column = iota((tokens, topk), 1)
        result = jnp.zeros((tokens, topk), F32)
        for k in range(topk):
            hit = names == ids[:, k : k + 1]
            picked = jnp.sum(jnp.where(hit, table, 0.0), axis=1, keepdims=True)
            result = result + jnp.where(column == k, picked, 0.0)
        half = tokens // 2
        grad_ref[...] = jnp.where(at_ref[0] == 0, result[:half], result[half:]).astype(BF16)

    main = dot(w_ref[: 2 * tokens, :], back_ref[:, : 2 * tile])
    rest = dot(w_ref[2 * tokens :, :], back_ref[:, 2 * tile :])
    main = main[:tokens] + main[tokens:]
    out_ref[0] = (main[:, :tile] + (rest[:tokens] + rest[tokens : 2 * tokens])).astype(BF16)
    out_ref[1] = (
        main[:, tile:] + (rest[2 * tokens : 3 * tokens] + rest[3 * tokens :])
    ).astype(BF16)


def combine(at, ids, weights, back):
    tokens, topk = ids.shape
    rows, lanes = back.shape
    tile = 256
    steps = lanes // (3 * tile)
    return pl.pallas_call(
        combine_kernel,
        grid_spec=pltpu.PrefetchScalarGridSpec(
            num_scalar_prefetch=1,
            grid=(steps,),
            in_specs=[
                pl.BlockSpec((tokens, topk), lambda j, at: (0, 0)),
                pl.BlockSpec((tokens, topk), lambda j, at: (0, 0)),
                pl.BlockSpec((rows, 3 * tile), lambda j, at: (0, j)),
                pl.BlockSpec((rows, 128), lambda j, at: (0, 6 * steps)),
            ],
            out_specs=[
                pl.BlockSpec((2, tokens, tile), lambda j, at: (0, 0, j)),
                pl.BlockSpec((tokens // 2, topk), lambda j, at: (0, 0)),
            ],
            scratch_shapes=[pltpu.VMEM((6 * tokens, rows), BF16)],
        ),
        out_shape=[
            jax.ShapeDtypeStruct((2, tokens, steps * tile), BF16),
            jax.ShapeDtypeStruct((tokens // 2, topk), BF16),
        ],
        compiler_params=params(),
        cost_estimate=pl.CostEstimate(flops=4 * 10**9, bytes_accessed=8 * 10**6, transcendentals=0),
        name="combine",
    )(at, ids, weights, back, back)


def by_part(value, groups):
    units = value.shape[1]
    value = value.reshape(groups, MAIN + REST, units)
    first = value[:, :MAIN].reshape(groups * MAIN, units)
    return jnp.concatenate([first, value[:, MAIN:].reshape(groups * REST, units)], axis=0)


def on_device(out_grad, route_ids, route_weights, gate_pre, up_pre, w_gate, w_up, w_down):
    groups = lax.axis_size("expert")
    seq_at = lax.axis_index("seq")
    at = seq_at.astype(jnp.int32).reshape(1)
    local, width = out_grad.shape
    part = width // 2
    w_gate, w_up, w_down = w_gate[0], w_up[0], w_down[0]
    away = (1 - seq_at) * part
    other = swap(lax.dynamic_slice_in_dim(out_grad, away, part, 1))
    sent = dispatch(at, route_ids.T, out_grad, other, groups)
    w_gate, w_up, w_down, gate, up, sent = lax.optimization_barrier(
        (w_gate, w_up, w_down, gate_pre[0], up_pre[0], sent)
    )
    received = lax.all_to_all(
        sent.reshape(groups, MAIN, sent.shape[1]), "expert", split_axis=0, concat_axis=0, tiled=True
    )
    received = received.reshape(groups * MAIN, sent.shape[1])
    down_other = swap(lax.dynamic_slice_in_dim(w_down, away, part, 1))
    gate_other = swap(lax.dynamic_slice_in_dim(w_gate, away, part, 0))
    up_other = swap(lax.dynamic_slice_in_dim(w_up, away, part, 0))
    gate = by_part(gate, groups)
    up = by_part(up, groups)
    grad_other = swap(hidden(at, received, down_other, False))
    grad_mine = hidden(at, received, w_down, True)
    mine = diffs(grad_mine, grad_other, gate, up)
    theirs = swap(mine)
    slots = inputs(at, mine, theirs, w_gate, w_up, gate_other, up_other)
    back = lax.all_to_all(
        slots.reshape(groups, MAIN, slots.shape[1]), "expert", split_axis=0, concat_axis=0, tiled=True
    )
    total, weight_grad = combine(
        at, route_ids, route_weights, back.reshape(groups * MAIN, slots.shape[1])
    )
    keep = lax.dynamic_slice_in_dim(total, seq_at * local, local, 1)
    came = swap(lax.dynamic_slice_in_dim(total, (1 - seq_at) * local, local, 1))
    first = jnp.where(seq_at == 0, keep, came)
    second = jnp.where(seq_at == 0, came, keep)
    return jnp.concatenate([first[0], first[1], second[0], second[1]], axis=1), weight_grad


def solution(mesh):
    in_specs = (
        P(("expert", "seq"), None),
        P("expert", None),
        P("expert", None),
        P("expert", None, "seq"),
        P("expert", None, "seq"),
        P("expert", None, "seq"),
        P("expert", None, "seq"),
        P("expert", "seq", None),
    )
    out_specs = (P(("expert", "seq"), None), P(("expert", "seq"), None))
    return jax.shard_map(
        on_device, mesh=mesh, in_specs=in_specs, out_specs=out_specs, check_vma=False
    )
```

time: 906 us -> 267 us (0.29)
  waiting for transfers between devices: 453 us -> 145 us
  local copies, waits for them, and re-layouts: 253 us -> 35.4 us
  other arithmetic: 92.7 us -> 3.95 us
  Pallas kernels: 0 us -> 53.3 us
  matrix products: 41.1 us -> 0 us
  between operations: 14.6 us -> 0.83 us
  starting transfers between devices: 35.6 us -> 26.4 us
    all_to_all x3 -> x2, waiting for transfers between devices: 416 us -> 138 us  [the longest x1 75.3 us: on_device(): lax.all_to_all(slots.reshape(groups, MAIN, slots.shape[1]), 'expert', spl...]
    gather x12 -> x0, local copies, waits for them, and re-layouts: 125 us -> none  [the longest x8 81 us: combine_rows(): flat_input[indices[:, column]].astype(jnp.float32)]
    unnamed x1, other arithmetic: 65.5 us -> 0.01 us
    unnamed x18 -> x23, local copies, waits for them, and re-layouts: 71.7 us -> 12.5 us
    pallas_call x0 -> x6, Pallas kernels: none -> 53.3 us  [the longest x2 22.5 us: hidden(): pl.pallas_call(hidden_kernel, grid_spec=pltpu.PrefetchScalarGridSpec(num_...]
    dot_general x3 -> x0, matrix products: 41.1 us -> none  [the longest x1 15.6 us: on_device(): lax.dot_general(up_diff, w_up[0], contract, preferred_element_type=jnp.fl...]
    psum x1 -> x0, waiting for transfers between devices: 36.2 us -> none  [on_device(): lax.psum(input_term.astype(jnp.bfloat16), 'seq').astype(jnp.float32)]
    psum x2 -> x0, local copies, waits for them, and re-layouts: 20.6 us -> none  [the longest x1 20 us: on_device(): lax.psum(input_term.astype(jnp.bfloat16), 'seq').astype(jnp.float32)]
  transfers between devices with their start and end apart: 5 -> 9, of which waited for: 3 -> 5; matrix products, arithmetic and copies ran while one was open for 16% -> 9% of each run, Pallas kernels for 0% -> 9%
where the time goes in v1:
time: 267 us; the launch traced here: 265 us
  waiting for transfers between devices  145 us (54%)
  Pallas kernels  53.3 us (20%)
  local copies, waits for them, and re-layouts  35.4 us (13%)
  starting transfers between devices  26.4 us (10%)
  other arithmetic  3.95 us (1%)
    all_to_all x1, waiting for transfers between devices, on_device(): lax.all_to_all(slots.reshape(groups, MAIN, slots.shape[1]), 'expert', spl...  75.3 us
    all_to_all x1, waiting for transfers between devices, on_device(): lax.all_to_all(sent.reshape(groups, MAIN, sent.shape[1]), 'expert', split...  62.3 us
    pallas_call x2, Pallas kernels, hidden(): pl.pallas_call(hidden_kernel, grid_spec=pltpu.PrefetchScalarGridSpec(num_...  22.5 us
    pallas_call x1, Pallas kernels, inputs(): pl.pallas_call(inputs_kernel, grid_spec=pltpu.PrefetchScalarGridSpec(num_...  16 us
    unnamed x23, local copies, waits for them, and re-layouts  12.5 us
    all_to_all x1, starting transfers between devices, on_device(): lax.all_to_all(sent.reshape(groups, MAIN, sent.shape[1]), 'expert', split...  11.7 us
    all_to_all x1, starting transfers between devices, on_device(): lax.all_to_all(slots.reshape(groups, MAIN, slots.shape[1]), 'expert', spl...  9.55 us
    pallas_call x1, Pallas kernels, combine(): pl.pallas_call(combine_kernel, grid_spec=pltpu.PrefetchScalarGridSpec(num...  9.26 us
  transfers between devices with their start and end apart: 9, of which 5 were waited for; matrix products, arithmetic and copies ran while one was open for 9% of the time, Pallas kernels for 9%

profile of v1, /device:TPU:1, one launch (start us, length us, event | category | flops | bytes accessed | tf_op | source)
XLA Modules:
  0.0 264.8 jit_solution(13033673960690876201)
XLA Ops:
  0.6 1.2 constant_dynamic-slice_fusion.4
  1.9 1.5 collective-permute-start
  3.4 2.1 collective-permute-done.other_ref
  5.5 1.5 copy-done.2
  7.0 0.7 copy-done.3
  7.7 4.5 %dispatch.1 = bf16[512,5376]{1,0:T(8,128)(2,1)S(1)} custom-call(s32[1]{0:T(128)} %bitcast.at_ref, s32[8,256]{1,0:T(8,128)S(1)} %bitcast.26, bf16[128,7168]{1,0:T(8,128)(2,1)S(1)} %copy-done.2, bf16[128,3584]{1,0:T(8,128)(2,1)S(1)} %collective-permute-done.other_ref), custom_call_target="tpu_custom_call" | custom-call | flops 2000000000 | bytes 8000000 | tf_op jit(solution)/shard_map/dispatch/pallas_call | solution.py:88
  12.2 2.5 copy-done
  14.7 11.7 %all-to-all-start = ((bf16[64,8,5376]{2,1,0:T(8,128)(2,1)}), bf16[64,8,5376]{2,1,0:T(8,128)(2,1)}, u32[]{:S(2)}, u32[]{:S(2)}) async-start(bf16[64,8,5376]{2,1,0:T(8,128)(2,1)} %bitcast.23), calls=%async_computation | async-start | bytes 11010048 | tf_op jit(solution)/shard_map/all_to_all | solution.py:379
  26.4 0.0 slice-start.1
  26.4 2.4 constant_dynamic-slice_fusion.3
  28.8 0.7 collective-permute-start.1
  29.6 4.1 %constant_dynamic-slice_fusion.2 = bf16[3584,512]{1,0:T(8,128)(2,1)} fusion(bf16[7168,512]{1,0:T(8,128)(2,1)} %bitcast.27, s32[]{:T(128)S(6)} %select_n.25), kind=kLoop, calls=%fused_computation.13 | loop fusion | bytes 7340036 | tf_op jit(solution)/shard_map/dynamic_slice | solution.py:384
  33.7 0.0 collective-permute-start.4
  33.7 2.1 constant_dynamic-slice_fusion.1
  35.8 0.5 collective-permute-start.5
  36.3 1.8 copy-done.5
  38.1 62.3 %all-to-all-done = bf16[64,8,5376]{2,1,0:T(8,128)(2,1)} async-done(((bf16[64,8,5376]{2,1,0:T(8,128)(2,1)}), bf16[64,8,5376]{2,1,0:T(8,128)(2,1)}, u32[]{:S(2)}, u32[]{:S(2)}) %all-to-all-start) | async-done | bytes 5505056 | tf_op jit(solution)/shard_map/all_to_all | solution.py:379
  100.4 2.0 copy-done.6
  102.4 11.2 %hidden_other.1 = f32[768,512]{1,0:T(8,128)S(1)} custom-call(s32[1]{0:T(128)} %bitcast.at_ref, bf16[512,5376]{1,0:T(8,128)(2,1)} %bitcast.8.x_ref, bf16[512,3584]{1,0:T(8,128)(2,1)S(1)} %copy-done.6), custom_call_target="tpu_custom_call" | custom-call | flops 3758096384 | bytes 12000000 | tf_op jit(solution)/shard_map/hidden_other/pallas_call | solution.py:140
  113.7 1.3 collective-permute-start.2
  115.0 2.1 reshape.40
  117.1 1.8 slice.33
  118.9 1.0 reshape.42
  119.9 2.1 reshape.43
  122.0 1.8 slice.35
  123.9 1.7 reshape.45
  125.6 1.1 slice_bitcast_fusion
  126.7 1.1 slice_bitcast_fusion.1
  127.8 1.1 pad_maximum_fusion.1
  128.8 3.1 %copy-done.1 = bf16[1,512,7168]{2,1,0:T(8,128)(2,1)S(1)} copy-done((bf16[1,512,7168]{2,1,0:T(8,128)(2,1)S(1)}, bf16[1,512,7168]{2,1,0:T(8,128)(2,1)}, u32[]{:S(2)}) %copy-start.1) | copy-done | bytes 7340056
  131.9 11.2 %hidden_own.1.mine_ref = f32[768,512]{1,0:T(8,128)S(1)} custom-call(s32[1]{0:T(128)} %bitcast.at_ref, bf16[512,5376]{1,0:T(8,128)(2,1)} %bitcast.8.x_ref, bf16[512,7168]{1,0:T(8,128)(2,1)S(1)} %bitcast.25), custom_call_target="tpu_custom_call" | custom-call | flops 3758096384 | bytes 12000000 | tf_op jit(solution)/shard_map/hidden_own/pallas_call | solution.py:140
  143.1 1.1 diffs.1.mine_ref
  144.2 0.1 collective-permute-start.3
  144.4 3.7 %collective-permute-done.3.other_ref = bf16[768,1152]{1,0:T(8,128)(2,1)S(1)} collective-permute-done((bf16[768,1152]{1,0:T(8,128)(2,1)S(1)}, bf16[768,1152]{1,0:T(8,128)(2,1)S(1)}, u32[]{:S(2)}, u32[]{:S(2)}) %collective-permute-start.3) | collective-permute-done | bytes 1769504 | tf_op jit(solution)/shard_map/ppermute | solution.py:33
  148.0 16.0 %inputs.1 = bf16[512,5504]{1,0:T(8,128)(2,1)} custom-call(s32[1]{0:T(128)} %bitcast.at_ref, bf16[768,1152]{1,0:T(8,128)(2,1)S(1)} %diffs.1.mine_ref, bf16[768,1152]{1,0:T(8,128)(2,1)S(1)} %collective-permute-done.3.other_ref, bf16[7168,512]{1,0:T(8,128)(2,1)} %bitcast.28, bf16[7168,512]{1,0:T(8,128)(2,1)} %bitcast.29, bf16[7168,512]{1,0:T(8,128)(2,1)} %bitcast.30, ...), custom_call_target="tpu_custom_call" | custom-call | flops 11274289152 | bytes 24000000 | tf_op jit(solution)/shard_map/inputs/pallas_call | solution.py:252
  164.0 9.6 %all-to-all-start.1 = ((bf16[64,8,5504]{2,1,0:T(8,128)(2,1)}), bf16[64,8,5504]{2,1,0:T(8,128)(2,1)}, u32[]{:S(2)}, u32[]{:S(2)}) async-start(bf16[64,8,5504]{2,1,0:T(8,128)(2,1)} %bitcast.35), calls=%async_computation.1 | async-start | bytes 11272192 | tf_op jit(solution)/shard_map/all_to_all | solution.py:393
  173.6 0.1 copy.13.ids_ref
  173.7 0.1 copy.14.weight_ref
  173.8 75.3 %all-to-all-done.1 = bf16[64,8,5504]{2,1,0:T(8,128)(2,1)} async-done(((bf16[64,8,5504]{2,1,0:T(8,128)(2,1)}), bf16[64,8,5504]{2,1,0:T(8,128)(2,1)}, u32[]{:S(2)}, u32[]{:S(2)}) %all-to-all-start.1) | async-done | bytes 5636128 | tf_op jit(solution)/shard_map/all_to_all | solution.py:393
  249.2 9.3 %combine.1 = (bf16[2,256,1792]{2,1,0:T(8,128)(2,1)S(1)}, bf16[128,8]{1,0:T(8,128)(2,1)S(1)}) custom-call(s32[1]{0:T(128)} %bitcast.at_ref, s32[256,8]{1,0:T(8,128)S(1)} %copy.13.ids_ref, f32[256,8]{1,0:T(8,128)S(1)} %copy.14.weight_ref, bf16[512,5504]{1,0:T(8,128)(2,1)} %bitcast.12.back_ref.score_ref, bf16[512,5504]{1,0:T(8,128)(2,1)} %bitcast.12.back_ref.score_ref), custom_call_target="tpu_custom_call" | custom-call | flops 4000000000 | bytes 8000000 | tf_op jit(solution)/shard_map/combine/pallas_call | solution.py:332
  258.4 0.1 constant_dynamic-slice_fusion
  258.5 1.0 collective-permute-start.6
  259.5 0.7 copy.15
  260.2 1.6 collective-permute-done.6
  261.8 1.5 broadcast_select_fusion.1
  263.2 0.1 slice_bitcast_fusion.5
  263.3 0.1 slice_bitcast_fusion.3
  263.4 1.4 pad_maximum_fusion
  (18 shorter events, 0.0 us)
Async XLA Ops:
  1.9 3.6 %collective-permute-start = (bf16[128,3584]{1,0:T(8,128)(2,1)S(1)}, bf16[128,3584]{1,0:T(8,128)(2,1)S(1)}, u32[]{:S(2)}, u32[]{:S(2)}) collective-permute-start(bf16[128,3584]{1,0:T(8,128)(2,1)S(1)} %constant_dynamic-slice_fusion.4), channel_id=1, source_target_pairs={{0,1},{1,0},{2,3},{3,2},{4,5},{5,4},{6,7},{7,6},{8,9},{9,8},{10,11... | collective-permute-start | bytes 2752520 | tf_op jit(solution)/shard_map/ppermute | solution.py:33
  5.5 1.5 copy-start.2
  7.0 0.7 copy-start.3
  12.2 2.5 copy-start
  14.7 19.1 %slice-start = ((s8[7340032]{0:T(1024)(128)(4,1)}), s8[3145728]{0:T(1024)(128)(4,1)S(1)}, s32[]{:S(2)}) async-start(s8[7340032]{0:T(1024)(128)(4,1)} %bitcast.32), calls=%async_computation.2 | async-start | bytes 6291456
  14.7 85.7 %all-to-all-start = ((bf16[64,8,5376]{2,1,0:T(8,128)(2,1)}), bf16[64,8,5376]{2,1,0:T(8,128)(2,1)}, u32[]{:S(2)}, u32[]{:S(2)}) async-start(bf16[64,8,5376]{2,1,0:T(8,128)(2,1)} %bitcast.23), calls=%async_computation | async-start | bytes 11010048 | tf_op jit(solution)/shard_map/all_to_all | solution.py:379
  26.4 7.4 %slice-start.1 = ((s8[7340032]{0:T(1024)(128)(4,1)}), s8[4194304]{0:T(1024)(128)(4,1)S(1)}, s32[]{:S(2)}) async-start(s8[7340032]{0:T(1024)(128)(4,1)} %bitcast.32), calls=%async_computation.3 | async-start | bytes 8388608
  28.8 7.5 %collective-permute-start.1 = (bf16[512,3584]{1,0:T(8,128)(2,1)S(1)}, bf16[512,3584]{1,0:T(8,128)(2,1)S(1)}, u32[]{:S(2)}, u32[]{:S(2)}) collective-permute-start(bf16[512,3584]{1,0:T(8,128)(2,1)S(1)} %constant_dynamic-slice_fusion.3), channel_id=1, source_target_pairs={{0,1},{1,0},{2,3},{3,2},{4,5},{5,4},{6,7},{7,6},{8,9},{9,8},{10,11... | collective-permute-start | bytes 11010056 | tf_op jit(solution)/shard_map/ppermute | solution.py:33
  33.7 110.6 %collective-permute-start.4 = (bf16[3584,512]{1,0:T(8,128)(2,1)}, bf16[3584,512]{1,0:T(8,128)(2,1)}, u32[]{:S(2)}, u32[]{:S(2)}) collective-permute-start(bf16[3584,512]{1,0:T(8,128)(2,1)} %constant_dynamic-slice_fusion.2), channel_id=1, source_target_pairs={{0,1},{1,0},{2,3},{3,2},{4,5},{5,4},{6,7},{7,6},{8,9},{9,8},{10,11... | collective-permute-start | bytes 11010056 | tf_op jit(solution)/shard_map/ppermute | solution.py:33
  35.8 108.5 %collective-permute-start.5 = (bf16[3584,512]{1,0:T(8,128)(2,1)}, bf16[3584,512]{1,0:T(8,128)(2,1)}, u32[]{:S(2)}, u32[]{:S(2)}) collective-permute-start(bf16[3584,512]{1,0:T(8,128)(2,1)} %constant_dynamic-slice_fusion.1), channel_id=1, source_target_pairs={{0,1},{1,0},{2,3},{3,2},{4,5},{5,4},{6,7},{7,6},{8,9},{9,8},{10,11... | collective-permute-start | bytes 11010056 | tf_op jit(solution)/shard_map/ppermute | solution.py:33
  36.3 1.8 copy-start.5
  100.4 2.0 copy-start.6
  113.7 29.5 %collective-permute-start.2 = (f32[768,512]{1,0:T(8,128)S(1)}, f32[768,512]{1,0:T(8,128)S(1)}, u32[]{:S(2)}, u32[]{:S(2)}) collective-permute-start(f32[768,512]{1,0:T(8,128)S(1)} %hidden_other.1), channel_id=1, source_target_pairs={{0,1},{1,0},{2,3},{3,2},{4,5},{5,4},{6,7},{7,6},{8,9},{9,8},{10,11... | collective-permute-start | bytes 4718600 | tf_op jit(solution)/shard_map/ppermute | solution.py:33
  128.8 3.1 %copy-start.1 = (bf16[1,512,7168]{2,1,0:T(8,128)(2,1)S(1)}, bf16[1,512,7168]{2,1,0:T(8,128)(2,1)}, u32[]{:S(2)}) copy-start(bf16[1,512,7168]{2,1,0:T(8,128)(2,1)} %param.15) | copy-start | bytes 22020100
  144.2 3.8 %collective-permute-start.3 = (bf16[768,1152]{1,0:T(8,128)(2,1)S(1)}, bf16[768,1152]{1,0:T(8,128)(2,1)S(1)}, u32[]{:S(2)}, u32[]{:S(2)}) collective-permute-start(bf16[768,1152]{1,0:T(8,128)(2,1)S(1)} %diffs.1.mine_ref), channel_id=1, source_target_pairs={{0,1},{1,0},{2,3},{3,2},{4,5},{5,4},{6,7},{7,6},{8,9},{9,8},{10,11... | collective-permute-start | bytes 5308424 | tf_op jit(solution)/shard_map/ppermute | solution.py:33
  164.0 9.6 %copy-start.4 = (s32[256,8]{0,1:T(8,128)S(1)}, s32[256,8]{0,1:T(8,128)}, u32[]{:S(2)}) copy-start(s32[256,8]{0,1:T(8,128)} %param.9) | copy-start | bytes 24580
  164.0 9.7 %copy-start.7 = (f32[256,8]{0,1:T(8,128)S(1)}, f32[256,8]{0,1:T(8,128)}, u32[]{:S(2)}) copy-start(f32[256,8]{0,1:T(8,128)} %param.10) | copy-start | bytes 24580
  164.0 85.2 %all-to-all-start.1 = ((bf16[64,8,5504]{2,1,0:T(8,128)(2,1)}), bf16[64,8,5504]{2,1,0:T(8,128)(2,1)}, u32[]{:S(2)}, u32[]{:S(2)}) async-start(bf16[64,8,5504]{2,1,0:T(8,128)(2,1)} %bitcast.35), calls=%async_computation.1 | async-start | bytes 11272192 | tf_op jit(solution)/shard_map/all_to_all | solution.py:393
  258.5 3.3 %collective-permute-start.6 = (bf16[2,128,1792]{2,1,0:T(8,128)(2,1)S(1)}, bf16[2,128,1792]{2,1,0:T(8,128)(2,1)}, u32[]{:S(2)}, u32[]{:S(2)}) collective-permute-start(bf16[2,128,1792]{2,1,0:T(8,128)(2,1)S(1)} %constant_dynamic-slice_fusion), channel_id=1, source_target_pairs={{0,1},{1,0},{2,3},{3,2},{4,5},{5,4},{6,7},{7,6},{8,9},{9,8},{10,11... | collective-permute-start | bytes 2752520 | tf_op jit(solution)/shard_map/ppermute | solution.py:33

commit v2 on v0

v2 whole, which is shorter than its diff:
```python
import jax
import jax.numpy as jnp
from jax import lax
from jax.experimental import pallas as pl
from jax.experimental.pallas import tpu as pltpu
from jax.sharding import PartitionSpec as P

F32 = jnp.float32
BF16 = jnp.bfloat16
NT = (((1,), (1,)), ((), ()))
MAIN = 8
REST = 4
MIB = 1024 * 1024
LIMIT = 20 * MIB
TILE = 256


def iota(shape, dim):
    return lax.broadcasted_iota(jnp.int32, shape, dim)


def flag(cond):
    return jnp.where(cond, 1.0, 0.0).astype(F32)


def dot(a, b):
    return jnp.dot(a, b, preferred_element_type=F32)


def params(limit=LIMIT):
    return pltpu.CompilerParams(vmem_limit_bytes=limit)


def in_hbm(*values):
    return [pltpu.with_memory_space_constraint(v, pltpu.HBM) for v in values]


def swap(value):
    return lax.ppermute(value, "seq", [(0, 1), (1, 0)])


def actual(index, at, half):
    return (index + half * at) % (2 * half)


def routes_kernel(at_ref, own_ids, other_ids, own_weights, other_weights, pa_ref, pb_ref, w_ref):
    at = at_ref[0]
    ids = jnp.concatenate([own_ids[...], other_ids[...]], axis=1)
    weights = jnp.concatenate([own_weights[...], other_weights[...]], axis=1)
    topk, tokens = ids.shape
    rows = pa_ref.shape[0]
    experts = rows // MAIN
    names = iota((experts, tokens), 0)
    member = jnp.zeros((experts, tokens), F32)
    gate = jnp.zeros((experts, tokens), F32)
    for k in range(topk):
        hit = names == ids[k : k + 1, :]
        member = member + flag(hit)
        gate = gate + jnp.where(hit, weights[k : k + 1, :], 0.0)
    first = actual(iota((tokens, tokens), 0), at, tokens // 2)
    before = flag(first < actual(iota((tokens, tokens), 1), at, tokens // 2)).astype(BF16)
    place = dot(member.astype(BF16), before)
    place = jnp.where(member > 0.5, place, -1.0).astype(BF16)
    spread = flag(iota((rows, experts), 0) // MAIN == iota((rows, experts), 1)).astype(BF16)
    wide = dot(spread, place).astype(jnp.int32)
    row = iota((rows, tokens), 0)
    pa_ref[...] = flag(wide == row % MAIN).astype(BF16)
    rest = flag(wide == MAIN + row % REST)
    upper = (row // REST) % 2
    pb_ref[:, :tokens] = jnp.where(upper == 0, rest, 0.0).astype(BF16)
    pb_ref[:, tokens:] = jnp.where(upper == 1, rest, 0.0).astype(BF16)

    def by_token(value):
        return lax.dot_general(value, spread, (((0,), (1,)), ((), ())), preferred_element_type=F32)

    wide = by_token(place).astype(jnp.int32)
    gate_high = gate.astype(BF16)
    gate_low = (gate - gate_high.astype(F32)).astype(BF16)
    lane = iota((tokens, rows), 1)
    in_rest = wide == MAIN + lane % REST
    upper = (lane // REST) % 2
    masks = (wide == lane % MAIN, in_rest & (upper == 0), in_rest & (upper == 1))
    for at_part, part in enumerate((by_token(gate_high), by_token(gate_low))):
        for at_mask, mask in enumerate(masks):
            low = (2 * at_mask + at_part) * tokens
            w_ref[low : low + tokens, :] = jnp.where(mask, part, 0.0).astype(BF16)


def routes(at, ids_t, weights_t, experts):
    topk, tokens = ids_t.shape
    half = tokens // 2
    rows = experts * MAIN
    own = pl.BlockSpec((topk, half), lambda j, at: (0, at[0]))
    other = pl.BlockSpec((topk, half), lambda j, at: (0, 1 - at[0]))
    shapes = [(rows, tokens), (rows, 2 * tokens), (6 * tokens, rows)]
    return pl.pallas_call(
        routes_kernel,
        grid_spec=pltpu.PrefetchScalarGridSpec(
            num_scalar_prefetch=1,
            grid=(1,),
            in_specs=[own, other, own, other],
            out_specs=[pl.BlockSpec(shape, lambda j, at: (0, 0)) for shape in shapes],
        ),
        out_shape=[jax.ShapeDtypeStruct(shape, BF16) for shape in shapes],
        compiler_params=params(),
        cost_estimate=pl.CostEstimate(flops=10**9, bytes_accessed=10**6, transcendentals=0),
        name="routes",
    )(at, ids_t, ids_t, weights_t, weights_t)


def dispatch_kernel(at_ref, pa_ref, pb_ref, own0, own1, other0, other1, out_ref):
    step = pl.program_id(0)
    first = jnp.concatenate([own0[...], other0[...]], axis=0)

    @pl.when(step < 4)
    def _():
        out_ref[...] = dot(pa_ref[...], first).astype(BF16)

    @pl.when(step >= 4)
    def _():
        both = jnp.concatenate([first, own1[...], other1[...]], axis=0)
        out_ref[...] = dot(pb_ref[...], both).astype(BF16)


def dispatch(at, pa, pb, out_grad, other):
    local, width = out_grad.shape
    rows = pa.shape[0]
    tile = width // 8

    def low(j):
        return jnp.where(j < 4, j, j - 4)

    def high(j):
        return jnp.maximum(j - 2, 2)

    return pl.pallas_call(
        dispatch_kernel,
        grid_spec=pltpu.PrefetchScalarGridSpec(
            num_scalar_prefetch=1,
            grid=(6,),
            in_specs=[
                pl.BlockSpec(pa.shape, lambda j, at: (0, 0)),
                pl.BlockSpec(pb.shape, lambda j, at: (0, 0)),
                pl.BlockSpec((local, tile), lambda j, at: (0, 4 * at[0] + low(j))),
                pl.BlockSpec((local, tile), lambda j, at: (0, 4 * at[0] + high(j))),
                pl.BlockSpec((local, tile), lambda j, at: (0, low(j))),
                pl.BlockSpec((local, tile), lambda j, at: (0, high(j))),
            ],
            out_specs=pl.BlockSpec((rows, tile), lambda j, at: (0, j)),
        ),
        out_shape=jax.ShapeDtypeStruct((rows, 6 * tile), BF16),
        compiler_params=params(),
        cost_estimate=pl.CostEstimate(flops=2 * 10**9, bytes_accessed=8 * 10**6, transcendentals=0),
        name="dispatch",
    )(at, pa, pb, out_grad, out_grad, other, other)


def hidden_kernel(at_ref, x_ref, w_ref, out_ref):
    main = x_ref.shape[0]
    units, part = w_ref.shape
    quarter = part // 2

    def product(low, high, start):
        return lax.dot_general(
            x_ref[:, low:high],
            w_ref[:, start : start + high - low],
            NT,
            preferred_element_type=F32,
        )

    pairs = main // 16
    first = product(0, part, 0).reshape(pairs, 2, 8, units)
    low = product(part, part + quarter, 0).reshape(pairs, 2, 8, units)
    high = product(part, part + quarter, quarter).reshape(pairs, 2, 8, units)
    top = iota((pairs, 8, units), 1) < REST
    even = low[:, 0] + pltpu.roll(high[:, 0], REST, 1)
    odd = high[:, 1] + pltpu.roll(low[:, 1], REST, 1)
    turned = pltpu.roll(first[:, 1], REST, 1)
    out_ref[...] = jnp.stack(
        [first[:, 0], jnp.where(top, even, turned), jnp.where(top, turned, odd)], axis=1
    ).reshape(main // 2 * 3, units)


def hidden(at, x, w, name):
    rows, lanes = x.shape
    units = w.shape[0]
    part = w.shape[1] // 2
    tile = 256
    return pl.pallas_call(
        hidden_kernel,
        grid_spec=pltpu.PrefetchScalarGridSpec(
            num_scalar_prefetch=1,
            grid=(units // tile,),
            in_specs=[
                pl.BlockSpec(memory_space=pltpu.VMEM),
                pl.BlockSpec((tile, part), lambda j, at: (j, at[0])),
            ],
            out_specs=pl.BlockSpec((rows // 2 * 3, tile), lambda j, at: (0, j)),
        ),
        out_shape=jax.ShapeDtypeStruct((rows // 2 * 3, units), F32),
        compiler_params=params(),
        cost_estimate=pl.CostEstimate(flops=0, bytes_accessed=0, transcendentals=0),
        name=name,
    )(at, x, w)


def diff_kernel(mine_ref, other_ref, gate_ref, up_ref, out_ref):
    units = mine_ref.shape[1]
    grad = mine_ref[...] + other_ref[...]
    value = gate_ref[...].astype(F32)
    up = up_ref[...].astype(F32)
    sigma = jax.nn.sigmoid(value)
    active = value * sigma
    slope = sigma * (1.0 + value * (1.0 - sigma))
    through = grad * active
    score = jnp.sum(through * up, axis=1, keepdims=True)
    out_ref[:, :units] = (grad * up * slope).astype(BF16)
    out_ref[:, units : 2 * units] = through.astype(BF16)
    out_ref[:, 2 * units :] = jnp.broadcast_to(score, (score.shape[0], 128)).astype(BF16)


def diffs(mine, other, gate, up):
    rows, units = mine.shape
    tile = 256
    spec = pl.BlockSpec((tile, units), lambda i: (i, 0))
    return pl.pallas_call(
        diff_kernel,
        grid=(rows // tile,),
        in_specs=[spec] * 4,
        out_specs=pl.BlockSpec((tile, 2 * units + 128), lambda i: (i, 0)),
        out_shape=jax.ShapeDtypeStruct((rows, 2 * units + 128), BF16),
        compiler_params=params(),
        cost_estimate=pl.CostEstimate(flops=0, bytes_accessed=0, transcendentals=0),
        name="diffs",
    )(mine, other, gate, up)


def parts_of(value):
    rows, lanes = value.shape
    pairs = rows // 24
    value = value.reshape(pairs, 3, 8, lanes)
    top = iota((pairs, 8, lanes), 1) < REST
    odd = jnp.where(top, pltpu.roll(value[:, 1], REST, 1), pltpu.roll(value[:, 2], REST, 1))
    main = jnp.stack([value[:, 0], odd], axis=1).reshape(16 * pairs, lanes)
    return main, value[:, 1], value[:, 2]


def both_quarters(low, high):
    top = iota(low[1].shape, 1) < REST
    even = jnp.where(top, low[1], pltpu.roll(high[1], REST, 1))
    odd = jnp.where(top, pltpu.roll(low[2], REST, 1), high[2])
    return jnp.stack([even, odd], axis=1).reshape(low[0].shape)


def inputs_kernel(at_ref, mine_ref, other_ref, g0, g1, u0, u1, og_ref, ou_ref, out_ref):
    step = pl.program_id(0)
    last = pl.num_programs(0) - 1
    units = g0.shape[1]
    quarter = last * TILE

    @pl.when(step < last)
    def _():
        x = jnp.concatenate([mine_ref[:, : 2 * units], other_ref[:, : 2 * units]], axis=1)

        def product(g, u, start):
            far = pl.ds(pl.multiple_of(2 * quarter * at_ref[0] + start + step * TILE, TILE), TILE)
            w = jnp.concatenate([g[...], u[...], og_ref[far, :], ou_ref[far, :]], axis=1)
            return lax.dot_general(x, w, NT, preferred_element_type=F32)

        low = parts_of(product(g0, u0, 0))
        high = parts_of(product(g1, u1, quarter))
        out_ref[:, :TILE] = low[0].astype(BF16)
        out_ref[:, TILE : 2 * TILE] = high[0].astype(BF16)
        out_ref[:, 2 * TILE :] = both_quarters(low, high).astype(BF16)

    @pl.when(step == last)
    def _():
        score = mine_ref[:, 2 * units :].astype(F32) + other_ref[:, 2 * units :].astype(F32)
        score = parts_of(score)
        lane = iota(score[0].shape, 1)
        out_ref[:, :128] = jnp.where(lane == 0, score[0], both_quarters(score, score)).astype(BF16)


def inputs(at, mine, other, w_gate, w_up, gate_other, up_other):
    w_gate, w_up = in_hbm(w_gate, w_up)
    rows, lanes = mine.shape
    units = w_gate.shape[1]
    part = w_gate.shape[0] // 2
    steps = part // 2 // TILE
    main = rows // 3 * 2

    def block(shift):
        return pl.BlockSpec(
            (TILE, units),
            lambda j, at: (at[0] * 2 * steps + shift * steps + jnp.minimum(j, steps - 1), 0),
        )

    whole = pl.BlockSpec(memory_space=pltpu.VMEM)
    return pl.pallas_call(
        inputs_kernel,
        grid_spec=pltpu.PrefetchScalarGridSpec(
            num_scalar_prefetch=1,
            grid=(steps + 1,),
            in_specs=[whole, whole, block(0), block(1), block(0), block(1), whole, whole],
            out_specs=pl.BlockSpec((main, 3 * TILE), lambda j, at: (0, j)),
        ),
        out_shape=jax.ShapeDtypeStruct((main, 3 * TILE * steps + 128), BF16),
        compiler_params=params(),
        cost_estimate=pl.CostEstimate(
            flops=8 * rows * part * units, bytes_accessed=24 * 10**6, transcendentals=0
        ),
        name="inputs",
    )(at, mine, other, w_gate, w_gate, w_up, w_up, gate_other, up_other)


def combine_kernel(
    at_ref, ids_ref, pa_ref, pb_ref, w_ref, back_ref, score_ref, keep_ref, send_ref, grad_ref
):
    step = pl.program_id(0)
    topk, half = ids_ref.shape
    tokens = 2 * half
    rows = back_ref.shape[0]
    experts = rows // MAIN

    @pl.when(step == 0)
    def _():
        block = iota((rows, experts), 0) // MAIN == iota((rows, experts), 1)
        score = score_ref[...].astype(F32)

        def one(column, slots):
            value = jnp.where(block, column, 0.0).astype(BF16)
            return lax.dot_general(value, slots, (((0,), (0,)), ((), ())), preferred_element_type=F32)

        table = one(score[:, 0:1], pa_ref[...]) + one(score[:, 1:2], pb_ref[...])
        names = iota((experts, half), 0)
        row = iota((topk, half), 0)
        ids = ids_ref[...]
        result = jnp.zeros((topk, half), F32)
        for k in range(topk):
            hit = names == ids[k : k + 1, :]
            picked = jnp.sum(jnp.where(hit, table, 0.0), axis=0, keepdims=True)
            result = result + jnp.where(row == k, picked, 0.0)
        grad_ref[...] = result.astype(BF16)

    main = dot(w_ref[: 2 * tokens, :], back_ref[:, : 2 * TILE])
    rest = dot(w_ref[2 * tokens :, :], back_ref[:, 2 * TILE :])
    main = main[:tokens] + main[tokens:]
    low = (main[:, :TILE] + (rest[:tokens] + rest[tokens : 2 * tokens])).astype(BF16)
    high = (main[:, TILE:] + (rest[2 * tokens : 3 * tokens] + rest[3 * tokens :])).astype(BF16)
    keep_ref[0] = low[:half]
    keep_ref[1] = high[:half]
    send_ref[0] = low[half:]
    send_ref[1] = high[half:]


def combine(at, ids_t, pa, pb, w, back):
    topk, tokens = ids_t.shape
    half = tokens // 2
    rows, lanes = back.shape
    steps = lanes // (3 * TILE)
    half_spec = pl.BlockSpec((2, half, TILE), lambda j, at: (0, 0, j))
    half_shape = jax.ShapeDtypeStruct((2, half, steps * TILE), BF16)
    return pl.pallas_call(
        combine_kernel,
        grid_spec=pltpu.PrefetchScalarGridSpec(
            num_scalar_prefetch=1,
            grid=(steps,),
            in_specs=[
                pl.BlockSpec((topk, half), lambda j, at: (0, at[0])),
                pl.BlockSpec((rows, half), lambda j, at: (0, 0)),
                pl.BlockSpec((rows, half), lambda j, at: (0, 0)),
                pl.BlockSpec(memory_space=pltpu.VMEM),
                pl.BlockSpec((rows, 3 * TILE), lambda j, at: (0, j)),
                pl.BlockSpec((rows, 128), lambda j, at: (0, steps * 3 * TILE // 128)),
            ],
            out_specs=[half_spec, half_spec, pl.BlockSpec((topk, half), lambda j, at: (0, 0))],
        ),
        out_shape=[half_shape, half_shape, jax.ShapeDtypeStruct((topk, half), BF16)],
        compiler_params=params(),
        cost_estimate=pl.CostEstimate(flops=4 * 10**9, bytes_accessed=8 * 10**6, transcendentals=0),
        name="combine",
    )(at, ids_t, pa, pb, w, back, back)


def join_kernel(at_ref, keep_ref, came_ref, out_ref):
    own = pl.program_id(0) // 2 == at_ref[0]

    @pl.when(own)
    def _():
        out_ref[...] = keep_ref[0]

    @pl.when(jnp.logical_not(own))
    def _():
        out_ref[...] = came_ref[0]


def join(at, keep, came):
    _, half, quarter = keep.shape
    spec = pl.BlockSpec((1, half, quarter), lambda j, at: (j % 2, 0, 0))
    return pl.pallas_call(
        join_kernel,
        grid_spec=pltpu.PrefetchScalarGridSpec(
            num_scalar_prefetch=1,
            grid=(4,),
            in_specs=[spec, spec],
            out_specs=pl.BlockSpec((half, quarter), lambda j, at: (0, j)),
        ),
        out_shape=jax.ShapeDtypeStruct((half, 4 * quarter), BF16),
        compiler_params=params(),
        cost_estimate=pl.CostEstimate(flops=0, bytes_accessed=4 * 10**6, transcendentals=0),
        name="join",
    )(at, keep, came)


def exchange(value, groups):
    rows, lanes = value.shape
    value = lax.all_to_all(
        value.reshape(groups, MAIN, lanes), "expert", split_axis=0, concat_axis=0, tiled=True
    )
    return value.reshape(rows, lanes)


def on_device(out_grad, route_ids, route_weights, gate_pre, up_pre, w_gate, w_up, w_down):
    groups = lax.axis_size("expert")
    seq_at = lax.axis_index("seq")
    at = seq_at.astype(jnp.int32).reshape(1)
    part = out_grad.shape[1] // 2
    w_gate, w_up, w_down = w_gate[0], w_up[0], w_down[0]
    other = swap(lax.dynamic_slice_in_dim(out_grad, (1 - seq_at) * part, part, 1))
    ids_t = route_ids.T
    pa, pb, w = routes(at, ids_t, route_weights.T, groups)
    sent = dispatch(at, pa, pb, out_grad, other)
    w_gate, w_up, w_down, sent = lax.optimization_barrier((w_gate, w_up, w_down, sent))
    down_other, gate_other, up_other = swap(w_down), swap(w_gate), swap(w_up)
    received = exchange(sent, groups)
    received, down_other, gate_other, up_other = lax.optimization_barrier(
        (received, down_other, gate_other, up_other)
    )
    grad_other = swap(hidden(at, received, down_other, "hidden_other"))
    grad_mine = hidden(at, received, in_hbm(w_down)[0], "hidden_own")
    mine = diffs(grad_mine, grad_other, gate_pre[0], up_pre[0])
    theirs = swap(mine)
    slots = inputs(at, mine, theirs, w_gate, w_up, gate_other, up_other)
    keep, send, weight_grad = combine(at, ids_t, pa, pb, w, exchange(slots, groups))
    return join(at, keep, swap(send)), weight_grad.T


def solution(mesh):
    in_specs = (
        P(("expert", "seq"), None),
        P("expert", None),
        P("expert", None),
        P("expert", None, "seq"),
        P("expert", None, "seq"),
        P("expert", None, "seq"),
        P("expert", None, "seq"),
        P("expert", "seq", None),
    )
    out_specs = (P(("expert", "seq"), None), P(("expert", "seq"), None))
    return jax.shard_map(
        on_device, mesh=mesh, in_specs=in_specs, out_specs=out_specs, check_vma=False
    )
```

time: 906 us -> 205 us (0.23); the launches traced: 896 us -> 204 us
  waiting for transfers between devices: 453 us -> 5.66 us
  local copies, waits for them, and re-layouts: 253 us -> 2.78 us
  blocking collectives: 6.31 us -> 148 us
  other arithmetic: 92.7 us -> 0 us
  matrix products: 41.1 us -> 0 us
  Pallas kernels: 0 us -> 40.5 us
  starting transfers between devices: 35.6 us -> 6.82 us
  between operations: 14.6 us -> 0.75 us
    all_to_all x3 -> x0, waiting for transfers between devices: 416 us -> none  [the longest x1 241 us: on_device(): lax.all_to_all(outgoing, 'expert', split_axis=0, concat_axis=1, tiled=True)]
    all_to_all x0 -> x2, blocking collectives: none -> 148 us  [exchange(): lax.all_to_all(value.reshape(groups, MAIN, lanes), 'expert', split_axis=0...]
    gather x12 -> x0, local copies, waits for them, and re-layouts: 125 us -> none  [the longest x8 81 us: combine_rows(): flat_input[indices[:, column]].astype(jnp.float32)]
    unnamed x18 -> x10, local copies, waits for them, and re-layouts: 71.7 us -> 1.41 us
    unnamed x1 -> x0, other arithmetic: 65.5 us -> none
    dot_general x3 -> x0, matrix products: 41.1 us -> none  [the longest x1 15.6 us: on_device(): lax.dot_general(up_diff, w_up[0], contract, preferred_element_type=jnp.fl...]
    pallas_call x0 -> x8, Pallas kernels: none -> 40.5 us  [the longest x1 15 us: inputs(): pl.pallas_call(inputs_kernel, grid_spec=pltpu.PrefetchScalarGridSpec(num_...]
    psum x1 -> x0, waiting for transfers between devices: 36.2 us -> none  [on_device(): lax.psum(input_term.astype(jnp.bfloat16), 'seq').astype(jnp.float32)]
  transfers between devices with their start and end apart: 5 -> 7, of which waited for: 3 -> 2; matrix products, arithmetic and copies ran while one was open for 16% -> 0% of each run, Pallas kernels for 0% -> 3%
where the time goes in v2:
time: 205 us; the launch traced here: 204 us
  blocking collectives  148 us (72%)
  Pallas kernels  40.5 us (20%)
  starting transfers between devices  6.82 us (3%)
  waiting for transfers between devices  5.66 us (3%)
  local copies, waits for them, and re-layouts  2.78 us (1%)
    all_to_all x2, blocking collectives, exchange(): lax.all_to_all(value.reshape(groups, MAIN, lanes), 'expert', split_axis=0...  148 us
    pallas_call x1, Pallas kernels, inputs(): pl.pallas_call(inputs_kernel, grid_spec=pltpu.PrefetchScalarGridSpec(num_...  15 us
    pallas_call x2, Pallas kernels, hidden(): pl.pallas_call(hidden_kernel, grid_spec=pltpu.PrefetchScalarGridSpec(num_...  10.4 us
    ppermute x7, starting transfers between devices, swap(): return lax.ppermute(value, 'seq', [(0, 1), (1, 0)])  6.82 us
    pallas_call x1, Pallas kernels, combine(): pl.pallas_call(combine_kernel, grid_spec=pltpu.PrefetchScalarGridSpec(num...  6.8 us
    ppermute x7, waiting for transfers between devices, swap(): return lax.ppermute(value, 'seq', [(0, 1), (1, 0)])  5.66 us
    pallas_call x1, Pallas kernels, dispatch(): pl.pallas_call(dispatch_kernel, grid_spec=pltpu.PrefetchScalarGridSpec(nu...  4.38 us
  transfers between devices with their start and end apart: 7, of which 2 were waited for; matrix products, arithmetic and copies ran while one was open for 0% of the time, Pallas kernels for 3%

profile of v2, /device:TPU:1, one launch (start us, length us, event | category | flops | bytes accessed | tf_op | source)
XLA Modules:
  0.0 204.3 jit_solution(4865375136565772840)
XLA Ops:
  0.6 0.0 copy-start
  0.6 1.4 constant_dynamic-slice_fusion
  2.0 1.5 collective-permute-start
  3.5 0.0 copy-start.3
  3.5 0.7 copy-done.3
  4.2 0.0 copy-start.4
  4.2 0.7 copy-done.4
  4.9 1.0 routes.1
  6.0 0.0 collective-permute-done.other0.other1
  6.0 0.0 copy-done
  6.0 4.4 %dispatch.1 = bf16[512,5376]{1,0:T(8,128)(2,1)S(1)} custom-call(s32[1]{0:T(128)} %bitcast.at_ref, bf16[512,256]{1,0:T(8,128)(2,1)S(1)} %get-tuple-element.16.pa_ref, bf16[512,512]{1,0:T(8,128)(2,1)S(1)} %get-tuple-element.17.pb_ref, bf16[128,7168]{1,0:T(8,128)(2,1)S(1)} %copy-done, bf16[128,7168]{1,0:T(8,128)(2,1)S(1)} %copy-done, ...), custom_call_target="tpu_custom_call" | custom-call | flops 2000000000 | bytes 8000000 | tf_op jit(solution)/shard_map/dispatch/pallas_call | solution.py:136
  10.4 0.1 collective-permute-start.1
  10.5 0.5 collective-permute-start.2
  11.0 0.1 collective-permute-start.3
  11.0 76.0 %all_to_all.10 = bf16[64,8,5376]{2,1,0:T(8,128)(2,1)S(1)} all-to-all(bf16[64,8,5376]{2,1,0:T(8,128)(2,1)S(1)} %bitcast.16), channel_id=1, replica_groups=mesh['expert'=64,'seq'=2] {'expert'}, dimensions={0} | all-to-all | bytes 11010048 | tf_op jit(solution)/shard_map/all_to_all | solution.py:417
  87.1 0.0 collective-permute-done.1.w_ref
  87.1 0.0 collective-permute-done.2.og_ref
  87.1 0.0 collective-permute-done.3.ou_ref
  87.1 4.6 %hidden_other.1 = f32[768,512]{1,0:T(8,128)S(1)} custom-call(s32[1]{0:T(128)} %bitcast.at_ref, bf16[512,5376]{1,0:T(8,128)(2,1)S(1)} %bitcast.13, bf16[512,7168]{1,0:T(8,128)(2,1)S(1)} %collective-permute-done.1.w_ref), custom_call_target="tpu_custom_call" | custom-call | tf_op jit(solution)/shard_map/hidden_other/pallas_call | solution.py:189
  91.7 0.0 copy-start.1
  91.7 0.0 copy-start.2
  91.7 2.4 %collective-permute-start.4 = (f32[768,512]{1,0:T(8,128)S(1)}, f32[768,512]{1,0:T(8,128)S(1)}, u32[]{:S(2)}, u32[]{:S(2)}) collective-permute-start(f32[768,512]{1,0:T(8,128)S(1)} %hidden_other.1), channel_id=1, source_target_pairs={{0,1},{1,0},{2,3},{3,2},{4,5},{5,4},{6,7},{7,6},{8,9},{9,8},{10,11... | collective-permute-start | bytes 4718600 | tf_op jit(solution)/shard_map/ppermute | solution.py:39
  94.1 5.8 %hidden_own.1.mine_ref = f32[768,512]{1,0:T(8,128)S(1)} custom-call(s32[1]{0:T(128)} %bitcast.at_ref, bf16[512,5376]{1,0:T(8,128)(2,1)S(1)} %bitcast.14, bf16[512,7168]{1,0:T(8,128)(2,1)} %bitcast.5.w_ref), custom_call_target="tpu_custom_call" | custom-call | tf_op jit(solution)/shard_map/hidden_own/pallas_call | solution.py:189
  99.9 0.0 collective-permute-done.4.other_ref
  100.0 0.0 copy-done.1
  100.0 0.0 copy-done.2
  100.0 1.1 diffs.1.mine_ref
  101.1 0.2 collective-permute-start.5
  101.3 3.6 %collective-permute-done.5.other_ref = bf16[768,1152]{1,0:T(8,128)(2,1)S(1)} collective-permute-done((bf16[768,1152]{1,0:T(8,128)(2,1)S(1)}, bf16[768,1152]{1,0:T(8,128)(2,1)S(1)}, u32[]{:S(2)}, u32[]{:S(2)}) %collective-permute-start.5) | collective-permute-done | bytes 1769504 | tf_op jit(solution)/shard_map/ppermute | solution.py:39
  104.8 15.0 %inputs.1 = bf16[512,5504]{1,0:T(8,128)(2,1)S(1)} custom-call(s32[1]{0:T(128)} %bitcast.at_ref, bf16[768,1152]{1,0:T(8,128)(2,1)S(1)} %diffs.1.mine_ref, bf16[768,1152]{1,0:T(8,128)(2,1)S(1)} %collective-permute-done.5.other_ref, bf16[7168,512]{1,0:T(8,128)(2,1)} %bitcast.3.g0.g1, bf16[7168,512]{1,0:T(8,128)(2,1)} %bitcast.3.g0.g1, ...), custom_call_target="tpu_custom_call" | custom-call | flops 11274289152 | bytes 24000000 | tf_op jit(solution)/shard_map/inputs/pallas_call | solution.py:299
  119.9 71.7 %all_to_all.11 = bf16[64,8,5504]{2,1,0:T(8,128)(2,1)S(1)} all-to-all(bf16[64,8,5504]{2,1,0:T(8,128)(2,1)S(1)} %bitcast.15), channel_id=1, replica_groups=mesh['expert'=64,'seq'=2] {'expert'}, dimensions={0} | all-to-all | bytes 11272192 | tf_op jit(solution)/shard_map/all_to_all | solution.py:417
  191.6 6.8 %combine.1 = (bf16[2,128,1792]{2,1,0:T(8,128)(2,1)S(1)}, bf16[2,128,1792]{2,1,0:T(8,128)(2,1)S(1)}, bf16[8,128]{1,0:T(8,128)(2,1)}) custom-call(s32[1]{0:T(128)} %bitcast.at_ref, s32[8,256]{1,0:T(8,128)S(1)} %bitcast.25, bf16[512,256]{1,0:T(8,128)(2,1)S(1)} %get-tuple-element.16.pa_ref, bf16[512,512]{1,0:T(8,128)(2,1)S(1)} %get-tuple-element.17.pb_ref, ...), custom_call_target="tpu_custom_call" | custom-call | flops 4000000000 | bytes 8000000 | tf_op jit(solution)/shard_map/combine/pallas_call | solution.py:363
  198.4 2.0 %collective-permute-start.6 = (bf16[2,128,1792]{2,1,0:T(8,128)(2,1)S(1)}, bf16[2,128,1792]{2,1,0:T(8,128)(2,1)S(1)}, u32[]{:S(2)}, u32[]{:S(2)}) collective-permute-start(bf16[2,128,1792]{2,1,0:T(8,128)(2,1)S(1)} %get-tuple-element.28), channel_id=1, source_target_pairs={{0,1},{1,0},{2,3},{3,2},{4,5},{5,4},{6,7},{7,6},{8,9},{9,8},{10,11... | collective-permute-start | bytes 2752520 | tf_op jit(solution)/shard_map/ppermute | solution.py:39
  200.5 2.1 %collective-permute-done.6.came_ref = bf16[2,128,1792]{2,1,0:T(8,128)(2,1)S(1)} collective-permute-done((bf16[2,128,1792]{2,1,0:T(8,128)(2,1)S(1)}, bf16[2,128,1792]{2,1,0:T(8,128)(2,1)S(1)}, u32[]{:S(2)}, u32[]{:S(2)}) %collective-permute-start.6) | collective-permute-done | bytes 917536 | tf_op jit(solution)/shard_map/ppermute | solution.py:39
  202.6 1.7 join.1
Async XLA Ops:
  0.6 5.3 %copy-start = (bf16[128,7168]{1,0:T(8,128)(2,1)S(1)}, bf16[128,7168]{1,0:T(8,128)(2,1)}, u32[]{:S(2)}) copy-start(bf16[128,7168]{1,0:T(8,128)(2,1)} %own1.1) | copy-start | bytes 5505028
  2.0 3.9 %collective-permute-start = (bf16[128,3584]{1,0:T(8,128)(2,1)S(1)}, bf16[128,3584]{1,0:T(8,128)(2,1)S(1)}, u32[]{:S(2)}, u32[]{:S(2)}) collective-permute-start(bf16[128,3584]{1,0:T(8,128)(2,1)S(1)} %constant_dynamic-slice_fusion), channel_id=1, source_target_pairs={{0,1},{1,0},{2,3},{3,2},{4,5},{5,4},{6,7},{7,6},{8,9},{9,8},{10,11... | collective-permute-start | bytes 2752520 | tf_op jit(solution)/shard_map/ppermute | solution.py:39
  3.5 0.7 copy-start.3
  4.2 0.7 copy-start.4
  10.4 76.7 %collective-permute-start.1 = (bf16[512,7168]{1,0:T(8,128)(2,1)}, bf16[512,7168]{1,0:T(8,128)(2,1)S(1)}, u32[]{:S(2)}, u32[]{:S(2)}) collective-permute-start(bf16[512,7168]{1,0:T(8,128)(2,1)} %bitcast.5.w_ref), channel_id=1, source_target_pairs={{0,1},{1,0},{2,3},{3,2},{4,5},{5,4},{6,7},{7,6},{8,9},{9,8},{10,11... | collective-permute-start | bytes 22020104 | tf_op jit(solution)/shard_map/ppermute | solution.py:39
  10.5 76.6 %collective-permute-start.2 = (bf16[7168,512]{1,0:T(8,128)(2,1)}, bf16[7168,512]{1,0:T(8,128)(2,1)S(1)}, u32[]{:S(2)}, u32[]{:S(2)}) collective-permute-start(bf16[7168,512]{1,0:T(8,128)(2,1)} %bitcast.3.g0.g1), channel_id=1, source_target_pairs={{0,1},{1,0},{2,3},{3,2},{4,5},{5,4},{6,7},{7,6},{8,9},{9,8},{10,11... | collective-permute-start | bytes 22020104 | tf_op jit(solution)/shard_map/ppermute | solution.py:39
  11.0 76.1 %collective-permute-start.3 = (bf16[7168,512]{1,0:T(8,128)(2,1)}, bf16[7168,512]{1,0:T(8,128)(2,1)S(1)}, u32[]{:S(2)}, u32[]{:S(2)}) collective-permute-start(bf16[7168,512]{1,0:T(8,128)(2,1)} %bitcast.4.u0.u1), channel_id=1, source_target_pairs={{0,1},{1,0},{2,3},{3,2},{4,5},{5,4},{6,7},{7,6},{8,9},{9,8},{10,11... | collective-permute-start | bytes 22020104 | tf_op jit(solution)/shard_map/ppermute | solution.py:39
  91.7 8.2 %copy-start.1 = (bf16[1,768,512]{2,1,0:T(8,128)(2,1)S(1)}, bf16[1,768,512]{2,1,0:T(8,128)(2,1)}, u32[]{:S(2)}) copy-start(bf16[1,768,512]{2,1,0:T(8,128)(2,1)} %param.11) | copy-start | bytes 2359300
  91.7 8.2 %copy-start.2 = (bf16[1,768,512]{2,1,0:T(8,128)(2,1)S(1)}, bf16[1,768,512]{2,1,0:T(8,128)(2,1)}, u32[]{:S(2)}) copy-start(bf16[1,768,512]{2,1,0:T(8,128)(2,1)} %param.12) | copy-start | bytes 2359300
  91.7 8.2 %collective-permute-start.4 = (f32[768,512]{1,0:T(8,128)S(1)}, f32[768,512]{1,0:T(8,128)S(1)}, u32[]{:S(2)}, u32[]{:S(2)}) collective-permute-start(f32[768,512]{1,0:T(8,128)S(1)} %hidden_other.1), channel_id=1, source_target_pairs={{0,1},{1,0},{2,3},{3,2},{4,5},{5,4},{6,7},{7,6},{8,9},{9,8},{10,11... | collective-permute-start | bytes 4718600 | tf_op jit(solution)/shard_map/ppermute | solution.py:39
  101.1 3.8 %collective-permute-start.5 = (bf16[768,1152]{1,0:T(8,128)(2,1)S(1)}, bf16[768,1152]{1,0:T(8,128)(2,1)S(1)}, u32[]{:S(2)}, u32[]{:S(2)}) collective-permute-start(bf16[768,1152]{1,0:T(8,128)(2,1)S(1)} %diffs.1.mine_ref), channel_id=1, source_target_pairs={{0,1},{1,0},{2,3},{3,2},{4,5},{5,4},{6,7},{7,6},{8,9},{9,8},{10,11... | collective-permute-start | bytes 5308424 | tf_op jit(solution)/shard_map/ppermute | solution.py:39
  198.4 4.1 %collective-permute-start.6 = (bf16[2,128,1792]{2,1,0:T(8,128)(2,1)S(1)}, bf16[2,128,1792]{2,1,0:T(8,128)(2,1)S(1)}, u32[]{:S(2)}, u32[]{:S(2)}) collective-permute-start(bf16[2,128,1792]{2,1,0:T(8,128)(2,1)S(1)} %get-tuple-element.28), channel_id=1, source_target_pairs={{0,1},{1,0},{2,3},{3,2},{4,5},{5,4},{6,7},{7,6},{8,9},{9,8},{10,11... | collective-permute-start | bytes 2752520 | tf_op jit(solution)/shard_map/ppermute | solution.py:39

commit v3 on v2

--- a/solution.py
+++ b/solution.py
@@ -74,16 +74,14 @@
         return lax.dot_general(value, spread, (((0,), (1,)), ((), ())), preferred_element_type=F32)
 
     wide = by_token(place).astype(jnp.int32)
-    gate_high = gate.astype(BF16)
-    gate_low = (gate - gate_high.astype(F32)).astype(BF16)
     lane = iota((tokens, rows), 1)
     in_rest = wide == MAIN + lane % REST
     upper = (lane // REST) % 2
+    gate = by_token(gate.astype(BF16))
     masks = (wide == lane % MAIN, in_rest & (upper == 0), in_rest & (upper == 1))
-    for at_part, part in enumerate((by_token(gate_high), by_token(gate_low))):
-        for at_mask, mask in enumerate(masks):
-            low = (2 * at_mask + at_part) * tokens
-            w_ref[low : low + tokens, :] = jnp.where(mask, part, 0.0).astype(BF16)
+    for at_mask, mask in enumerate(masks):
+        low = at_mask * tokens
+        w_ref[low : low + tokens, :] = jnp.where(mask, gate, 0.0).astype(BF16)
 
 
 def routes(at, ids_t, weights_t, experts):
@@ -92,7 +90,7 @@
     rows = experts * MAIN
     own = pl.BlockSpec((topk, half), lambda j, at: (0, at[0]))
     other = pl.BlockSpec((topk, half), lambda j, at: (0, 1 - at[0]))
-    shapes = [(rows, tokens), (rows, 2 * tokens), (6 * tokens, rows)]
+    shapes = [(rows, tokens), (rows, 2 * tokens), (3 * tokens, rows)]
     return pl.pallas_call(
         routes_kernel,
         grid_spec=pltpu.PrefetchScalarGridSpec(
@@ -110,16 +108,18 @@
 
 def dispatch_kernel(at_ref, pa_ref, pb_ref, own0, own1, other0, other1, out_ref):
     step = pl.program_id(0)
+    tile = own0.shape[1]
+    cols = pl.ds(pl.multiple_of(step * tile, 128), tile)
     first = jnp.concatenate([own0[...], other0[...]], axis=0)
 
     @pl.when(step < 4)
     def _():
-        out_ref[...] = dot(pa_ref[...], first).astype(BF16)
+        out_ref[:, cols] = dot(pa_ref[...], first).astype(BF16)
 
     @pl.when(step >= 4)
     def _():
         both = jnp.concatenate([first, own1[...], other1[...]], axis=0)
-        out_ref[...] = dot(pb_ref[...], both).astype(BF16)
+        out_ref[:, cols] = dot(pb_ref[...], both).astype(BF16)
 
 
 def dispatch(at, pa, pb, out_grad, other):
@@ -146,7 +146,7 @@
                 pl.BlockSpec((local, tile), lambda j, at: (0, low(j))),
                 pl.BlockSpec((local, tile), lambda j, at: (0, high(j))),
             ],
-            out_specs=pl.BlockSpec((rows, tile), lambda j, at: (0, j)),
+            out_specs=pl.BlockSpec(memory_space=pltpu.VMEM),
         ),
         out_shape=jax.ShapeDtypeStruct((rows, 6 * tile), BF16),
         compiler_params=params(),
@@ -254,31 +254,32 @@
 
 def inputs_kernel(at_ref, mine_ref, other_ref, g0, g1, u0, u1, og_ref, ou_ref, out_ref):
     step = pl.program_id(0)
-    last = pl.num_programs(0) - 1
     units = g0.shape[1]
-    quarter = last * TILE
-
-    @pl.when(step < last)
-    def _():
-        x = jnp.concatenate([mine_ref[:, : 2 * units], other_ref[:, : 2 * units]], axis=1)
-
-        def product(g, u, start):
-            far = pl.ds(pl.multiple_of(2 * quarter * at_ref[0] + start + step * TILE, TILE), TILE)
-            w = jnp.concatenate([g[...], u[...], og_ref[far, :], ou_ref[far, :]], axis=1)
-            return lax.dot_general(x, w, NT, preferred_element_type=F32)
-
-        low = parts_of(product(g0, u0, 0))
-        high = parts_of(product(g1, u1, quarter))
-        out_ref[:, :TILE] = low[0].astype(BF16)
-        out_ref[:, TILE : 2 * TILE] = high[0].astype(BF16)
-        out_ref[:, 2 * TILE :] = both_quarters(low, high).astype(BF16)
-
-    @pl.when(step == last)
+    quarter = pl.num_programs(0) * TILE
+    x = jnp.concatenate([mine_ref[:, : 2 * units], other_ref[:, : 2 * units]], axis=1)
+
+    def at_cols(start):
+        return pl.ds(pl.multiple_of(start + step * TILE, TILE), TILE)
+
+    def block(g, u, start):
+        far = at_cols(2 * quarter * at_ref[0] + start)
+        return jnp.concatenate([g[...], u[...], og_ref[far, :], ou_ref[far, :]], axis=1)
+
+    w = jnp.concatenate([block(g0, u0, 0), block(g1, u1, quarter)], axis=0)
+    result = lax.dot_general(x, w, NT, preferred_element_type=F32)
+    low = parts_of(result[:, :TILE])
+    high = parts_of(result[:, TILE:])
+    out_ref[:, at_cols(0)] = low[0].astype(BF16)
+    out_ref[:, at_cols(quarter)] = high[0].astype(BF16)
+    out_ref[:, at_cols(2 * quarter)] = both_quarters(low, high).astype(BF16)
+
+    @pl.when(step == 0)
     def _():
         score = mine_ref[:, 2 * units :].astype(F32) + other_ref[:, 2 * units :].astype(F32)
         score = parts_of(score)
         lane = iota(score[0].shape, 1)
-        out_ref[:, :128] = jnp.where(lane == 0, score[0], both_quarters(score, score)).astype(BF16)
+        end = out_ref.shape[1] - 128
+        out_ref[:, end:] = jnp.where(lane == 0, score[0], both_quarters(score, score)).astype(BF16)
 
 
 def inputs(at, mine, other, w_gate, w_up, gate_other, up_other):
@@ -292,7 +293,7 @@
     def block(shift):
         return pl.BlockSpec(
             (TILE, units),
-            lambda j, at: (at[0] * 2 * steps + shift * steps + jnp.minimum(j, steps - 1), 0),
+            lambda j, at: (at[0] * 2 * steps + shift * steps + j, 0),
         )
 
     whole = pl.BlockSpec(memory_space=pltpu.VMEM)
@@ -300,9 +301,9 @@
         inputs_kernel,
         grid_spec=pltpu.PrefetchScalarGridSpec(
             num_scalar_prefetch=1,
-            grid=(steps + 1,),
+            grid=(steps,),
             in_specs=[whole, whole, block(0), block(1), block(0), block(1), whole, whole],
-            out_specs=pl.BlockSpec((main, 3 * TILE), lambda j, at: (0, j)),
+            out_specs=whole,
         ),
         out_shape=jax.ShapeDtypeStruct((main, 3 * TILE * steps + 128), BF16),
         compiler_params=params(),
@@ -314,7 +315,7 @@
 
 
 def combine_kernel(
-    at_ref, ids_ref, pa_ref, pb_ref, w_ref, back_ref, score_ref, keep_ref, send_ref, grad_ref
+    at_ref, ids_ref, pa_ref, pb_ref, w_ref, back_ref, keep_ref, send_ref, grad_ref
 ):
     step = pl.program_id(0)
     topk, half = ids_ref.shape
@@ -325,7 +326,7 @@
     @pl.when(step == 0)
     def _():
         block = iota((rows, experts), 0) // MAIN == iota((rows, experts), 1)
-        score = score_ref[...].astype(F32)
+        score = back_ref[:, back_ref.shape[1] - 128 :].astype(F32)
 
         def one(column, slots):
             value = jnp.where(block, column, 0.0).astype(BF16)
@@ -342,74 +343,74 @@
             result = result + jnp.where(row == k, picked, 0.0)
         grad_ref[...] = result.astype(BF16)
 
-    main = dot(w_ref[: 2 * tokens, :], back_ref[:, : 2 * TILE])
-    rest = dot(w_ref[2 * tokens :, :], back_ref[:, 2 * TILE :])
-    main = main[:tokens] + main[tokens:]
-    low = (main[:, :TILE] + (rest[:tokens] + rest[tokens : 2 * tokens])).astype(BF16)
-    high = (main[:, TILE:] + (rest[2 * tokens : 3 * tokens] + rest[3 * tokens :])).astype(BF16)
-    keep_ref[0] = low[:half]
-    keep_ref[1] = high[:half]
-    send_ref[0] = low[half:]
-    send_ref[1] = high[half:]
+    tile = keep_ref.shape[1]
+    low = pl.ds(pl.multiple_of(step * tile, 128), tile)
+    rest = pl.ds(pl.multiple_of((4 + step % 2) * tile, 128), tile)
+    part = pl.ds(pl.multiple_of((1 + step // 2) * tokens, tokens), tokens)
+    slots = jnp.concatenate([back_ref[:, low], back_ref[:, rest]], axis=0)
+    total = dot(jnp.concatenate([w_ref[:tokens, :], w_ref[part, :]], axis=1), slots).astype(BF16)
+    keep_ref[...] = total[:half]
+    send_ref[...] = total[half:]
 
 
 def combine(at, ids_t, pa, pb, w, back):
     topk, tokens = ids_t.shape
     half = tokens // 2
     rows, lanes = back.shape
-    steps = lanes // (3 * TILE)
-    half_spec = pl.BlockSpec((2, half, TILE), lambda j, at: (0, 0, j))
-    half_shape = jax.ShapeDtypeStruct((2, half, steps * TILE), BF16)
+    tile = (lanes - 128) // 6
+    whole = pl.BlockSpec(memory_space=pltpu.VMEM)
     return pl.pallas_call(
         combine_kernel,
         grid_spec=pltpu.PrefetchScalarGridSpec(
             num_scalar_prefetch=1,
-            grid=(steps,),
+            grid=(4,),
             in_specs=[
                 pl.BlockSpec((topk, half), lambda j, at: (0, at[0])),
                 pl.BlockSpec((rows, half), lambda j, at: (0, 0)),
                 pl.BlockSpec((rows, half), lambda j, at: (0, 0)),
-                pl.BlockSpec(memory_space=pltpu.VMEM),
-                pl.BlockSpec((rows, 3 * TILE), lambda j, at: (0, j)),
-                pl.BlockSpec((rows, 128), lambda j, at: (0, steps * 3 * TILE // 128)),
+                whole,
+                whole,
             ],
-            out_specs=[half_spec, half_spec, pl.BlockSpec((topk, half), lambda j, at: (0, 0))],
-        ),
-        out_shape=[half_shape, half_shape, jax.ShapeDtypeStruct((topk, half), BF16)],
-        compiler_params=params(),
-        cost_estimate=pl.CostEstimate(flops=4 * 10**9, bytes_accessed=8 * 10**6, transcendentals=0),
+            out_specs=[
+                pl.BlockSpec((half, tile), lambda j, at: (0, 4 * at[0] + j)),
+                pl.BlockSpec((half, tile), lambda j, at: (0, j)),
+                pl.BlockSpec((topk, half), lambda j, at: (0, 0)),
+            ],
+        ),
+        out_shape=[
+            jax.ShapeDtypeStruct((half, 8 * tile), BF16),
+            jax.ShapeDtypeStruct((half, 4 * tile), BF16),
+            jax.ShapeDtypeStruct((topk, half), BF16),
+        ],
+        compiler_params=params(),
+        cost_estimate=pl.CostEstimate(flops=2 * 10**9, bytes_accessed=8 * 10**6, transcendentals=0),
         name="combine",
-    )(at, ids_t, pa, pb, w, back, back)
-
-
-def join_kernel(at_ref, keep_ref, came_ref, out_ref):
-    own = pl.program_id(0) // 2 == at_ref[0]
-
-    @pl.when(own)
-    def _():
-        out_ref[...] = keep_ref[0]
-
-    @pl.when(jnp.logical_not(own))
-    def _():
-        out_ref[...] = came_ref[0]
-
-
-def join(at, keep, came):
-    _, half, quarter = keep.shape
-    spec = pl.BlockSpec((1, half, quarter), lambda j, at: (j % 2, 0, 0))
+    )(at, ids_t, pa, pb, w, back)
+
+
+def join_kernel(at_ref, base_ref, came_ref, out_ref):
+    out_ref[...] = came_ref[...]
+
+
+def join(at, base, came):
+    half, part = came.shape
     return pl.pallas_call(
         join_kernel,
         grid_spec=pltpu.PrefetchScalarGridSpec(
             num_scalar_prefetch=1,
-            grid=(4,),
-            in_specs=[spec, spec],
-            out_specs=pl.BlockSpec((half, quarter), lambda j, at: (0, j)),
-        ),
-        out_shape=jax.ShapeDtypeStruct((half, 4 * quarter), BF16),
-        compiler_params=params(),
-        cost_estimate=pl.CostEstimate(flops=0, bytes_accessed=4 * 10**6, transcendentals=0),
+            grid=(2,),
+            in_specs=[
+                pl.BlockSpec(memory_space=pl.ANY),
+                pl.BlockSpec((half, part // 2), lambda j, at: (0, j)),
+            ],
+            out_specs=pl.BlockSpec((half, part // 2), lambda j, at: (0, 2 * (1 - at[0]) + j)),
+        ),
+        out_shape=jax.ShapeDtypeStruct(base.shape, BF16),
+        input_output_aliases={1: 0},
+        compiler_params=params(),
+        cost_estimate=pl.CostEstimate(flops=0, bytes_accessed=2 * 10**6, transcendentals=0),
         name="join",
-    )(at, keep, came)
+    )(at, base, came)
 
 
 def exchange(value, groups):

time: 205 us -> 200 us (0.976)
  Pallas kernels: 40.5 us -> 36 us
    pallas_call x1, Pallas kernels: 6.8 us -> 4.09 us  [combine(): pl.pallas_call(combine_kernel, grid_spec=pltpu.PrefetchScalarGridSpec(num...]
where the time goes in v3:
time: 200 us
  blocking collectives  148 us (74%)
  Pallas kernels  36 us (18%)
  starting transfers between devices  6.8 us (3%)
  waiting for transfers between devices  5.68 us (3%)
  local copies, waits for them, and re-layouts  2.78 us (1%)
    all_to_all x2, blocking collectives, exchange(): lax.all_to_all(value.reshape(groups, MAIN, lanes), 'expert', split_axis=0...  148 us
    pallas_call x1, Pallas kernels, inputs(): pl.pallas_call(inputs_kernel, grid_spec=pltpu.PrefetchScalarGridSpec(num_...  14.6 us
    pallas_call x2, Pallas kernels, hidden(): pl.pallas_call(hidden_kernel, grid_spec=pltpu.PrefetchScalarGridSpec(num_...  10.4 us
    ppermute x7, starting transfers between devices, swap(): return lax.ppermute(value, 'seq', [(0, 1), (1, 0)])  6.8 us
    ppermute x7, waiting for transfers between devices, swap(): return lax.ppermute(value, 'seq', [(0, 1), (1, 0)])  5.68 us
    pallas_call x1, Pallas kernels, combine(): pl.pallas_call(combine_kernel, grid_spec=pltpu.PrefetchScalarGridSpec(num...  4.09 us
  transfers between devices with their start and end apart: 7, of which 2 were waited for; matrix products, arithmetic and copies ran while one was open for 0% of the time, Pallas kernels for 3%

profile of v3, /device:TPU:1, one launch (start us, length us, event | category | flops | bytes accessed | tf_op | source)
XLA Modules:
  0.0 199.6 jit_solution(13045347273499985537)
XLA Ops:
  0.6 0.0 copy-start
  0.6 1.4 constant_dynamic-slice_fusion
  2.0 1.5 collective-permute-start
  3.5 0.0 copy-start.3
  3.5 0.7 copy-done.3
  4.2 0.0 copy-start.4
  4.2 0.7 copy-done.4
  4.9 0.8 routes.1
  5.8 0.0 collective-permute-done.other0.other1
  5.8 0.0 copy-done
  5.8 3.9 %dispatch.1 = bf16[512,5376]{1,0:T(8,128)(2,1)S(1)} custom-call(s32[1]{0:T(128)} %bitcast.at_ref, bf16[512,256]{1,0:T(8,128)(2,1)S(1)} %get-tuple-element.16.pa_ref, bf16[512,512]{1,0:T(8,128)(2,1)S(1)} %get-tuple-element.17.pb_ref, bf16[128,7168]{1,0:T(8,128)(2,1)S(1)} %copy-done, bf16[128,7168]{1,0:T(8,128)(2,1)S(1)} %copy-done, ...), custom_call_target="tpu_custom_call" | custom-call | flops 2000000000 | bytes 8000000 | tf_op jit(solution)/shard_map/dispatch/pallas_call | solution.py:136
  9.7 0.3 collective-permute-start.1
  10.0 0.3 collective-permute-start.2
  10.3 0.2 collective-permute-start.3
  10.5 76.1 %all_to_all.10 = bf16[64,8,5376]{2,1,0:T(8,128)(2,1)S(1)} all-to-all(bf16[64,8,5376]{2,1,0:T(8,128)(2,1)S(1)} %bitcast.16), channel_id=1, replica_groups=mesh['expert'=64,'seq'=2] {'expert'}, dimensions={0} | all-to-all | bytes 11010048 | tf_op jit(solution)/shard_map/all_to_all | solution.py:418
  86.6 0.0 collective-permute-done.1.w_ref
  86.6 0.0 collective-permute-done.2.og_ref
  86.7 0.0 collective-permute-done.3.ou_ref
  86.7 4.6 %hidden_other.1 = f32[768,512]{1,0:T(8,128)S(1)} custom-call(s32[1]{0:T(128)} %bitcast.at_ref, bf16[512,5376]{1,0:T(8,128)(2,1)S(1)} %bitcast.13, bf16[512,7168]{1,0:T(8,128)(2,1)S(1)} %collective-permute-done.1.w_ref), custom_call_target="tpu_custom_call" | custom-call | tf_op jit(solution)/shard_map/hidden_other/pallas_call | solution.py:189
  91.3 0.0 copy-start.1
  91.3 0.0 copy-start.2
  91.3 2.3 %collective-permute-start.4 = (f32[768,512]{1,0:T(8,128)S(1)}, f32[768,512]{1,0:T(8,128)S(1)}, u32[]{:S(2)}, u32[]{:S(2)}) collective-permute-start(f32[768,512]{1,0:T(8,128)S(1)} %hidden_other.1), channel_id=1, source_target_pairs={{0,1},{1,0},{2,3},{3,2},{4,5},{5,4},{6,7},{7,6},{8,9},{9,8},{10,11... | collective-permute-start | bytes 4718600 | tf_op jit(solution)/shard_map/ppermute | solution.py:39
  93.6 5.8 %hidden_own.1.mine_ref = f32[768,512]{1,0:T(8,128)S(1)} custom-call(s32[1]{0:T(128)} %bitcast.at_ref, bf16[512,5376]{1,0:T(8,128)(2,1)S(1)} %bitcast.14, bf16[512,7168]{1,0:T(8,128)(2,1)} %bitcast.5.w_ref), custom_call_target="tpu_custom_call" | custom-call | tf_op jit(solution)/shard_map/hidden_own/pallas_call | solution.py:189
  99.4 0.0 collective-permute-done.4.other_ref
  99.4 0.0 copy-done.1
  99.4 0.0 copy-done.2
  99.4 1.1 diffs.1.mine_ref
  100.5 0.2 collective-permute-start.5
  100.7 3.6 %collective-permute-done.5.other_ref = bf16[768,1152]{1,0:T(8,128)(2,1)S(1)} collective-permute-done((bf16[768,1152]{1,0:T(8,128)(2,1)S(1)}, bf16[768,1152]{1,0:T(8,128)(2,1)S(1)}, u32[]{:S(2)}, u32[]{:S(2)}) %collective-permute-start.5) | collective-permute-done | bytes 1769504 | tf_op jit(solution)/shard_map/ppermute | solution.py:39
  104.3 14.6 %inputs.1 = bf16[512,5504]{1,0:T(8,128)(2,1)S(1)} custom-call(s32[1]{0:T(128)} %bitcast.at_ref, bf16[768,1152]{1,0:T(8,128)(2,1)S(1)} %diffs.1.mine_ref, bf16[768,1152]{1,0:T(8,128)(2,1)S(1)} %collective-permute-done.5.other_ref, bf16[7168,512]{1,0:T(8,128)(2,1)} %bitcast.3.g0.g1, bf16[7168,512]{1,0:T(8,128)(2,1)} %bitcast.3.g0.g1, ...), custom_call_target="tpu_custom_call" | custom-call | flops 11274289152 | bytes 24000000 | tf_op jit(solution)/shard_map/inputs/pallas_call | solution.py:300
  118.9 71.4 %all_to_all.11 = bf16[64,8,5504]{2,1,0:T(8,128)(2,1)S(1)} all-to-all(bf16[64,8,5504]{2,1,0:T(8,128)(2,1)S(1)} %bitcast.15), channel_id=1, replica_groups=mesh['expert'=64,'seq'=2] {'expert'}, dimensions={0} | all-to-all | bytes 11272192 | tf_op jit(solution)/shard_map/all_to_all | solution.py:418
  190.4 4.1 %combine.1 = (bf16[128,7168]{1,0:T(8,128)(2,1)}, bf16[128,3584]{1,0:T(8,128)(2,1)S(1)}, bf16[8,128]{1,0:T(8,128)(2,1)}) custom-call(s32[1]{0:T(128)} %bitcast.at_ref, s32[8,256]{1,0:T(8,128)S(1)} %bitcast.24, bf16[512,256]{1,0:T(8,128)(2,1)S(1)} %get-tuple-element.16.pa_ref, bf16[512,512]{1,0:T(8,128)(2,1)S(1)} %get-tuple-element.17.pb_ref, ...), custom_call_target="tpu_custom_call" | custom-call | flops 2000000000 | bytes 8000000 | tf_op jit(solution)/shard_map/combine/pallas_call | solution.py:362
  194.4 2.0 %collective-permute-start.6 = (bf16[128,3584]{1,0:T(8,128)(2,1)S(1)}, bf16[128,3584]{1,0:T(8,128)(2,1)S(1)}, u32[]{:S(2)}, u32[]{:S(2)}) collective-permute-start(bf16[128,3584]{1,0:T(8,128)(2,1)S(1)} %get-tuple-element.28), channel_id=1, source_target_pairs={{0,1},{1,0},{2,3},{3,2},{4,5},{5,4},{6,7},{7,6},{8,9},{9,8},{10,11... | collective-permute-start | bytes 2752520 | tf_op jit(solution)/shard_map/ppermute | solution.py:39
  196.5 2.1 %collective-permute-done.6.came_ref = bf16[128,3584]{1,0:T(8,128)(2,1)S(1)} collective-permute-done((bf16[128,3584]{1,0:T(8,128)(2,1)S(1)}, bf16[128,3584]{1,0:T(8,128)(2,1)S(1)}, u32[]{:S(2)}, u32[]{:S(2)}) %collective-permute-start.6) | collective-permute-done | bytes 917536 | tf_op jit(solution)/shard_map/ppermute | solution.py:39
  198.6 1.0 join.1
Async XLA Ops:
  0.6 5.1 %copy-start = (bf16[128,7168]{1,0:T(8,128)(2,1)S(1)}, bf16[128,7168]{1,0:T(8,128)(2,1)}, u32[]{:S(2)}) copy-start(bf16[128,7168]{1,0:T(8,128)(2,1)} %own1.1) | copy-start | bytes 5505028
  2.0 3.7 %collective-permute-start = (bf16[128,3584]{1,0:T(8,128)(2,1)S(1)}, bf16[128,3584]{1,0:T(8,128)(2,1)S(1)}, u32[]{:S(2)}, u32[]{:S(2)}) collective-permute-start(bf16[128,3584]{1,0:T(8,128)(2,1)S(1)} %constant_dynamic-slice_fusion), channel_id=1, source_target_pairs={{0,1},{1,0},{2,3},{3,2},{4,5},{5,4},{6,7},{7,6},{8,9},{9,8},{10,11... | collective-permute-start | bytes 2752520 | tf_op jit(solution)/shard_map/ppermute | solution.py:39
  3.5 0.7 copy-start.3
  4.2 0.7 copy-start.4
  9.7 76.9 %collective-permute-start.1 = (bf16[512,7168]{1,0:T(8,128)(2,1)}, bf16[512,7168]{1,0:T(8,128)(2,1)S(1)}, u32[]{:S(2)}, u32[]{:S(2)}) collective-permute-start(bf16[512,7168]{1,0:T(8,128)(2,1)} %bitcast.5.w_ref), channel_id=1, source_target_pairs={{0,1},{1,0},{2,3},{3,2},{4,5},{5,4},{6,7},{7,6},{8,9},{9,8},{10,11... | collective-permute-start | bytes 22020104 | tf_op jit(solution)/shard_map/ppermute | solution.py:39
  10.0 76.7 %collective-permute-start.2 = (bf16[7168,512]{1,0:T(8,128)(2,1)}, bf16[7168,512]{1,0:T(8,128)(2,1)S(1)}, u32[]{:S(2)}, u32[]{:S(2)}) collective-permute-start(bf16[7168,512]{1,0:T(8,128)(2,1)} %bitcast.3.g0.g1), channel_id=1, source_target_pairs={{0,1},{1,0},{2,3},{3,2},{4,5},{5,4},{6,7},{7,6},{8,9},{9,8},{10,11... | collective-permute-start | bytes 22020104 | tf_op jit(solution)/shard_map/ppermute | solution.py:39
  10.3 76.3 %collective-permute-start.3 = (bf16[7168,512]{1,0:T(8,128)(2,1)}, bf16[7168,512]{1,0:T(8,128)(2,1)S(1)}, u32[]{:S(2)}, u32[]{:S(2)}) collective-permute-start(bf16[7168,512]{1,0:T(8,128)(2,1)} %bitcast.4.u0.u1), channel_id=1, source_target_pairs={{0,1},{1,0},{2,3},{3,2},{4,5},{5,4},{6,7},{7,6},{8,9},{9,8},{10,11... | collective-permute-start | bytes 22020104 | tf_op jit(solution)/shard_map/ppermute | solution.py:39
  91.3 8.1 %copy-start.1 = (bf16[1,768,512]{2,1,0:T(8,128)(2,1)S(1)}, bf16[1,768,512]{2,1,0:T(8,128)(2,1)}, u32[]{:S(2)}) copy-start(bf16[1,768,512]{2,1,0:T(8,128)(2,1)} %param.11) | copy-start | bytes 2359300
  91.3 8.1 %copy-start.2 = (bf16[1,768,512]{2,1,0:T(8,128)(2,1)S(1)}, bf16[1,768,512]{2,1,0:T(8,128)(2,1)}, u32[]{:S(2)}) copy-start(bf16[1,768,512]{2,1,0:T(8,128)(2,1)} %param.12) | copy-start | bytes 2359300
  91.3 8.1 %collective-permute-start.4 = (f32[768,512]{1,0:T(8,128)S(1)}, f32[768,512]{1,0:T(8,128)S(1)}, u32[]{:S(2)}, u32[]{:S(2)}) collective-permute-start(f32[768,512]{1,0:T(8,128)S(1)} %hidden_other.1), channel_id=1, source_target_pairs={{0,1},{1,0},{2,3},{3,2},{4,5},{5,4},{6,7},{7,6},{8,9},{9,8},{10,11... | collective-permute-start | bytes 4718600 | tf_op jit(solution)/shard_map/ppermute | solution.py:39
  100.5 3.8 %collective-permute-start.5 = (bf16[768,1152]{1,0:T(8,128)(2,1)S(1)}, bf16[768,1152]{1,0:T(8,128)(2,1)S(1)}, u32[]{:S(2)}, u32[]{:S(2)}) collective-permute-start(bf16[768,1152]{1,0:T(8,128)(2,1)S(1)} %diffs.1.mine_ref), channel_id=1, source_target_pairs={{0,1},{1,0},{2,3},{3,2},{4,5},{5,4},{6,7},{7,6},{8,9},{9,8},{10,11... | collective-permute-start | bytes 5308424 | tf_op jit(solution)/shard_map/ppermute | solution.py:39
  194.4 4.1 %collective-permute-start.6 = (bf16[128,3584]{1,0:T(8,128)(2,1)S(1)}, bf16[128,3584]{1,0:T(8,128)(2,1)S(1)}, u32[]{:S(2)}, u32[]{:S(2)}) collective-permute-start(bf16[128,3584]{1,0:T(8,128)(2,1)S(1)} %get-tuple-element.28), channel_id=1, source_target_pairs={{0,1},{1,0},{2,3},{3,2},{4,5},{5,4},{6,7},{7,6},{8,9},{9,8},{10,11... | collective-permute-start | bytes 2752520 | tf_op jit(solution)/shard_map/ppermute | solution.py:39

commit v4 on v3

--- a/solution.py
+++ b/solution.py
@@ -11,8 +11,9 @@
 MAIN = 8
 REST = 4
 MIB = 1024 * 1024
-LIMIT = 20 * MIB
+LIMIT = 14 * MIB
 TILE = 256
+EARLY = 3
 
 
 def iota(shape, dim):
@@ -156,17 +157,16 @@
 
 
 def hidden_kernel(at_ref, x_ref, w_ref, out_ref):
+    step = pl.program_id(0)
     main = x_ref.shape[0]
-    units, part = w_ref.shape
+    units = out_ref.shape[1]
+    part = w_ref.shape[1] // 2
     quarter = part // 2
 
     def product(low, high, start):
-        return lax.dot_general(
-            x_ref[:, low:high],
-            w_ref[:, start : start + high - low],
-            NT,
-            preferred_element_type=F32,
-        )
+        rows = pl.ds(pl.multiple_of(step * units, units), units)
+        cols = pl.ds(pl.multiple_of(at_ref[0] * part + start, 128), high - low)
+        return lax.dot_general(x_ref[:, low:high], w_ref[rows, cols], NT, preferred_element_type=F32)
 
     pairs = main // 16
     first = product(0, part, 0).reshape(pairs, 2, 8, units)
@@ -184,17 +184,14 @@
 def hidden(at, x, w, name):
     rows, lanes = x.shape
     units = w.shape[0]
-    part = w.shape[1] // 2
     tile = 256
+    whole = pl.BlockSpec(memory_space=pltpu.VMEM)
     return pl.pallas_call(
         hidden_kernel,
         grid_spec=pltpu.PrefetchScalarGridSpec(
             num_scalar_prefetch=1,
             grid=(units // tile,),
-            in_specs=[
-                pl.BlockSpec(memory_space=pltpu.VMEM),
-                pl.BlockSpec((tile, part), lambda j, at: (j, at[0])),
-            ],
+            in_specs=[whole, whole],
             out_specs=pl.BlockSpec((rows // 2 * 3, tile), lambda j, at: (0, j)),
         ),
         out_shape=jax.ShapeDtypeStruct((rows // 2 * 3, units), F32),
@@ -252,26 +249,85 @@
     return jnp.stack([even, odd], axis=1).reshape(low[0].shape)
 
 
-def inputs_kernel(at_ref, mine_ref, other_ref, g0, g1, u0, u1, og_ref, ou_ref, out_ref):
+def own_block(units, steps, shift):
+    return pl.BlockSpec((TILE, units), lambda j, at: (at[0] * 2 * steps + shift * steps + j, 0))
+
+
+def early_kernel(at_ref, mine_ref, g0, g1, u0, u1, out_ref):
+    units = g0.shape[1]
+    w = jnp.concatenate(
+        [
+            jnp.concatenate([g0[...], u0[...]], axis=1),
+            jnp.concatenate([g1[...], u1[...]], axis=1),
+        ],
+        axis=0,
+    )
+    cols = pl.ds(pl.multiple_of(pl.program_id(0) * 2 * TILE, TILE), 2 * TILE)
+    out_ref[:, cols] = lax.dot_general(mine_ref[:, : 2 * units], w, NT, preferred_element_type=F32)
+
+
+def early_inputs(at, mine, w_gate, w_up):
+    w_gate, w_up = in_hbm(w_gate, w_up)
+    rows = mine.shape[0]
+    units = w_gate.shape[1]
+    steps = w_gate.shape[0] // 4 // TILE
+    whole = pl.BlockSpec(memory_space=pltpu.VMEM)
+    blocks = [own_block(units, steps, 0), own_block(units, steps, 1)]
+    return pl.pallas_call(
+        early_kernel,
+        grid_spec=pltpu.PrefetchScalarGridSpec(
+            num_scalar_prefetch=1,
+            grid=(EARLY,),
+            in_specs=[whole] + blocks + blocks,
+            out_specs=whole,
+        ),
+        out_shape=jax.ShapeDtypeStruct((rows, EARLY * 2 * TILE), F32),
+        compiler_params=params(),
+        cost_estimate=pl.CostEstimate(
+            flops=8 * EARLY * rows * TILE * units, bytes_accessed=10**7, transcendentals=0
+        ),
+        name="early_inputs",
+    )(at, mine, w_gate, w_gate, w_up, w_up)
+
+
+def inputs_kernel(
+    at_ref, mine_ref, other_ref, early_ref, g0, g1, u0, u1, og_ref, ou_ref, out_ref
+):
     step = pl.program_id(0)
     units = g0.shape[1]
     quarter = pl.num_programs(0) * TILE
-    x = jnp.concatenate([mine_ref[:, : 2 * units], other_ref[:, : 2 * units]], axis=1)
 
     def at_cols(start):
         return pl.ds(pl.multiple_of(start + step * TILE, TILE), TILE)
 
-    def block(g, u, start):
-        far = at_cols(2 * quarter * at_ref[0] + start)
-        return jnp.concatenate([g[...], u[...], og_ref[far, :], ou_ref[far, :]], axis=1)
-
-    w = jnp.concatenate([block(g0, u0, 0), block(g1, u1, quarter)], axis=0)
-    result = lax.dot_general(x, w, NT, preferred_element_type=F32)
-    low = parts_of(result[:, :TILE])
-    high = parts_of(result[:, TILE:])
-    out_ref[:, at_cols(0)] = low[0].astype(BF16)
-    out_ref[:, at_cols(quarter)] = high[0].astype(BF16)
-    out_ref[:, at_cols(2 * quarter)] = both_quarters(low, high).astype(BF16)
+    def far(start):
+        rows = at_cols(2 * quarter * at_ref[0] + start)
+        return [og_ref[rows, :], ou_ref[rows, :]]
+
+    def product(x, low, high):
+        w = jnp.concatenate(
+            [jnp.concatenate(low, axis=1), jnp.concatenate(high, axis=1)], axis=0
+        )
+        return lax.dot_general(x, w, NT, preferred_element_type=F32)
+
+    def finish(result):
+        low = parts_of(result[:, :TILE])
+        high = parts_of(result[:, TILE:])
+        out_ref[:, at_cols(0)] = low[0].astype(BF16)
+        out_ref[:, at_cols(quarter)] = high[0].astype(BF16)
+        out_ref[:, at_cols(2 * quarter)] = both_quarters(low, high).astype(BF16)
+
+    @pl.when(step < EARLY)
+    def _():
+        cols = pl.ds(pl.multiple_of(step * 2 * TILE, TILE), 2 * TILE)
+        finish(product(other_ref[:, : 2 * units], far(0), far(quarter)) + early_ref[:, cols])
+
+    @pl.when(step >= EARLY)
+    def _():
+        x = jnp.concatenate([mine_ref[:, : 2 * units], other_ref[:, : 2 * units]], axis=1)
+        low = [g0[...], u0[...]] + far(0)
+        high = [g1[...], u1[...]] + far(quarter)
+        finish(product(x, low, high))
 
     @pl.when(step == 0)
     def _():
@@ -282,7 +338,7 @@
         out_ref[:, end:] = jnp.where(lane == 0, score[0], both_quarters(score, score)).astype(BF16)
 
 
-def inputs(at, mine, other, w_gate, w_up, gate_other, up_other):
+def inputs(at, mine, other, early, w_gate, w_up, gate_other, up_other):
     w_gate, w_up = in_hbm(w_gate, w_up)
     rows, lanes = mine.shape
     units = w_gate.shape[1]
@@ -293,7 +349,7 @@
     def block(shift):
         return pl.BlockSpec(
             (TILE, units),
-            lambda j, at: (at[0] * 2 * steps + shift * steps + j, 0),
+            lambda j, at: (at[0] * 2 * steps + shift * steps + jnp.maximum(j, EARLY), 0),
         )
 
     whole = pl.BlockSpec(memory_space=pltpu.VMEM)
@@ -302,7 +358,7 @@
         grid_spec=pltpu.PrefetchScalarGridSpec(
             num_scalar_prefetch=1,
             grid=(steps,),
-            in_specs=[whole, whole, block(0), block(1), block(0), block(1), whole, whole],
+            in_specs=[whole] * 3 + [block(0), block(1), block(0), block(1), whole, whole],
             out_specs=whole,
         ),
         out_shape=jax.ShapeDtypeStruct((main, 3 * TILE * steps + 128), BF16),
@@ -311,19 +367,47 @@
             flops=8 * rows * part * units, bytes_accessed=24 * 10**6, transcendentals=0
         ),
         name="inputs",
-    )(at, mine, other, w_gate, w_gate, w_up, w_up, gate_other, up_other)
-
-
-def combine_kernel(
-    at_ref, ids_ref, pa_ref, pb_ref, w_ref, back_ref, keep_ref, send_ref, grad_ref
-):
+    )(at, mine, other, early, w_gate, w_gate, w_up, w_up, gate_other, up_other)
+
+
+def tokens_of(w_ref, back_ref, out_ref, first):
     step = pl.program_id(0)
+    half, tile = out_ref.shape
+    tokens = 2 * half
+    low = pl.ds(pl.multiple_of(step * tile, 128), tile)
+    rest = pl.ds(pl.multiple_of((4 + step % 2) * tile, 128), tile)
+    part = pl.ds(pl.multiple_of((1 + step // 2) * tokens + first, half), half)
+    slots = jnp.concatenate([back_ref[:, low], back_ref[:, rest]], axis=0)
+    w = jnp.concatenate([w_ref[first : first + half, :], w_ref[part, :]], axis=1)
+    out_ref[...] = dot(w, slots).astype(BF16)
+
+
+def send_kernel(w_ref, back_ref, send_ref):
+    tokens_of(w_ref, back_ref, send_ref, send_ref.shape[0])
+
+
+def combine_send(w, back):
+    half = w.shape[0] // 6
+    tile = (back.shape[1] - 128) // 6
+    whole = pl.BlockSpec(memory_space=pltpu.VMEM)
+    return pl.pallas_call(
+        send_kernel,
+        grid=(4,),
+        in_specs=[whole, whole],
+        out_specs=pl.BlockSpec((half, tile), lambda j: (0, j)),
+        out_shape=jax.ShapeDtypeStruct((half, 4 * tile), BF16),
+        compiler_params=params(),
+        cost_estimate=pl.CostEstimate(flops=10**9, bytes_accessed=7 * 10**6, transcendentals=0),
+        name="combine_send",
+    )(w, back)
+
+
+def keep_kernel(at_ref, ids_ref, pa_ref, pb_ref, w_ref, back_ref, keep_ref, grad_ref):
     topk, half = ids_ref.shape
-    tokens = 2 * half
     rows = back_ref.shape[0]
     experts = rows // MAIN
 
-    @pl.when(step == 0)
+    @pl.when(pl.program_id(0) == 0)
     def _():
         block = iota((rows, experts), 0) // MAIN == iota((rows, experts), 1)
         score = back_ref[:, back_ref.shape[1] - 128 :].astype(F32)
@@ -343,24 +427,17 @@
             result = result + jnp.where(row == k, picked, 0.0)
         grad_ref[...] = result.astype(BF16)
 
-    tile = keep_ref.shape[1]
-    low = pl.ds(pl.multiple_of(step * tile, 128), tile)
-    rest = pl.ds(pl.multiple_of((4 + step % 2) * tile, 128), tile)
-    part = pl.ds(pl.multiple_of((1 + step // 2) * tokens, tokens), tokens)
-    slots = jnp.concatenate([back_ref[:, low], back_ref[:, rest]], axis=0)
-    total = dot(jnp.concatenate([w_ref[:tokens, :], w_ref[part, :]], axis=1), slots).astype(BF16)
-    keep_ref[...] = total[:half]
-    send_ref[...] = total[half:]
-
-
-def combine(at, ids_t, pa, pb, w, back):
+    tokens_of(w_ref, back_ref, keep_ref, 0)
+
+
+def combine_keep(at, ids_t, pa, pb, w, back):
     topk, tokens = ids_t.shape
     half = tokens // 2
     rows, lanes = back.shape
     tile = (lanes - 128) // 6
     whole = pl.BlockSpec(memory_space=pltpu.VMEM)
     return pl.pallas_call(
-        combine_kernel,
+        keep_kernel,
         grid_spec=pltpu.PrefetchScalarGridSpec(
             num_scalar_prefetch=1,
             grid=(4,),
@@ -373,18 +450,16 @@
             ],
             out_specs=[
                 pl.BlockSpec((half, tile), lambda j, at: (0, 4 * at[0] + j)),
-                pl.BlockSpec((half, tile), lambda j, at: (0, j)),
                 pl.BlockSpec((topk, half), lambda j, at: (0, 0)),
             ],
         ),
         out_shape=[
             jax.ShapeDtypeStruct((half, 8 * tile), BF16),
-            jax.ShapeDtypeStruct((half, 4 * tile), BF16),
             jax.ShapeDtypeStruct((topk, half), BF16),
         ],
         compiler_params=params(),
-        cost_estimate=pl.CostEstimate(flops=2 * 10**9, bytes_accessed=8 * 10**6, transcendentals=0),
-        name="combine",
+        cost_estimate=pl.CostEstimate(flops=10**9, bytes_accessed=7 * 10**6, transcendentals=0),
+        name="combine_keep",
     )(at, ids_t, pa, pb, w, back)
 
 
@@ -438,12 +513,15 @@
         (received, down_other, gate_other, up_other)
     )
     grad_other = swap(hidden(at, received, down_other, "hidden_other"))
-    grad_mine = hidden(at, received, in_hbm(w_down)[0], "hidden_own")
+    grad_mine = hidden(at, received, w_down, "hidden_own")
     mine = diffs(grad_mine, grad_other, gate_pre[0], up_pre[0])
     theirs = swap(mine)
-    slots = inputs(at, mine, theirs, w_gate, w_up, gate_other, up_other)
-    keep, send, weight_grad = combine(at, ids_t, pa, pb, w, exchange(slots, groups))
-    return join(at, keep, swap(send)), weight_grad.T
+    early = early_inputs(at, mine, w_gate, w_up)
+    slots = inputs(at, mine, theirs, early, w_gate, w_up, gate_other, up_other)
+    back = exchange(slots, groups)
+    came = swap(combine_send(w, back))
+    keep, weight_grad = combine_keep(at, ids_t, pa, pb, w, back)
+    return join(at, keep, came), weight_grad.T
 
 
 def solution(mesh):

time: 200 us -> 196 us (0.980)
  waiting for transfers between devices: 5.68 us -> 0.02 us
    ppermute x7, waiting for transfers between devices: 5.68 us -> 0.02 us  [swap(): return lax.ppermute(value, 'seq', [(0, 1), (1, 0)])]
    pallas_call x1 -> x3, Pallas kernels: 4.09 us -> 9.57 us  [the longest x1 4.46 us: early_inputs(): pl.pallas_call(early_kernel, grid_spec=pltpu.PrefetchScalarGridSpec(num_s...]
    pallas_call x1, Pallas kernels: 14.6 us -> 12.3 us  [inputs(): pl.pallas_call(inputs_kernel, grid_spec=pltpu.PrefetchScalarGridSpec(num_...]
  transfers between devices with their start and end apart: 7 -> 7, of which waited for: 2 -> 0; matrix products, arithmetic and copies ran while one was open for 0% -> 0% of each run, Pallas kernels for 3% -> 7%
where the time goes in v4:
time: 196 us
  blocking collectives  147 us (75%)
  Pallas kernels  37.5 us (19%)
  starting transfers between devices  7.05 us (4%)
  local copies, waits for them, and re-layouts  2.8 us (1%)
    all_to_all x2, blocking collectives, exchange(): lax.all_to_all(value.reshape(groups, MAIN, lanes), 'expert', split_axis=0...  147 us
    pallas_call x1, Pallas kernels, inputs(): pl.pallas_call(inputs_kernel, grid_spec=pltpu.PrefetchScalarGridSpec(num_...  12.3 us
    pallas_call x2, Pallas kernels, hidden(): pl.pallas_call(hidden_kernel, grid_spec=pltpu.PrefetchScalarGridSpec(num_...  8.71 us
    ppermute x7, starting transfers between devices, swap(): return lax.ppermute(value, 'seq', [(0, 1), (1, 0)])  7.05 us
    pallas_call x1, Pallas kernels, early_inputs(): pl.pallas_call(early_kernel, grid_spec=pltpu.PrefetchScalarGridSpec(num_s...  4.46 us
    pallas_call x1, Pallas kernels, dispatch(): pl.pallas_call(dispatch_kernel, grid_spec=pltpu.PrefetchScalarGridSpec(nu...  3.93 us
  transfers between devices with their start and end apart: 7, of which 0 were waited for; matrix products, arithmetic and copies ran while one was open for 0% of the time, Pallas kernels for 7%

profile of v4, /device:TPU:1, one launch (start us, length us, event | category | flops | bytes accessed | tf_op | source)
XLA Modules:
  0.0 195.5 jit_solution(14843645340653249899)
XLA Ops:
  0.6 0.0 copy-start
  0.6 1.4 constant_dynamic-slice_fusion
  2.0 1.5 collective-permute-start
  3.5 0.0 copy-start.3
  3.5 0.7 copy-done.3
  4.2 0.0 copy-start.4
  4.2 0.7 copy-done.4
  4.9 0.0 slice-start
  4.9 0.8 routes.1
  5.8 0.0 collective-permute-done.other0.other1
  5.8 0.0 copy-done
  5.8 0.0 slice-start.1
  5.8 3.9 %dispatch.1 = bf16[512,5376]{1,0:T(8,128)(2,1)S(1)} custom-call(s32[1]{0:T(128)} %bitcast.at_ref, bf16[512,256]{1,0:T(8,128)(2,1)S(1)} %get-tuple-element.15.pa_ref, bf16[512,512]{1,0:T(8,128)(2,1)S(1)} %get-tuple-element.16.pb_ref, bf16[128,7168]{1,0:T(8,128)(2,1)S(1)} %copy-done, bf16[128,7168]{1,0:T(8,128)(2,1)S(1)} %copy-done, ...), custom_call_target="tpu_custom_call" | custom-call | flops 2000000000 | bytes 8000000 | tf_op jit(solution)/shard_map/dispatch/pallas_call | solution.py:137
  9.7 0.0 slice-done
  9.7 0.0 slice-done.1
  9.8 0.3 collective-permute-start.1
  10.0 0.3 collective-permute-start.2
  10.4 0.2 collective-permute-start.3
  10.5 76.1 %all_to_all.10 = bf16[64,8,5376]{2,1,0:T(8,128)(2,1)S(1)} all-to-all(bf16[64,8,5376]{2,1,0:T(8,128)(2,1)S(1)} %bitcast.18), channel_id=1, replica_groups=mesh['expert'=64,'seq'=2] {'expert'}, dimensions={0} | all-to-all | bytes 11010048 | tf_op jit(solution)/shard_map/all_to_all | solution.py:493
  86.7 0.0 collective-permute-done.1.w_ref
  86.7 0.0 collective-permute-done.2.og_ref
  86.7 0.0 collective-permute-done.3.ou_ref
  86.7 4.4 %hidden_other.1 = f32[768,512]{1,0:T(8,128)S(1)} custom-call(s32[1]{0:T(128)} %bitcast.at_ref, bf16[512,5376]{1,0:T(8,128)(2,1)S(1)} %bitcast.15, bf16[512,7168]{1,0:T(8,128)(2,1)S(1)} %collective-permute-done.1.w_ref), custom_call_target="tpu_custom_call" | custom-call | tf_op jit(solution)/shard_map/hidden_other/pallas_call | solution.py:189
  91.0 0.0 copy-start.1
  91.1 0.0 copy-start.2
  91.1 2.3 %collective-permute-start.4 = (f32[768,512]{1,0:T(8,128)S(1)}, f32[768,512]{1,0:T(8,128)S(1)}, u32[]{:S(2)}, u32[]{:S(2)}) collective-permute-start(f32[768,512]{1,0:T(8,128)S(1)} %hidden_other.1), channel_id=1, source_target_pairs={{0,1},{1,0},{2,3},{3,2},{4,5},{5,4},{6,7},{7,6},{8,9},{9,8},{10,11... | collective-permute-start | bytes 4718600 | tf_op jit(solution)/shard_map/ppermute | solution.py:40
  93.3 4.3 %hidden_own.1.mine_ref = f32[768,512]{1,0:T(8,128)S(1)} custom-call(s32[1]{0:T(128)} %bitcast.at_ref, bf16[512,5376]{1,0:T(8,128)(2,1)S(1)} %bitcast.16, bf16[512,7168]{1,0:T(8,128)(2,1)S(1)} %bitcast.22), custom_call_target="tpu_custom_call" | custom-call | tf_op jit(solution)/shard_map/hidden_own/pallas_call | solution.py:189
  97.7 0.0 collective-permute-done.4.other_ref
  97.7 0.0 copy-done.1
  97.7 0.0 copy-done.2
  97.7 1.1 diffs.1.mine_ref
  98.8 0.1 collective-permute-start.5
  98.9 4.5 %early_inputs.1.early_ref = f32[768,1536]{1,0:T(8,128)S(1)} custom-call(s32[1]{0:T(128)} %bitcast.at_ref, bf16[768,1152]{1,0:T(8,128)(2,1)S(1)} %diffs.1.mine_ref, bf16[7168,512]{1,0:T(8,128)(2,1)} %bitcast.3.g0.g1, bf16[7168,512]{1,0:T(8,128)(2,1)} %bitcast.3.g0.g1, bf16[7168,512]{1,0:T(8,128)(2,1)} %bitcast.4.u0.u1, bf16[7168,512]{1,0:T(8,128)(2,1)} %bitcast.4.u0.u1), custom_call_target="tpu_custom_call" | custom-call | flops 2415919104 | bytes 10000000 | tf_op jit(solution)/shard_map/early_inputs/pallas_call | solution.py:276
  103.4 0.0 collective-permute-done.5.other_ref
  103.4 12.3 %inputs.1 = bf16[512,5504]{1,0:T(8,128)(2,1)S(1)} custom-call(s32[1]{0:T(128)} %bitcast.at_ref, bf16[768,1152]{1,0:T(8,128)(2,1)S(1)} %diffs.1.mine_ref, bf16[768,1152]{1,0:T(8,128)(2,1)S(1)} %collective-permute-done.5.other_ref, f32[768,1536]{1,0:T(8,128)S(1)} %early_inputs.1.early_ref, bf16[7168,512]{1,0:T(8,128)(2,1)} %bitcast.3.g0.g1, ...), custom_call_target="tpu_custom_call" | custom-call | flops 11274289152 | bytes 24000000 | tf_op jit(solution)/shard_map/inputs/pallas_call | solution.py:356
  115.8 71.2 %all_to_all.11 = bf16[64,8,5504]{2,1,0:T(8,128)(2,1)S(1)} all-to-all(bf16[64,8,5504]{2,1,0:T(8,128)(2,1)S(1)} %bitcast.17), channel_id=1, replica_groups=mesh['expert'=64,'seq'=2] {'expert'}, dimensions={0} | all-to-all | bytes 11272192 | tf_op jit(solution)/shard_map/all_to_all | solution.py:493
  187.0 1.9 combine_send.1
  188.9 2.4 %collective-permute-start.6 = (bf16[128,3584]{1,0:T(8,128)(2,1)S(1)}, bf16[128,3584]{1,0:T(8,128)(2,1)S(1)}, u32[]{:S(2)}, u32[]{:S(2)}) collective-permute-start(bf16[128,3584]{1,0:T(8,128)(2,1)S(1)} %combine_send.1), channel_id=1, source_target_pairs={{0,1},{1,0},{2,3},{3,2},{4,5},{5,4},{6,7},{7,6},{8,9},{9,8},{10,11... | collective-permute-start | bytes 2752520 | tf_op jit(solution)/shard_map/ppermute | solution.py:40
  191.3 3.2 %combine_keep.1 = (bf16[128,7168]{1,0:T(8,128)(2,1)}, bf16[8,128]{1,0:T(8,128)(2,1)}) custom-call(s32[1]{0:T(128)} %bitcast.at_ref, s32[8,256]{1,0:T(8,128)S(1)} %bitcast.27, bf16[512,256]{1,0:T(8,128)(2,1)S(1)} %get-tuple-element.15.pa_ref, bf16[512,512]{1,0:T(8,128)(2,1)S(1)} %get-tuple-element.16.pb_ref, bf16[768,512]{1,0:T(8,128)(2,1)S(1)} %get-tuple-element.17.w_ref, ...), custom_call_target="tpu_custom_call" | custom-call | flops 1000000000 | bytes 7000000 | tf_op jit(solution)/shard_map/combine_keep/pallas_call | solution.py:439
  194.5 0.0 collective-permute-done.6.came_ref
  194.5 1.0 join.1
  (1 shorter events, 0.0 us)
Async XLA Ops:
  0.6 5.1 %copy-start = (bf16[128,7168]{1,0:T(8,128)(2,1)S(1)}, bf16[128,7168]{1,0:T(8,128)(2,1)}, u32[]{:S(2)}) copy-start(bf16[128,7168]{1,0:T(8,128)(2,1)} %own1.1) | copy-start | bytes 5505028
  2.0 3.7 %collective-permute-start = (bf16[128,3584]{1,0:T(8,128)(2,1)S(1)}, bf16[128,3584]{1,0:T(8,128)(2,1)S(1)}, u32[]{:S(2)}, u32[]{:S(2)}) collective-permute-start(bf16[128,3584]{1,0:T(8,128)(2,1)S(1)} %constant_dynamic-slice_fusion), channel_id=1, source_target_pairs={{0,1},{1,0},{2,3},{3,2},{4,5},{5,4},{6,7},{7,6},{8,9},{9,8},{10,11... | collective-permute-start | bytes 2752520 | tf_op jit(solution)/shard_map/ppermute | solution.py:40
  3.5 0.7 copy-start.3
  4.2 0.7 copy-start.4
  4.9 4.8 %slice-start = ((s8[7340032]{0:T(1024)(128)(4,1)}), s8[4194304]{0:T(1024)(128)(4,1)S(1)}, s32[]{:S(2)}) async-start(s8[7340032]{0:T(1024)(128)(4,1)} %bitcast.19), calls=%async_computation.2 | async-start | bytes 8388608
  5.8 4.0 %slice-start.1 = ((s8[7340032]{0:T(1024)(128)(4,1)}), s8[3145728]{0:T(1024)(128)(4,1)S(1)}, s32[]{:S(2)}) async-start(s8[7340032]{0:T(1024)(128)(4,1)} %bitcast.19), calls=%async_computation.3 | async-start | bytes 6291456
  9.8 76.9 %collective-permute-start.1 = (bf16[512,7168]{1,0:T(8,128)(2,1)S(1)}, bf16[512,7168]{1,0:T(8,128)(2,1)S(1)}, u32[]{:S(2)}, u32[]{:S(2)}) collective-permute-start(bf16[512,7168]{1,0:T(8,128)(2,1)S(1)} %bitcast.21), channel_id=1, source_target_pairs={{0,1},{1,0},{2,3},{3,2},{4,5},{5,4},{6,7},{7,6},{8,9},{9,8},{10,11... | collective-permute-start | bytes 22020104 | tf_op jit(solution)/shard_map/ppermute | solution.py:40
  10.0 76.6 %collective-permute-start.2 = (bf16[7168,512]{1,0:T(8,128)(2,1)}, bf16[7168,512]{1,0:T(8,128)(2,1)S(1)}, u32[]{:S(2)}, u32[]{:S(2)}) collective-permute-start(bf16[7168,512]{1,0:T(8,128)(2,1)} %bitcast.3.g0.g1), channel_id=1, source_target_pairs={{0,1},{1,0},{2,3},{3,2},{4,5},{5,4},{6,7},{7,6},{8,9},{9,8},{10,11... | collective-permute-start | bytes 22020104 | tf_op jit(solution)/shard_map/ppermute | solution.py:40
  10.4 76.3 %collective-permute-start.3 = (bf16[7168,512]{1,0:T(8,128)(2,1)}, bf16[7168,512]{1,0:T(8,128)(2,1)S(1)}, u32[]{:S(2)}, u32[]{:S(2)}) collective-permute-start(bf16[7168,512]{1,0:T(8,128)(2,1)} %bitcast.4.u0.u1), channel_id=1, source_target_pairs={{0,1},{1,0},{2,3},{3,2},{4,5},{5,4},{6,7},{7,6},{8,9},{9,8},{10,11... | collective-permute-start | bytes 22020104 | tf_op jit(solution)/shard_map/ppermute | solution.py:40
  91.0 6.7 %copy-start.1 = (bf16[1,768,512]{2,1,0:T(8,128)(2,1)S(1)}, bf16[1,768,512]{2,1,0:T(8,128)(2,1)}, u32[]{:S(2)}) copy-start(bf16[1,768,512]{2,1,0:T(8,128)(2,1)} %param.11) | copy-start | bytes 2359300
  91.1 6.7 %copy-start.2 = (bf16[1,768,512]{2,1,0:T(8,128)(2,1)S(1)}, bf16[1,768,512]{2,1,0:T(8,128)(2,1)}, u32[]{:S(2)}) copy-start(bf16[1,768,512]{2,1,0:T(8,128)(2,1)} %param.12) | copy-start | bytes 2359300
  91.1 6.6 %collective-permute-start.4 = (f32[768,512]{1,0:T(8,128)S(1)}, f32[768,512]{1,0:T(8,128)S(1)}, u32[]{:S(2)}, u32[]{:S(2)}) collective-permute-start(f32[768,512]{1,0:T(8,128)S(1)} %hidden_other.1), channel_id=1, source_target_pairs={{0,1},{1,0},{2,3},{3,2},{4,5},{5,4},{6,7},{7,6},{8,9},{9,8},{10,11... | collective-permute-start | bytes 4718600 | tf_op jit(solution)/shard_map/ppermute | solution.py:40
  98.8 4.6 %collective-permute-start.5 = (bf16[768,1152]{1,0:T(8,128)(2,1)S(1)}, bf16[768,1152]{1,0:T(8,128)(2,1)S(1)}, u32[]{:S(2)}, u32[]{:S(2)}) collective-permute-start(bf16[768,1152]{1,0:T(8,128)(2,1)S(1)} %diffs.1.mine_ref), channel_id=1, source_target_pairs={{0,1},{1,0},{2,3},{3,2},{4,5},{5,4},{6,7},{7,6},{8,9},{9,8},{10,11... | collective-permute-start | bytes 5308424 | tf_op jit(solution)/shard_map/ppermute | solution.py:40
  188.9 5.6 %collective-permute-start.6 = (bf16[128,3584]{1,0:T(8,128)(2,1)S(1)}, bf16[128,3584]{1,0:T(8,128)(2,1)S(1)}, u32[]{:S(2)}, u32[]{:S(2)}) collective-permute-start(bf16[128,3584]{1,0:T(8,128)(2,1)S(1)} %combine_send.1), channel_id=1, source_target_pairs={{0,1},{1,0},{2,3},{3,2},{4,5},{5,4},{6,7},{7,6},{8,9},{9,8},{10,11... | collective-permute-start | bytes 2752520 | tf_op jit(solution)/shard_map/ppermute | solution.py:40

commit v5 on v4

--- a/solution.py
+++ b/solution.py
@@ -13,7 +13,7 @@
 MIB = 1024 * 1024
 LIMIT = 14 * MIB
 TILE = 256
-EARLY = 3
+EARLY = 2
 
 
 def iota(shape, dim):
@@ -107,53 +107,43 @@
     )(at, ids_t, ids_t, weights_t, weights_t)
 
 
-def dispatch_kernel(at_ref, pa_ref, pb_ref, own0, own1, other0, other1, out_ref):
+def dispatch_kernel(at_ref, pa_ref, pb_ref, own_ref, other_ref, out_ref):
     step = pl.program_id(0)
-    tile = own0.shape[1]
+    part = other_ref.shape[1]
+    tile = part // 4
     cols = pl.ds(pl.multiple_of(step * tile, 128), tile)
-    first = jnp.concatenate([own0[...], other0[...]], axis=0)
+
+    def tokens(index):
+        own = pl.ds(pl.multiple_of(at_ref[0] * part + index * tile, 128), tile)
+        other = pl.ds(pl.multiple_of(index * tile, 128), tile)
+        return [own_ref[:, own], other_ref[:, other]]
 
     @pl.when(step < 4)
     def _():
-        out_ref[:, cols] = dot(pa_ref[...], first).astype(BF16)
+        out_ref[:, cols] = dot(pa_ref[...], jnp.concatenate(tokens(step), axis=0)).astype(BF16)
 
     @pl.when(step >= 4)
     def _():
-        both = jnp.concatenate([first, own1[...], other1[...]], axis=0)
+        both = jnp.concatenate(tokens(step - 4) + tokens(step - 2), axis=0)
         out_ref[:, cols] = dot(pb_ref[...], both).astype(BF16)
 
 
 def dispatch(at, pa, pb, out_grad, other):
-    local, width = out_grad.shape
     rows = pa.shape[0]
-    tile = width // 8
-
-    def low(j):
-        return jnp.where(j < 4, j, j - 4)
-
-    def high(j):
-        return jnp.maximum(j - 2, 2)
-
+    whole = pl.BlockSpec(memory_space=pltpu.VMEM)
     return pl.pallas_call(
         dispatch_kernel,
         grid_spec=pltpu.PrefetchScalarGridSpec(
             num_scalar_prefetch=1,
             grid=(6,),
-            in_specs=[
-                pl.BlockSpec(pa.shape, lambda j, at: (0, 0)),
-                pl.BlockSpec(pb.shape, lambda j, at: (0, 0)),
-                pl.BlockSpec((local, tile), lambda j, at: (0, 4 * at[0] + low(j))),
-                pl.BlockSpec((local, tile), lambda j, at: (0, 4 * at[0] + high(j))),
-                pl.BlockSpec((local, tile), lambda j, at: (0, low(j))),
-                pl.BlockSpec((local, tile), lambda j, at: (0, high(j))),
-            ],
-            out_specs=pl.BlockSpec(memory_space=pltpu.VMEM),
-        ),
-        out_shape=jax.ShapeDtypeStruct((rows, 6 * tile), BF16),
+            in_specs=[whole] * 4,
+            out_specs=whole,
+        ),
+        out_shape=jax.ShapeDtypeStruct((rows, other.shape[1] // 2 * 3), BF16),
         compiler_params=params(),
         cost_estimate=pl.CostEstimate(flops=2 * 10**9, bytes_accessed=8 * 10**6, transcendentals=0),
         name="dispatch",
-    )(at, pa, pb, out_grad, out_grad, other, other)
+    )(at, pa, pb, out_grad, other)
 
 
 def hidden_kernel(at_ref, x_ref, w_ref, out_ref):
@@ -203,28 +193,28 @@
 
 def diff_kernel(mine_ref, other_ref, gate_ref, up_ref, out_ref):
     units = mine_ref.shape[1]
-    grad = mine_ref[...] + other_ref[...]
-    value = gate_ref[...].astype(F32)
-    up = up_ref[...].astype(F32)
+    rows = pl.ds(pl.multiple_of(pl.program_id(0) * TILE, TILE), TILE)
+    grad = mine_ref[rows, :] + other_ref[rows, :]
+    value = gate_ref[rows, :].astype(F32)
+    up = up_ref[rows, :].astype(F32)
     sigma = jax.nn.sigmoid(value)
     active = value * sigma
     slope = sigma * (1.0 + value * (1.0 - sigma))
     through = grad * active
     score = jnp.sum(through * up, axis=1, keepdims=True)
-    out_ref[:, :units] = (grad * up * slope).astype(BF16)
-    out_ref[:, units : 2 * units] = through.astype(BF16)
-    out_ref[:, 2 * units :] = jnp.broadcast_to(score, (score.shape[0], 128)).astype(BF16)
+    out_ref[rows, :units] = (grad * up * slope).astype(BF16)
+    out_ref[rows, units : 2 * units] = through.astype(BF16)
+    out_ref[rows, 2 * units :] = jnp.broadcast_to(score, (TILE, 128)).astype(BF16)
 
 
 def diffs(mine, other, gate, up):
     rows, units = mine.shape
-    tile = 256
-    spec = pl.BlockSpec((tile, units), lambda i: (i, 0))
+    whole = pl.BlockSpec(memory_space=pltpu.VMEM)
     return pl.pallas_call(
         diff_kernel,
-        grid=(rows // tile,),
-        in_specs=[spec] * 4,
-        out_specs=pl.BlockSpec((tile, 2 * units + 128), lambda i: (i, 0)),
+        grid=(rows // TILE,),
+        in_specs=[whole] * 4,
+        out_specs=whole,
         out_shape=jax.ShapeDtypeStruct((rows, 2 * units + 128), BF16),
         compiler_params=params(),
         cost_estimate=pl.CostEstimate(flops=0, bytes_accessed=0, transcendentals=0),
@@ -291,17 +281,18 @@
 
 
 def inputs_kernel(
-    at_ref, mine_ref, other_ref, early_ref, g0, g1, u0, u1, og_ref, ou_ref, out_ref
+    at_ref, mine_ref, other_ref, early_ref, g0, g1, u0, u1, og_ref, ou_ref, out_ref, sum_ref
 ):
     step = pl.program_id(0)
+    last = pl.num_programs(0) - 1
     units = g0.shape[1]
-    quarter = pl.num_programs(0) * TILE
-
-    def at_cols(start):
-        return pl.ds(pl.multiple_of(start + step * TILE, TILE), TILE)
+    quarter = last * TILE
+
+    def at_cols(tile, start):
+        return pl.ds(pl.multiple_of(start + tile * TILE, TILE), TILE)
 
     def far(start):
-        rows = at_cols(2 * quarter * at_ref[0] + start)
+        rows = at_cols(step, 2 * quarter * at_ref[0] + start)
         return [og_ref[rows, :], ou_ref[rows, :]]
 
     def product(x, low, high):
@@ -310,32 +301,48 @@
         )
         return lax.dot_general(x, w, NT, preferred_element_type=F32)
 
-    def finish(result):
-        low = parts_of(result[:, :TILE])
-        high = parts_of(result[:, TILE:])
-        out_ref[:, at_cols(0)] = low[0].astype(BF16)
-        out_ref[:, at_cols(quarter)] = high[0].astype(BF16)
-        out_ref[:, at_cols(2 * quarter)] = both_quarters(low, high).astype(BF16)
-
-    @pl.when(step < EARLY)
-    def _():
+    def early():
         cols = pl.ds(pl.multiple_of(step * 2 * TILE, TILE), 2 * TILE)
-        finish(product(other_ref[:, : 2 * units], far(0), far(quarter)) + early_ref[:, cols])
-
-    @pl.when(step >= EARLY)
-    def _():
+        far_terms = product(other_ref[:, : 2 * units], far(0), far(quarter))
+        sum_ref[step % 2] = far_terms + early_ref[:, cols]
+
+    def full():
         x = jnp.concatenate([mine_ref[:, : 2 * units], other_ref[:, : 2 * units]], axis=1)
         low = [g0[...], u0[...]] + far(0)
         high = [g1[...], u1[...]] + far(quarter)
-        finish(product(x, low, high))
+        sum_ref[step % 2] = product(x, low, high)
+
+    def finish():
+        tile = step - 1
+        result = sum_ref[tile % 2]
+        low = parts_of(result[:, :TILE])
+        high = parts_of(result[:, TILE:])
+        out_ref[:, at_cols(tile, 0)] = low[0].astype(BF16)
+        out_ref[:, at_cols(tile, quarter)] = high[0].astype(BF16)
+        out_ref[:, at_cols(tile, 2 * quarter)] = both_quarters(low, high).astype(BF16)
 
     @pl.when(step == 0)
     def _():
+        early()
         score = mine_ref[:, 2 * units :].astype(F32) + other_ref[:, 2 * units :].astype(F32)
         score = parts_of(score)
         lane = iota(score[0].shape, 1)
         end = out_ref.shape[1] - 128
         out_ref[:, end:] = jnp.where(lane == 0, score[0], both_quarters(score, score)).astype(BF16)
+
+    @pl.when((step > 0) & (step < EARLY))
+    def _():
+        finish()
+        early()
+
+    @pl.when((step >= EARLY) & (step < last))
+    def _():
+        finish()
+        full()
+
+    @pl.when(step == last)
+    def _():
+        finish()
 
 
 def inputs(at, mine, other, early, w_gate, w_up, gate_other, up_other):
@@ -349,7 +356,7 @@
     def block(shift):
         return pl.BlockSpec(
             (TILE, units),
-            lambda j, at: (at[0] * 2 * steps + shift * steps + jnp.maximum(j, EARLY), 0),
+            lambda j, at: (at[0] * 2 * steps + shift * steps + jnp.clip(j, EARLY, steps - 1), 0),
         )
 
     whole = pl.BlockSpec(memory_space=pltpu.VMEM)
@@ -357,9 +364,10 @@
         inputs_kernel,
         grid_spec=pltpu.PrefetchScalarGridSpec(
             num_scalar_prefetch=1,
-            grid=(steps,),
+            grid=(steps + 1,),
             in_specs=[whole] * 3 + [block(0), block(1), block(0), block(1), whole, whole],
             out_specs=whole,
+            scratch_shapes=[pltpu.VMEM((2, rows, 2 * TILE), F32)],
         ),
         out_shape=jax.ShapeDtypeStruct((main, 3 * TILE * steps + 128), BF16),
         compiler_params=params(),

time: 196 us -> 197 us (level)
  transfers between devices with their start and end apart: 7 -> 7, of which waited for: 0 -> 1; matrix products, arithmetic and copies ran while one was open for 0% -> 0% of each run, Pallas kernels for 7% -> 6%
where the time goes in v5:
time: 197 us
  blocking collectives  148 us (75%)
  Pallas kernels  37.7 us (19%)
  starting transfers between devices  6.86 us (3%)
  local copies, waits for them, and re-layouts  2.82 us (1%)
    all_to_all x2, blocking collectives, exchange(): lax.all_to_all(value.reshape(groups, MAIN, lanes), 'expert', split_axis=0...  148 us
    pallas_call x1, Pallas kernels, inputs(): pl.pallas_call(inputs_kernel, grid_spec=pltpu.PrefetchScalarGridSpec(num_...  14.3 us
    pallas_call x2, Pallas kernels, hidden(): pl.pallas_call(hidden_kernel, grid_spec=pltpu.PrefetchScalarGridSpec(num_...  8.7 us
    ppermute x7, starting transfers between devices, swap(): return lax.ppermute(value, 'seq', [(0, 1), (1, 0)])  6.86 us
  transfers between devices with their start and end apart: 7, of which 1 were waited for; matrix products, arithmetic and copies ran while one was open for 0% of the time, Pallas kernels for 6%

profile of v5, /device:TPU:1, one launch (start us, length us, event | category | flops | bytes accessed | tf_op | source)
XLA Modules:
  0.0 196.9 jit_solution(18256927919682801168)
XLA Ops:
  0.6 0.0 copy-start
  0.6 0.0 slice-start
  0.7 1.4 constant_dynamic-slice_fusion
  2.1 1.5 collective-permute-start
  3.6 0.0 copy-start.3
  3.6 0.7 copy-done.3
  4.3 0.0 copy-start.5
  4.3 0.7 copy-done.5
  5.0 0.8 routes.1
  5.8 0.0 collective-permute-done.other_ref
  5.8 0.0 copy-done
  5.8 0.0 slice-start.1
  5.8 3.3 %dispatch.1 = bf16[512,5376]{1,0:T(8,128)(2,1)S(1)} custom-call(s32[1]{0:T(128)} %bitcast.at_ref, bf16[512,256]{1,0:T(8,128)(2,1)S(1)} %get-tuple-element.15.pa_ref, bf16[512,512]{1,0:T(8,128)(2,1)S(1)} %get-tuple-element.16.pb_ref, bf16[128,7168]{1,0:T(8,128)(2,1)S(1)} %copy-done, bf16[128,3584]{1,0:T(8,128)(2,1)S(1)} %collective-permute-done.other_ref), custom_call_target="tpu_custom_call" | custom-call | flops 2000000000 | bytes 8000000 | tf_op jit(solution)/shard_map/dispatch/pallas_call | solution.py:134
  9.2 0.0 slice-done
  9.2 0.0 slice-done.1
  9.2 0.6 collective-permute-start.1
  9.8 0.1 collective-permute-start.2
  9.9 0.4 collective-permute-start.3
  10.3 76.4 %all_to_all.10 = bf16[64,8,5376]{2,1,0:T(8,128)(2,1)S(1)} all-to-all(bf16[64,8,5376]{2,1,0:T(8,128)(2,1)S(1)} %bitcast.18), channel_id=1, replica_groups=mesh['expert'=64,'seq'=2] {'expert'}, dimensions={0} | all-to-all | bytes 11010048 | tf_op jit(solution)/shard_map/all_to_all | solution.py:501
  86.7 0.0 collective-permute-done.1.w_ref
  86.8 0.0 collective-permute-done.2.og_ref
  86.8 0.0 collective-permute-done.3.ou_ref
  86.8 4.4 %hidden_other.1 = f32[768,512]{1,0:T(8,128)S(1)} custom-call(s32[1]{0:T(128)} %bitcast.at_ref, bf16[512,5376]{1,0:T(8,128)(2,1)S(1)} %bitcast.15, bf16[512,7168]{1,0:T(8,128)(2,1)S(1)} %collective-permute-done.1.w_ref), custom_call_target="tpu_custom_call" | custom-call | tf_op jit(solution)/shard_map/hidden_other/pallas_call | solution.py:179
  91.1 0.0 copy-start.1
  91.1 0.0 copy-start.2
  91.2 2.0 %collective-permute-start.4 = (f32[768,512]{1,0:T(8,128)S(1)}, f32[768,512]{1,0:T(8,128)S(1)}, u32[]{:S(2)}, u32[]{:S(2)}) collective-permute-start(f32[768,512]{1,0:T(8,128)S(1)} %hidden_other.1), channel_id=1, source_target_pairs={{0,1},{1,0},{2,3},{3,2},{4,5},{5,4},{6,7},{7,6},{8,9},{9,8},{10,11... | collective-permute-start | bytes 4718600 | tf_op jit(solution)/shard_map/ppermute | solution.py:40
  93.2 4.3 %hidden_own.1.mine_ref = f32[768,512]{1,0:T(8,128)S(1)} custom-call(s32[1]{0:T(128)} %bitcast.at_ref, bf16[512,5376]{1,0:T(8,128)(2,1)S(1)} %bitcast.16, bf16[512,7168]{1,0:T(8,128)(2,1)S(1)} %bitcast.22), custom_call_target="tpu_custom_call" | custom-call | tf_op jit(solution)/shard_map/hidden_own/pallas_call | solution.py:179
  97.5 0.0 collective-permute-done.4.other_ref
  97.5 0.0 copy-done.1
  97.5 0.0 copy-done.2
  97.5 1.1 diffs.1.mine_ref
  98.6 0.1 collective-permute-start.5
  98.7 3.3 %early_inputs.1.early_ref = f32[768,1024]{1,0:T(8,128)S(1)} custom-call(s32[1]{0:T(128)} %bitcast.at_ref, bf16[768,1152]{1,0:T(8,128)(2,1)S(1)} %diffs.1.mine_ref, bf16[7168,512]{1,0:T(8,128)(2,1)} %bitcast.31, bf16[7168,512]{1,0:T(8,128)(2,1)} %bitcast.32, bf16[7168,512]{1,0:T(8,128)(2,1)} %bitcast.36, bf16[7168,512]{1,0:T(8,128)(2,1)} %bitcast.37), custom_call_target="tpu_custom_call" | custom-call | flops 1610612736 | bytes 10000000 | tf_op jit(solution)/shard_map/early_inputs/pallas_call | solution.py:266
  102.0 0.4 collective-permute-done.5.other_ref
  102.4 14.3 %inputs.1 = bf16[512,5504]{1,0:T(8,128)(2,1)S(1)} custom-call(s32[1]{0:T(128)} %bitcast.at_ref, bf16[768,1152]{1,0:T(8,128)(2,1)S(1)} %diffs.1.mine_ref, bf16[768,1152]{1,0:T(8,128)(2,1)S(1)} %collective-permute-done.5.other_ref, f32[768,1024]{1,0:T(8,128)S(1)} %early_inputs.1.early_ref, bf16[7168,512]{1,0:T(8,128)(2,1)} %bitcast.33, ...), custom_call_target="tpu_custom_call" | custom-call | flops 11274289152 | bytes 24000000 | tf_op jit(solution)/shard_map/inputs/pallas_call | solution.py:363
  116.7 71.9 %all_to_all.11 = bf16[64,8,5504]{2,1,0:T(8,128)(2,1)S(1)} all-to-all(bf16[64,8,5504]{2,1,0:T(8,128)(2,1)S(1)} %bitcast.17), channel_id=1, replica_groups=mesh['expert'=64,'seq'=2] {'expert'}, dimensions={0} | all-to-all | bytes 11272192 | tf_op jit(solution)/shard_map/all_to_all | solution.py:501
  188.6 0.0 copy-start.4
  188.6 1.9 combine_send.1
  190.5 2.1 %collective-permute-start.6 = (bf16[128,3584]{1,0:T(8,128)(2,1)S(1)}, bf16[128,3584]{1,0:T(8,128)(2,1)S(1)}, u32[]{:S(2)}, u32[]{:S(2)}) collective-permute-start(bf16[128,3584]{1,0:T(8,128)(2,1)S(1)} %combine_send.1), channel_id=1, source_target_pairs={{0,1},{1,0},{2,3},{3,2},{4,5},{5,4},{6,7},{7,6},{8,9},{9,8},{10,11... | collective-permute-start | bytes 2752520 | tf_op jit(solution)/shard_map/ppermute | solution.py:40
  192.7 0.0 copy-done.4
  192.7 3.2 %combine_keep.1 = (bf16[128,7168]{1,0:T(8,128)(2,1)}, bf16[8,128]{1,0:T(8,128)(2,1)}) custom-call(s32[1]{0:T(128)} %bitcast.at_ref, s32[8,256]{1,0:T(8,128)S(1)} %bitcast.27, bf16[512,256]{1,0:T(8,128)(2,1)S(1)} %get-tuple-element.15.pa_ref, bf16[512,512]{1,0:T(8,128)(2,1)S(1)} %get-tuple-element.16.pb_ref, bf16[768,512]{1,0:T(8,128)(2,1)S(1)} %get-tuple-element.17.w_ref, ...), custom_call_target="tpu_custom_call" | custom-call | flops 1000000000 | bytes 7000000 | tf_op jit(solution)/shard_map/combine_keep/pallas_call | solution.py:447
  195.9 0.0 collective-permute-done.6.came_ref
  195.9 1.0 join.1
  (1 shorter events, 0.0 us)
Async XLA Ops:
  0.6 5.2 %copy-start = (bf16[128,7168]{1,0:T(8,128)(2,1)S(1)}, bf16[128,7168]{1,0:T(8,128)(2,1)}, u32[]{:S(2)}) copy-start(bf16[128,7168]{1,0:T(8,128)(2,1)} %own_ref.1) | copy-start | bytes 5505028
  0.6 8.5 %slice-start = ((s8[7340032]{0:T(1024)(128)(4,1)}), s8[4194304]{0:T(1024)(128)(4,1)S(1)}, s32[]{:S(2)}) async-start(s8[7340032]{0:T(1024)(128)(4,1)} %bitcast.19), calls=%async_computation.2 | async-start | bytes 8388608
  2.1 3.7 %collective-permute-start = (bf16[128,3584]{1,0:T(8,128)(2,1)S(1)}, bf16[128,3584]{1,0:T(8,128)(2,1)S(1)}, u32[]{:S(2)}, u32[]{:S(2)}) collective-permute-start(bf16[128,3584]{1,0:T(8,128)(2,1)S(1)} %constant_dynamic-slice_fusion), channel_id=1, source_target_pairs={{0,1},{1,0},{2,3},{3,2},{4,5},{5,4},{6,7},{7,6},{8,9},{9,8},{10,11... | collective-permute-start | bytes 2752520 | tf_op jit(solution)/shard_map/ppermute | solution.py:40
  3.6 0.7 copy-start.3
  4.3 0.7 copy-start.5
  5.8 3.4 %slice-start.1 = ((s8[7340032]{0:T(1024)(128)(4,1)}), s8[3145728]{0:T(1024)(128)(4,1)S(1)}, s32[]{:S(2)}) async-start(s8[7340032]{0:T(1024)(128)(4,1)} %bitcast.19), calls=%async_computation.3 | async-start | bytes 6291456
  9.2 77.6 %collective-permute-start.1 = (bf16[512,7168]{1,0:T(8,128)(2,1)S(1)}, bf16[512,7168]{1,0:T(8,128)(2,1)S(1)}, u32[]{:S(2)}, u32[]{:S(2)}) collective-permute-start(bf16[512,7168]{1,0:T(8,128)(2,1)S(1)} %bitcast.21), channel_id=1, source_target_pairs={{0,1},{1,0},{2,3},{3,2},{4,5},{5,4},{6,7},{7,6},{8,9},{9,8},{10,11... | collective-permute-start | bytes 22020104 | tf_op jit(solution)/shard_map/ppermute | solution.py:40
  9.8 77.0 %collective-permute-start.2 = (bf16[7168,512]{1,0:T(8,128)(2,1)}, bf16[7168,512]{1,0:T(8,128)(2,1)S(1)}, u32[]{:S(2)}, u32[]{:S(2)}) collective-permute-start(bf16[7168,512]{1,0:T(8,128)(2,1)} %bitcast.30), channel_id=1, source_target_pairs={{0,1},{1,0},{2,3},{3,2},{4,5},{5,4},{6,7},{7,6},{8,9},{9,8},{10,11... | collective-permute-start | bytes 22020104 | tf_op jit(solution)/shard_map/ppermute | solution.py:40
  9.9 76.9 %collective-permute-start.3 = (bf16[7168,512]{1,0:T(8,128)(2,1)}, bf16[7168,512]{1,0:T(8,128)(2,1)S(1)}, u32[]{:S(2)}, u32[]{:S(2)}) collective-permute-start(bf16[7168,512]{1,0:T(8,128)(2,1)} %bitcast.35), channel_id=1, source_target_pairs={{0,1},{1,0},{2,3},{3,2},{4,5},{5,4},{6,7},{7,6},{8,9},{9,8},{10,11... | collective-permute-start | bytes 22020104 | tf_op jit(solution)/shard_map/ppermute | solution.py:40
  91.1 6.4 %copy-start.1 = (bf16[1,768,512]{2,1,0:T(8,128)(2,1)S(1)}, bf16[1,768,512]{2,1,0:T(8,128)(2,1)}, u32[]{:S(2)}) copy-start(bf16[1,768,512]{2,1,0:T(8,128)(2,1)} %param.11) | copy-start | bytes 2359300
  91.1 6.4 %copy-start.2 = (bf16[1,768,512]{2,1,0:T(8,128)(2,1)S(1)}, bf16[1,768,512]{2,1,0:T(8,128)(2,1)}, u32[]{:S(2)}) copy-start(bf16[1,768,512]{2,1,0:T(8,128)(2,1)} %param.12) | copy-start | bytes 2359300
  91.2 6.3 %collective-permute-start.4 = (f32[768,512]{1,0:T(8,128)S(1)}, f32[768,512]{1,0:T(8,128)S(1)}, u32[]{:S(2)}, u32[]{:S(2)}) collective-permute-start(f32[768,512]{1,0:T(8,128)S(1)} %hidden_other.1), channel_id=1, source_target_pairs={{0,1},{1,0},{2,3},{3,2},{4,5},{5,4},{6,7},{7,6},{8,9},{9,8},{10,11... | collective-permute-start | bytes 4718600 | tf_op jit(solution)/shard_map/ppermute | solution.py:40
  98.6 3.8 %collective-permute-start.5 = (bf16[768,1152]{1,0:T(8,128)(2,1)S(1)}, bf16[768,1152]{1,0:T(8,128)(2,1)S(1)}, u32[]{:S(2)}, u32[]{:S(2)}) collective-permute-start(bf16[768,1152]{1,0:T(8,128)(2,1)S(1)} %diffs.1.mine_ref), channel_id=1, source_target_pairs={{0,1},{1,0},{2,3},{3,2},{4,5},{5,4},{6,7},{7,6},{8,9},{9,8},{10,11... | collective-permute-start | bytes 5308424 | tf_op jit(solution)/shard_map/ppermute | solution.py:40
  188.6 4.1 %copy-start.4 = (s32[256,8]{0,1:T(8,128)S(1)}, s32[256,8]{0,1:T(8,128)}, u32[]{:S(2)}) copy-start(s32[256,8]{0,1:T(8,128)} %param.9) | copy-start | bytes 24580
  190.5 5.4 %collective-permute-start.6 = (bf16[128,3584]{1,0:T(8,128)(2,1)S(1)}, bf16[128,3584]{1,0:T(8,128)(2,1)S(1)}, u32[]{:S(2)}, u32[]{:S(2)}) collective-permute-start(bf16[128,3584]{1,0:T(8,128)(2,1)S(1)} %combine_send.1), channel_id=1, source_target_pairs={{0,1},{1,0},{2,3},{3,2},{4,5},{5,4},{6,7},{7,6},{8,9},{9,8},{10,11... | collective-permute-start | bytes 2752520 | tf_op jit(solution)/shard_map/ppermute | solution.py:40

commit v6 on v5

--- a/solution.py
+++ b/solution.py
@@ -192,8 +192,24 @@
 
 
 def diff_kernel(mine_ref, other_ref, gate_ref, up_ref, out_ref):
-    units = mine_ref.shape[1]
-    rows = pl.ds(pl.multiple_of(pl.program_id(0) * TILE, TILE), TILE)
+    step = pl.program_id(0)
+    total, units = mine_ref.shape
+    count = total // pl.num_programs(0)
+    pairs = count // 24
+    rows = pl.ds(pl.multiple_of(step * count, count), count)
+    main_rows = pl.ds(pl.multiple_of(step * 16 * pairs, 16 * pairs), 16 * pairs)
+    rest_rows = pl.ds(pl.multiple_of(total // 3 * 2 + step * 8 * pairs, 8 * pairs), 8 * pairs)
+
+    def put(value, low):
+        lanes = value.shape[1]
+        value = value.reshape(pairs, 3, 8, lanes)
+        top = iota((pairs, 8, lanes), 1) < REST
+        odd = jnp.where(top, pltpu.roll(value[:, 1], REST, 1), pltpu.roll(value[:, 2], REST, 1))
+        main = jnp.stack([value[:, 0], odd], axis=1).reshape(16 * pairs, lanes)
+        rest = jnp.where(top, value[:, 1], value[:, 2]).reshape(8 * pairs, lanes)
+        out_ref[main_rows, low : low + lanes] = main.astype(BF16)
+        out_ref[rest_rows, low : low + lanes] = rest.astype(BF16)
+
     grad = mine_ref[rows, :] + other_ref[rows, :]
     value = gate_ref[rows, :].astype(F32)
     up = up_ref[rows, :].astype(F32)
@@ -202,9 +218,9 @@
     slope = sigma * (1.0 + value * (1.0 - sigma))
     through = grad * active
     score = jnp.sum(through * up, axis=1, keepdims=True)
-    out_ref[rows, :units] = (grad * up * slope).astype(BF16)
-    out_ref[rows, units : 2 * units] = through.astype(BF16)
-    out_ref[rows, 2 * units :] = jnp.broadcast_to(score, (TILE, 128)).astype(BF16)
+    put(grad * up * slope, 0)
+    put(through, units)
+    put(jnp.broadcast_to(score, (count, 128)), 2 * units)
 
 
 def diffs(mine, other, gate, up):
@@ -212,7 +228,7 @@
     whole = pl.BlockSpec(memory_space=pltpu.VMEM)
     return pl.pallas_call(
         diff_kernel,
-        grid=(rows // TILE,),
+        grid=(2,),
         in_specs=[whole] * 4,
         out_specs=whole,
         out_shape=jax.ShapeDtypeStruct((rows, 2 * units + 128), BF16),
@@ -222,21 +238,15 @@
     )(mine, other, gate, up)
 
 
-def parts_of(value):
-    rows, lanes = value.shape
-    pairs = rows // 24
-    value = value.reshape(pairs, 3, 8, lanes)
+def spread_rows(low, high):
+    rows, lanes = low.shape
+    pairs = rows // 8
+    low = low.reshape(pairs, 8, lanes)
+    high = high.reshape(pairs, 8, lanes)
     top = iota((pairs, 8, lanes), 1) < REST
-    odd = jnp.where(top, pltpu.roll(value[:, 1], REST, 1), pltpu.roll(value[:, 2], REST, 1))
-    main = jnp.stack([value[:, 0], odd], axis=1).reshape(16 * pairs, lanes)
-    return main, value[:, 1], value[:, 2]
-
-
-def both_quarters(low, high):
-    top = iota(low[1].shape, 1) < REST
-    even = jnp.where(top, low[1], pltpu.roll(high[1], REST, 1))
-    odd = jnp.where(top, pltpu.roll(low[2], REST, 1), high[2])
-    return jnp.stack([even, odd], axis=1).reshape(low[0].shape)
+    even = jnp.where(top, low, pltpu.roll(high, REST, 1))
+    odd = jnp.where(top, pltpu.roll(low, REST, 1), high)
+    return jnp.stack([even, odd], axis=1).reshape(2 * rows, lanes)
 
 
 def own_block(units, steps, shift):
@@ -281,18 +291,18 @@
 
 
 def inputs_kernel(
-    at_ref, mine_ref, other_ref, early_ref, g0, g1, u0, u1, og_ref, ou_ref, out_ref, sum_ref
+    at_ref, mine_ref, other_ref, early_ref, g0, g1, u0, u1, og_ref, ou_ref, out_ref
 ):
     step = pl.program_id(0)
-    last = pl.num_programs(0) - 1
     units = g0.shape[1]
-    quarter = last * TILE
-
-    def at_cols(tile, start):
-        return pl.ds(pl.multiple_of(start + tile * TILE, TILE), TILE)
+    main = out_ref.shape[0]
+    quarter = pl.num_programs(0) * TILE
+
+    def at_cols(start):
+        return pl.ds(pl.multiple_of(start + step * TILE, TILE), TILE)
 
     def far(start):
-        rows = at_cols(step, 2 * quarter * at_ref[0] + start)
+        rows = at_cols(2 * quarter * at_ref[0] + start)
         return [og_ref[rows, :], ou_ref[rows, :]]
 
     def product(x, low, high):
@@ -301,48 +311,31 @@
         )
         return lax.dot_general(x, w, NT, preferred_element_type=F32)
 
-    def early():
+    def finish(result):
+        out_ref[:, at_cols(0)] = result[:main, :TILE].astype(BF16)
+        out_ref[:, at_cols(quarter)] = result[:main, TILE:].astype(BF16)
+        rest = spread_rows(result[main:, :TILE], result[main:, TILE:])
+        out_ref[:, at_cols(2 * quarter)] = rest.astype(BF16)
+
+    @pl.when(step < EARLY)
+    def _():
         cols = pl.ds(pl.multiple_of(step * 2 * TILE, TILE), 2 * TILE)
-        far_terms = product(other_ref[:, : 2 * units], far(0), far(quarter))
-        sum_ref[step % 2] = far_terms + early_ref[:, cols]
-
-    def full():
+        finish(product(other_ref[:, : 2 * units], far(0), far(quarter)) + early_ref[:, cols])
+
+    @pl.when(step >= EARLY)
+    def _():
         x = jnp.concatenate([mine_ref[:, : 2 * units], other_ref[:, : 2 * units]], axis=1)
         low = [g0[...], u0[...]] + far(0)
         high = [g1[...], u1[...]] + far(quarter)
-        sum_ref[step % 2] = product(x, low, high)
-
-    def finish():
-        tile = step - 1
-        result = sum_ref[tile % 2]
-        low = parts_of(result[:, :TILE])
-        high = parts_of(result[:, TILE:])
-        out_ref[:, at_cols(tile, 0)] = low[0].astype(BF16)
-        out_ref[:, at_cols(tile, quarter)] = high[0].astype(BF16)
-        out_ref[:, at_cols(tile, 2 * quarter)] = both_quarters(low, high).astype(BF16)
+        finish(product(x, low, high))
 
     @pl.when(step == 0)
     def _():
-        early()
         score = mine_ref[:, 2 * units :].astype(F32) + other_ref[:, 2 * units :].astype(F32)
-        score = parts_of(score)
-        lane = iota(score[0].shape, 1)
+        rest = spread_rows(score[main:], score[main:])
+        lane = iota(rest.shape, 1)
         end = out_ref.shape[1] - 128
-        out_ref[:, end:] = jnp.where(lane == 0, score[0], both_quarters(score, score)).astype(BF16)
-
-    @pl.when((step > 0) & (step < EARLY))
-    def _():
-        finish()
-        early()
-
-    @pl.when((step >= EARLY) & (step < last))
-    def _():
-        finish()
-        full()
-
-    @pl.when(step == last)
-    def _():
-        finish()
+        out_ref[:, end:] = jnp.where(lane == 0, score[:main], rest).astype(BF16)
 
 
 def inputs(at, mine, other, early, w_gate, w_up, gate_other, up_other):
@@ -356,7 +349,7 @@
     def block(shift):
         return pl.BlockSpec(
             (TILE, units),
-            lambda j, at: (at[0] * 2 * steps + shift * steps + jnp.clip(j, EARLY, steps - 1), 0),
+            lambda j, at: (at[0] * 2 * steps + shift * steps + jnp.maximum(j, EARLY), 0),
         )
 
     whole = pl.BlockSpec(memory_space=pltpu.VMEM)
@@ -364,10 +357,9 @@
         inputs_kernel,
         grid_spec=pltpu.PrefetchScalarGridSpec(
             num_scalar_prefetch=1,
-            grid=(steps + 1,),
+            grid=(steps,),
             in_specs=[whole] * 3 + [block(0), block(1), block(0), block(1), whole, whole],
             out_specs=whole,
-            scratch_shapes=[pltpu.VMEM((2, rows, 2 * TILE), F32)],
         ),
         out_shape=jax.ShapeDtypeStruct((main, 3 * TILE * steps + 128), BF16),
         compiler_params=params(),

time: 197 us -> 196 us (level)
  no operation moved by 1% of the time
where the time goes in v6:
time: 196 us; the launch traced here: 195 us
  blocking collectives  148 us (76%)
  Pallas kernels  36.2 us (18%)
  starting transfers between devices  6.87 us (4%)
  local copies, waits for them, and re-layouts  2.82 us (1%)
    all_to_all x2, blocking collectives, exchange(): lax.all_to_all(value.reshape(groups, MAIN, lanes), 'expert', split_axis=0...  148 us
    pallas_call x1, Pallas kernels, inputs(): pl.pallas_call(inputs_kernel, grid_spec=pltpu.PrefetchScalarGridSpec(num_...  12.8 us
    pallas_call x2, Pallas kernels, hidden(): pl.pallas_call(hidden_kernel, grid_spec=pltpu.PrefetchScalarGridSpec(num_...  8.7 us
    ppermute x7, starting transfers between devices, swap(): return lax.ppermute(value, 'seq', [(0, 1), (1, 0)])  6.87 us
  transfers between devices with their start and end apart: 7, of which 1 were waited for; matrix products, arithmetic and copies ran while one was open for 0% of the time, Pallas kernels for 6%

profile of v6, /device:TPU:1, one launch (start us, length us, event | category | flops | bytes accessed | tf_op | source)
XLA Modules:
  0.0 195.5 jit_solution(14175843790725073122)
XLA Ops:
  0.6 0.0 copy-start
  0.6 0.0 slice-start
  0.7 1.4 constant_dynamic-slice_fusion
  2.1 1.5 collective-permute-start
  3.6 0.0 copy-start.3
  3.6 0.7 copy-done.3
  4.3 0.0 copy-start.5
  4.3 0.7 copy-done.5
  5.0 0.8 routes.1
  5.8 0.0 collective-permute-done.other_ref
  5.8 0.0 copy-done
  5.8 0.0 slice-start.1
  5.8 3.3 %dispatch.1 = bf16[512,5376]{1,0:T(8,128)(2,1)S(1)} custom-call(s32[1]{0:T(128)} %bitcast.at_ref, bf16[512,256]{1,0:T(8,128)(2,1)S(1)} %get-tuple-element.15.pa_ref, bf16[512,512]{1,0:T(8,128)(2,1)S(1)} %get-tuple-element.16.pb_ref, bf16[128,7168]{1,0:T(8,128)(2,1)S(1)} %copy-done, bf16[128,3584]{1,0:T(8,128)(2,1)S(1)} %collective-permute-done.other_ref), custom_call_target="tpu_custom_call" | custom-call | flops 2000000000 | bytes 8000000 | tf_op jit(solution)/shard_map/dispatch/pallas_call | solution.py:134
  9.2 0.0 slice-done
  9.2 0.0 slice-done.1
  9.2 0.6 collective-permute-start.1
  9.8 0.1 collective-permute-start.2
  9.9 0.4 collective-permute-start.3
  10.3 76.4 %all_to_all.10 = bf16[64,8,5376]{2,1,0:T(8,128)(2,1)S(1)} all-to-all(bf16[64,8,5376]{2,1,0:T(8,128)(2,1)S(1)} %bitcast.18), channel_id=1, replica_groups=mesh['expert'=64,'seq'=2] {'expert'}, dimensions={0} | all-to-all | bytes 11010048 | tf_op jit(solution)/shard_map/all_to_all | solution.py:493
  86.7 0.0 collective-permute-done.1.w_ref
  86.8 0.0 collective-permute-done.2.og_ref
  86.8 0.0 collective-permute-done.3.ou_ref
  86.8 4.4 %hidden_other.1 = f32[768,512]{1,0:T(8,128)S(1)} custom-call(s32[1]{0:T(128)} %bitcast.at_ref, bf16[512,5376]{1,0:T(8,128)(2,1)S(1)} %bitcast.15, bf16[512,7168]{1,0:T(8,128)(2,1)S(1)} %collective-permute-done.1.w_ref), custom_call_target="tpu_custom_call" | custom-call | tf_op jit(solution)/shard_map/hidden_other/pallas_call | solution.py:179
  91.1 0.0 copy-start.1
  91.1 0.0 copy-start.2
  91.2 2.0 %collective-permute-start.4 = (f32[768,512]{1,0:T(8,128)S(1)}, f32[768,512]{1,0:T(8,128)S(1)}, u32[]{:S(2)}, u32[]{:S(2)}) collective-permute-start(f32[768,512]{1,0:T(8,128)S(1)} %hidden_other.1), channel_id=1, source_target_pairs={{0,1},{1,0},{2,3},{3,2},{4,5},{5,4},{6,7},{7,6},{8,9},{9,8},{10,11... | collective-permute-start | bytes 4718600 | tf_op jit(solution)/shard_map/ppermute | solution.py:40
  93.2 4.3 %hidden_own.1.mine_ref = f32[768,512]{1,0:T(8,128)S(1)} custom-call(s32[1]{0:T(128)} %bitcast.at_ref, bf16[512,5376]{1,0:T(8,128)(2,1)S(1)} %bitcast.16, bf16[512,7168]{1,0:T(8,128)(2,1)S(1)} %bitcast.22), custom_call_target="tpu_custom_call" | custom-call | tf_op jit(solution)/shard_map/hidden_own/pallas_call | solution.py:179
  97.5 0.0 collective-permute-done.4.other_ref
  97.5 0.0 copy-done.1
  97.5 0.0 copy-done.2
  97.5 1.2 diffs.1.mine_ref
  98.7 0.1 collective-permute-start.5
  98.8 3.3 %early_inputs.1.early_ref = f32[768,1024]{1,0:T(8,128)S(1)} custom-call(s32[1]{0:T(128)} %bitcast.at_ref, bf16[768,1152]{1,0:T(8,128)(2,1)S(1)} %diffs.1.mine_ref, bf16[7168,512]{1,0:T(8,128)(2,1)} %bitcast.31, bf16[7168,512]{1,0:T(8,128)(2,1)} %bitcast.32, bf16[7168,512]{1,0:T(8,128)(2,1)} %bitcast.36, bf16[7168,512]{1,0:T(8,128)(2,1)} %bitcast.37), custom_call_target="tpu_custom_call" | custom-call | flops 1610612736 | bytes 10000000 | tf_op jit(solution)/shard_map/early_inputs/pallas_call | solution.py:276
  102.1 0.4 collective-permute-done.5.other_ref
  102.5 12.8 %inputs.1 = bf16[512,5504]{1,0:T(8,128)(2,1)S(1)} custom-call(s32[1]{0:T(128)} %bitcast.at_ref, bf16[768,1152]{1,0:T(8,128)(2,1)S(1)} %diffs.1.mine_ref, bf16[768,1152]{1,0:T(8,128)(2,1)S(1)} %collective-permute-done.5.other_ref, f32[768,1024]{1,0:T(8,128)S(1)} %early_inputs.1.early_ref, bf16[7168,512]{1,0:T(8,128)(2,1)} %bitcast.33, ...), custom_call_target="tpu_custom_call" | custom-call | flops 11274289152 | bytes 24000000 | tf_op jit(solution)/shard_map/inputs/pallas_call | solution.py:356
  115.3 71.9 %all_to_all.11 = bf16[64,8,5504]{2,1,0:T(8,128)(2,1)S(1)} all-to-all(bf16[64,8,5504]{2,1,0:T(8,128)(2,1)S(1)} %bitcast.17), channel_id=1, replica_groups=mesh['expert'=64,'seq'=2] {'expert'}, dimensions={0} | all-to-all | bytes 11272192 | tf_op jit(solution)/shard_map/all_to_all | solution.py:493
  187.2 0.0 copy-start.4
  187.2 1.9 combine_send.1
  189.1 2.1 %collective-permute-start.6 = (bf16[128,3584]{1,0:T(8,128)(2,1)S(1)}, bf16[128,3584]{1,0:T(8,128)(2,1)S(1)}, u32[]{:S(2)}, u32[]{:S(2)}) collective-permute-start(bf16[128,3584]{1,0:T(8,128)(2,1)S(1)} %combine_send.1), channel_id=1, source_target_pairs={{0,1},{1,0},{2,3},{3,2},{4,5},{5,4},{6,7},{7,6},{8,9},{9,8},{10,11... | collective-permute-start | bytes 2752520 | tf_op jit(solution)/shard_map/ppermute | solution.py:40
  191.2 0.0 copy-done.4
  191.2 3.2 %combine_keep.1 = (bf16[128,7168]{1,0:T(8,128)(2,1)}, bf16[8,128]{1,0:T(8,128)(2,1)}) custom-call(s32[1]{0:T(128)} %bitcast.at_ref, s32[8,256]{1,0:T(8,128)S(1)} %bitcast.27, bf16[512,256]{1,0:T(8,128)(2,1)S(1)} %get-tuple-element.15.pa_ref, bf16[512,512]{1,0:T(8,128)(2,1)S(1)} %get-tuple-element.16.pb_ref, bf16[768,512]{1,0:T(8,128)(2,1)S(1)} %get-tuple-element.17.w_ref, ...), custom_call_target="tpu_custom_call" | custom-call | flops 1000000000 | bytes 7000000 | tf_op jit(solution)/shard_map/combine_keep/pallas_call | solution.py:439
  194.5 0.0 collective-permute-done.6.came_ref
  194.5 1.0 join.1
  (1 shorter events, 0.0 us)
Async XLA Ops:
  0.6 5.2 %copy-start = (bf16[128,7168]{1,0:T(8,128)(2,1)S(1)}, bf16[128,7168]{1,0:T(8,128)(2,1)}, u32[]{:S(2)}) copy-start(bf16[128,7168]{1,0:T(8,128)(2,1)} %own_ref.1) | copy-start | bytes 5505028
  0.6 8.5 %slice-start = ((s8[7340032]{0:T(1024)(128)(4,1)}), s8[4194304]{0:T(1024)(128)(4,1)S(1)}, s32[]{:S(2)}) async-start(s8[7340032]{0:T(1024)(128)(4,1)} %bitcast.19), calls=%async_computation.2 | async-start | bytes 8388608
  2.1 3.7 %collective-permute-start = (bf16[128,3584]{1,0:T(8,128)(2,1)S(1)}, bf16[128,3584]{1,0:T(8,128)(2,1)S(1)}, u32[]{:S(2)}, u32[]{:S(2)}) collective-permute-start(bf16[128,3584]{1,0:T(8,128)(2,1)S(1)} %constant_dynamic-slice_fusion), channel_id=1, source_target_pairs={{0,1},{1,0},{2,3},{3,2},{4,5},{5,4},{6,7},{7,6},{8,9},{9,8},{10,11... | collective-permute-start | bytes 2752520 | tf_op jit(solution)/shard_map/ppermute | solution.py:40
  3.6 0.7 copy-start.3
  4.3 0.7 copy-start.5
  5.8 3.4 %slice-start.1 = ((s8[7340032]{0:T(1024)(128)(4,1)}), s8[3145728]{0:T(1024)(128)(4,1)S(1)}, s32[]{:S(2)}) async-start(s8[7340032]{0:T(1024)(128)(4,1)} %bitcast.19), calls=%async_computation.3 | async-start | bytes 6291456
  9.2 77.6 %collective-permute-start.1 = (bf16[512,7168]{1,0:T(8,128)(2,1)S(1)}, bf16[512,7168]{1,0:T(8,128)(2,1)S(1)}, u32[]{:S(2)}, u32[]{:S(2)}) collective-permute-start(bf16[512,7168]{1,0:T(8,128)(2,1)S(1)} %bitcast.21), channel_id=1, source_target_pairs={{0,1},{1,0},{2,3},{3,2},{4,5},{5,4},{6,7},{7,6},{8,9},{9,8},{10,11... | collective-permute-start | bytes 22020104 | tf_op jit(solution)/shard_map/ppermute | solution.py:40
  9.8 77.0 %collective-permute-start.2 = (bf16[7168,512]{1,0:T(8,128)(2,1)}, bf16[7168,512]{1,0:T(8,128)(2,1)S(1)}, u32[]{:S(2)}, u32[]{:S(2)}) collective-permute-start(bf16[7168,512]{1,0:T(8,128)(2,1)} %bitcast.30), channel_id=1, source_target_pairs={{0,1},{1,0},{2,3},{3,2},{4,5},{5,4},{6,7},{7,6},{8,9},{9,8},{10,11... | collective-permute-start | bytes 22020104 | tf_op jit(solution)/shard_map/ppermute | solution.py:40
  9.9 76.9 %collective-permute-start.3 = (bf16[7168,512]{1,0:T(8,128)(2,1)}, bf16[7168,512]{1,0:T(8,128)(2,1)S(1)}, u32[]{:S(2)}, u32[]{:S(2)}) collective-permute-start(bf16[7168,512]{1,0:T(8,128)(2,1)} %bitcast.35), channel_id=1, source_target_pairs={{0,1},{1,0},{2,3},{3,2},{4,5},{5,4},{6,7},{7,6},{8,9},{9,8},{10,11... | collective-permute-start | bytes 22020104 | tf_op jit(solution)/shard_map/ppermute | solution.py:40
  91.1 6.4 %copy-start.1 = (bf16[1,768,512]{2,1,0:T(8,128)(2,1)S(1)}, bf16[1,768,512]{2,1,0:T(8,128)(2,1)}, u32[]{:S(2)}) copy-start(bf16[1,768,512]{2,1,0:T(8,128)(2,1)} %param.11) | copy-start | bytes 2359300
  91.1 6.4 %copy-start.2 = (bf16[1,768,512]{2,1,0:T(8,128)(2,1)S(1)}, bf16[1,768,512]{2,1,0:T(8,128)(2,1)}, u32[]{:S(2)}) copy-start(bf16[1,768,512]{2,1,0:T(8,128)(2,1)} %param.12) | copy-start | bytes 2359300
  91.2 6.3 %collective-permute-start.4 = (f32[768,512]{1,0:T(8,128)S(1)}, f32[768,512]{1,0:T(8,128)S(1)}, u32[]{:S(2)}, u32[]{:S(2)}) collective-permute-start(f32[768,512]{1,0:T(8,128)S(1)} %hidden_other.1), channel_id=1, source_target_pairs={{0,1},{1,0},{2,3},{3,2},{4,5},{5,4},{6,7},{7,6},{8,9},{9,8},{10,11... | collective-permute-start | bytes 4718600 | tf_op jit(solution)/shard_map/ppermute | solution.py:40
  98.7 3.8 %collective-permute-start.5 = (bf16[768,1152]{1,0:T(8,128)(2,1)S(1)}, bf16[768,1152]{1,0:T(8,128)(2,1)S(1)}, u32[]{:S(2)}, u32[]{:S(2)}) collective-permute-start(bf16[768,1152]{1,0:T(8,128)(2,1)S(1)} %diffs.1.mine_ref), channel_id=1, source_target_pairs={{0,1},{1,0},{2,3},{3,2},{4,5},{5,4},{6,7},{7,6},{8,9},{9,8},{10,11... | collective-permute-start | bytes 5308424 | tf_op jit(solution)/shard_map/ppermute | solution.py:40
  187.2 4.0 %copy-start.4 = (s32[256,8]{0,1:T(8,128)S(1)}, s32[256,8]{0,1:T(8,128)}, u32[]{:S(2)}) copy-start(s32[256,8]{0,1:T(8,128)} %param.9) | copy-start | bytes 24580
  189.1 5.4 %collective-permute-start.6 = (bf16[128,3584]{1,0:T(8,128)(2,1)S(1)}, bf16[128,3584]{1,0:T(8,128)(2,1)S(1)}, u32[]{:S(2)}, u32[]{:S(2)}) collective-permute-start(bf16[128,3584]{1,0:T(8,128)(2,1)S(1)} %combine_send.1), channel_id=1, source_target_pairs={{0,1},{1,0},{2,3},{3,2},{4,5},{5,4},{6,7},{7,6},{8,9},{9,8},{10,11... | collective-permute-start | bytes 2752520 | tf_op jit(solution)/shard_map/ppermute | solution.py:40

commit v7 on v6

--- a/solution.py
+++ b/solution.py
@@ -146,49 +146,65 @@
     )(at, pa, pb, out_grad, other)
 
 
-def hidden_kernel(at_ref, x_ref, w_ref, out_ref):
+def hidden_slots(at_ref, x_ref, rest_ref, w_ref, out_ref):
     step = pl.program_id(0)
     main = x_ref.shape[0]
     units = out_ref.shape[1]
-    part = w_ref.shape[1] // 2
-    quarter = part // 2
-
-    def product(low, high, start):
-        rows = pl.ds(pl.multiple_of(step * units, units), units)
-        cols = pl.ds(pl.multiple_of(at_ref[0] * part + start, 128), high - low)
-        return lax.dot_general(x_ref[:, low:high], w_ref[rows, cols], NT, preferred_element_type=F32)
-
+    part = rest_ref.shape[1]
+    rows = pl.ds(pl.multiple_of(step * units, units), units)
+    cols = pl.ds(pl.multiple_of(at_ref[0] * part, 128), part)
+    w = w_ref[rows, cols]
     pairs = main // 16
-    first = product(0, part, 0).reshape(pairs, 2, 8, units)
-    low = product(part, part + quarter, 0).reshape(pairs, 2, 8, units)
-    high = product(part, part + quarter, quarter).reshape(pairs, 2, 8, units)
+    first = lax.dot_general(x_ref[:, :part], w, NT, preferred_element_type=F32)
+    first = first.reshape(pairs, 2, 8, units)
+    rest = lax.dot_general(rest_ref[...], w, NT, preferred_element_type=F32)
+    rest = rest.reshape(pairs, 8, units)
     top = iota((pairs, 8, units), 1) < REST
-    even = low[:, 0] + pltpu.roll(high[:, 0], REST, 1)
-    odd = high[:, 1] + pltpu.roll(low[:, 1], REST, 1)
     turned = pltpu.roll(first[:, 1], REST, 1)
     out_ref[...] = jnp.stack(
-        [first[:, 0], jnp.where(top, even, turned), jnp.where(top, turned, odd)], axis=1
+        [first[:, 0], jnp.where(top, rest, turned), jnp.where(top, turned, rest)], axis=1
     ).reshape(main // 2 * 3, units)
 
 
-def hidden(at, x, w, name):
+def first_kernel(at_ref, x_ref, w_ref, out_ref, rest_ref):
+    rows, part = rest_ref.shape
+    pairs = rows // 8
+    quarter = part // 2
+
+    @pl.when(pl.program_id(0) == 0)
+    def _():
+        value = x_ref[:, part:].astype(F32).reshape(pairs, 2, 8, quarter)
+        top = iota((pairs, 8, quarter), 1) < REST
+        low = jnp.where(top, value[:, 0], pltpu.roll(value[:, 1], REST, 1))
+        high = jnp.where(top, pltpu.roll(value[:, 0], REST, 1), value[:, 1])
+        rest_ref[:, :quarter] = low.reshape(rows, quarter).astype(BF16)
+        rest_ref[:, quarter:] = high.reshape(rows, quarter).astype(BF16)
+
+    hidden_slots(at_ref, x_ref, rest_ref, w_ref, out_ref)
+
+
+def hidden(at, x, w, rest=None):
     rows, lanes = x.shape
     units = w.shape[0]
     tile = 256
     whole = pl.BlockSpec(memory_space=pltpu.VMEM)
-    return pl.pallas_call(
-        hidden_kernel,
+    out_spec = pl.BlockSpec((rows // 2 * 3, tile), lambda j, at: (0, j))
+    out_shape = jax.ShapeDtypeStruct((rows // 2 * 3, units), F32)
+    rest_shape = jax.ShapeDtypeStruct((rows // 2, lanes // 3 * 2), BF16)
+    first = rest is None
+    return pl.pallas_call(
+        first_kernel if first else hidden_slots,
         grid_spec=pltpu.PrefetchScalarGridSpec(
             num_scalar_prefetch=1,
             grid=(units // tile,),
-            in_specs=[whole, whole],
-            out_specs=pl.BlockSpec((rows // 2 * 3, tile), lambda j, at: (0, j)),
-        ),
-        out_shape=jax.ShapeDtypeStruct((rows // 2 * 3, units), F32),
+            in_specs=[whole] * (2 if first else 3),
+            out_specs=[out_spec, whole] if first else out_spec,
+        ),
+        out_shape=[out_shape, rest_shape] if first else out_shape,
         compiler_params=params(),
         cost_estimate=pl.CostEstimate(flops=0, bytes_accessed=0, transcendentals=0),
-        name=name,
-    )(at, x, w)
+        name="hidden_other" if first else "hidden_own",
+    )(*((at, x, w) if first else (at, x, rest, w)))
 
 
 def diff_kernel(mine_ref, other_ref, gate_ref, up_ref, out_ref):
@@ -512,8 +528,9 @@
     received, down_other, gate_other, up_other = lax.optimization_barrier(
         (received, down_other, gate_other, up_other)
     )
-    grad_other = swap(hidden(at, received, down_other, "hidden_other"))
-    grad_mine = hidden(at, received, w_down, "hidden_own")
+    grad_other, rest = hidden(at, received, down_other)
+    grad_other = swap(grad_other)
+    grad_mine = hidden(at, received, w_down, rest)
     mine = diffs(grad_mine, grad_other, gate_pre[0], up_pre[0])
     theirs = swap(mine)
     early = early_inputs(at, mine, w_gate, w_up)

time: 196 us -> 195 us (level)
  no operation moved by 1% of the time
where the time goes in v7:
time: 195 us; the launch traced here: 194 us
  blocking collectives  148 us (76%)
  Pallas kernels  35 us (18%)
  starting transfers between devices  6.93 us (4%)
  local copies, waits for them, and re-layouts  2.83 us (1%)
    all_to_all x2, blocking collectives, exchange(): lax.all_to_all(value.reshape(groups, MAIN, lanes), 'expert', split_axis=0...  148 us
    pallas_call x1, Pallas kernels, inputs(): pl.pallas_call(inputs_kernel, grid_spec=pltpu.PrefetchScalarGridSpec(num_...  12.8 us
    pallas_call x2, Pallas kernels, hidden(): pl.pallas_call(first_kernel if first else hidden_slots, grid_spec=pltpu.P...  7.41 us
    ppermute x7, starting transfers between devices, swap(): return lax.ppermute(value, 'seq', [(0, 1), (1, 0)])  6.93 us
  transfers between devices with their start and end apart: 7, of which 1 were waited for; matrix products, arithmetic and copies ran while one was open for 0% of the time, Pallas kernels for 6%

profile of v7, /device:TPU:1, one launch (start us, length us, event | category | flops | bytes accessed | tf_op | source)
XLA Modules:
  0.0 194.2 jit_solution(13067404783579987377)
XLA Ops:
  0.6 0.0 copy-start
  0.6 0.0 slice-start
  0.7 1.4 constant_dynamic-slice_fusion
  2.1 1.5 collective-permute-start
  3.6 0.0 copy-start.5
  3.6 0.7 copy-done.5
  4.3 0.0 copy-start.7
  4.3 0.7 copy-done.7
  5.0 0.8 routes.1
  5.8 0.0 copy-start.1
  5.8 0.0 collective-permute-done.other_ref
  5.8 0.0 copy-done
  5.8 0.0 slice-start.1
  5.8 3.3 %dispatch.1 = bf16[512,5376]{1,0:T(8,128)(2,1)S(1)} custom-call(s32[1]{0:T(128)} %bitcast.at_ref, bf16[512,256]{1,0:T(8,128)(2,1)S(1)} %get-tuple-element.17.pa_ref, bf16[512,512]{1,0:T(8,128)(2,1)S(1)} %get-tuple-element.18.pb_ref, bf16[128,7168]{1,0:T(8,128)(2,1)S(1)} %copy-done, bf16[128,3584]{1,0:T(8,128)(2,1)S(1)} %collective-permute-done.other_ref), custom_call_target="tpu_custom_call" | custom-call | flops 2000000000 | bytes 8000000 | tf_op jit(solution)/shard_map/dispatch/pallas_call | solution.py:134
  9.2 0.0 copy-done.1
  9.2 0.0 slice-done
  9.2 0.0 slice-done.1
  9.2 0.6 collective-permute-start.1
  9.8 0.1 collective-permute-start.2
  9.9 0.4 collective-permute-start.3
  10.3 76.4 %all_to_all.10 = bf16[64,8,5376]{2,1,0:T(8,128)(2,1)S(1)} all-to-all(bf16[64,8,5376]{2,1,0:T(8,128)(2,1)S(1)} %bitcast.18), channel_id=1, replica_groups=mesh['expert'=64,'seq'=2] {'expert'}, dimensions={0} | all-to-all | bytes 11010048 | tf_op jit(solution)/shard_map/all_to_all | solution.py:509
  86.8 0.0 collective-permute-done.1.w_ref
  86.8 0.0 collective-permute-done.2.og_ref
  86.8 0.0 collective-permute-done.3.ou_ref
  86.8 4.0 %hidden_other.1 = (f32[768,512]{1,0:T(8,128)S(1)}, bf16[256,3584]{1,0:T(8,128)(2,1)S(1)}) custom-call(s32[1]{0:T(128)} %bitcast.at_ref, bf16[512,5376]{1,0:T(8,128)(2,1)S(1)} %bitcast.15, bf16[512,7168]{1,0:T(8,128)(2,1)S(1)} %collective-permute-done.1.w_ref), custom_call_target="tpu_custom_call" | custom-call | tf_op jit(solution)/shard_map/hidden_other/pallas_call | solution.py:195
  90.8 2.0 %collective-permute-start.4 = (f32[768,512]{1,0:T(8,128)S(1)}, f32[768,512]{1,0:T(8,128)S(1)}, u32[]{:S(2)}, u32[]{:S(2)}) collective-permute-start(f32[768,512]{1,0:T(8,128)S(1)} %get-tuple-element.27), channel_id=1, source_target_pairs={{0,1},{1,0},{2,3},{3,2},{4,5},{5,4},{6,7},{7,6},{8,9},{9,8},{10,11... | collective-permute-start | bytes 4718600 | tf_op jit(solution)/shard_map/ppermute | solution.py:40
  92.8 0.0 copy-start.3
  92.8 0.0 copy-start.4
  92.8 3.4 %hidden_own.1.mine_ref = f32[768,512]{1,0:T(8,128)S(1)} custom-call(s32[1]{0:T(128)} %bitcast.at_ref, bf16[512,5376]{1,0:T(8,128)(2,1)S(1)} %bitcast.16, bf16[256,3584]{1,0:T(8,128)(2,1)S(1)} %get-tuple-element.26.rest_ref, bf16[512,7168]{1,0:T(8,128)(2,1)S(1)} %bitcast.22), custom_call_target="tpu_custom_call" | custom-call | tf_op jit(solution)/shard_map/hidden_own/pallas_call | solution.py:195
  96.2 0.0 collective-permute-done.4.other_ref
  96.2 0.0 copy-done.3
  96.2 0.0 copy-done.4
  96.3 1.2 diffs.1.mine_ref
  97.4 0.1 collective-permute-start.5
  97.6 3.3 %early_inputs.1.early_ref = f32[768,1024]{1,0:T(8,128)S(1)} custom-call(s32[1]{0:T(128)} %bitcast.at_ref, bf16[768,1152]{1,0:T(8,128)(2,1)S(1)} %diffs.1.mine_ref, bf16[7168,512]{1,0:T(8,128)(2,1)} %bitcast.31, bf16[7168,512]{1,0:T(8,128)(2,1)} %bitcast.32, bf16[7168,512]{1,0:T(8,128)(2,1)} %bitcast.36, bf16[7168,512]{1,0:T(8,128)(2,1)} %bitcast.37), custom_call_target="tpu_custom_call" | custom-call | flops 1610612736 | bytes 10000000 | tf_op jit(solution)/shard_map/early_inputs/pallas_call | solution.py:292
  100.9 0.3 collective-permute-done.5.other_ref
  101.2 12.8 %inputs.1 = bf16[512,5504]{1,0:T(8,128)(2,1)S(1)} custom-call(s32[1]{0:T(128)} %bitcast.at_ref, bf16[768,1152]{1,0:T(8,128)(2,1)S(1)} %diffs.1.mine_ref, bf16[768,1152]{1,0:T(8,128)(2,1)S(1)} %collective-permute-done.5.other_ref, f32[768,1024]{1,0:T(8,128)S(1)} %early_inputs.1.early_ref, bf16[7168,512]{1,0:T(8,128)(2,1)} %bitcast.33, ...), custom_call_target="tpu_custom_call" | custom-call | flops 11274289152 | bytes 24000000 | tf_op jit(solution)/shard_map/inputs/pallas_call | solution.py:372
  114.0 71.9 %all_to_all.11 = bf16[64,8,5504]{2,1,0:T(8,128)(2,1)S(1)} all-to-all(bf16[64,8,5504]{2,1,0:T(8,128)(2,1)S(1)} %bitcast.17), channel_id=1, replica_groups=mesh['expert'=64,'seq'=2] {'expert'}, dimensions={0} | all-to-all | bytes 11272192 | tf_op jit(solution)/shard_map/all_to_all | solution.py:509
  185.9 0.0 copy-start.2
  185.9 0.0 copy-start.6
  185.9 1.9 combine_send.1
  187.8 2.2 %collective-permute-start.6 = (bf16[128,3584]{1,0:T(8,128)(2,1)S(1)}, bf16[128,3584]{1,0:T(8,128)(2,1)S(1)}, u32[]{:S(2)}, u32[]{:S(2)}) collective-permute-start(bf16[128,3584]{1,0:T(8,128)(2,1)S(1)} %combine_send.1), channel_id=1, source_target_pairs={{0,1},{1,0},{2,3},{3,2},{4,5},{5,4},{6,7},{7,6},{8,9},{9,8},{10,11... | collective-permute-start | bytes 2752520 | tf_op jit(solution)/shard_map/ppermute | solution.py:40
  190.0 0.0 copy-done.2
  190.0 0.0 copy-done.6
  190.0 3.2 %combine_keep.1 = (bf16[128,7168]{1,0:T(8,128)(2,1)}, bf16[8,128]{1,0:T(8,128)(2,1)}) custom-call(s32[1]{0:T(128)} %bitcast.at_ref, s32[8,256]{1,0:T(8,128)S(1)} %bitcast.27, bf16[512,256]{1,0:T(8,128)(2,1)S(1)} %get-tuple-element.17.pa_ref, bf16[512,512]{1,0:T(8,128)(2,1)S(1)} %copy-done.2, bf16[768,512]{1,0:T(8,128)(2,1)S(1)} %get-tuple-element.19.w_ref, ...), custom_call_target="tpu_custom_call" | custom-call | flops 1000000000 | bytes 7000000 | tf_op jit(solution)/shard_map/combine_keep/pallas_call | solution.py:455
  193.2 0.0 collective-permute-done.6.came_ref
  193.2 1.0 join.1
  (1 shorter events, 0.0 us)
Async XLA Ops:
  0.6 5.2 %copy-start = (bf16[128,7168]{1,0:T(8,128)(2,1)S(1)}, bf16[128,7168]{1,0:T(8,128)(2,1)}, u32[]{:S(2)}) copy-start(bf16[128,7168]{1,0:T(8,128)(2,1)} %own_ref.1) | copy-start | bytes 5505028
  0.6 8.5 %slice-start = ((s8[7340032]{0:T(1024)(128)(4,1)}), s8[4194304]{0:T(1024)(128)(4,1)S(1)}, s32[]{:S(2)}) async-start(s8[7340032]{0:T(1024)(128)(4,1)} %bitcast.19), calls=%async_computation.2 | async-start | bytes 8388608
  2.1 3.8 %collective-permute-start = (bf16[128,3584]{1,0:T(8,128)(2,1)S(1)}, bf16[128,3584]{1,0:T(8,128)(2,1)S(1)}, u32[]{:S(2)}, u32[]{:S(2)}) collective-permute-start(bf16[128,3584]{1,0:T(8,128)(2,1)S(1)} %constant_dynamic-slice_fusion), channel_id=1, source_target_pairs={{0,1},{1,0},{2,3},{3,2},{4,5},{5,4},{6,7},{7,6},{8,9},{9,8},{10,11... | collective-permute-start | bytes 2752520 | tf_op jit(solution)/shard_map/ppermute | solution.py:40
  3.6 0.7 copy-start.5
  4.3 0.7 copy-start.7
  5.8 3.4 %copy-start.1 = (bf16[512,512]{1,0:T(8,128)(2,1)}, bf16[512,512]{1,0:T(8,128)(2,1)S(1)}, u32[]{:S(2)}) copy-start(bf16[512,512]{1,0:T(8,128)(2,1)S(1)} %get-tuple-element.18.pb_ref) | copy-start | bytes 1572868
  5.8 3.4 %slice-start.1 = ((s8[7340032]{0:T(1024)(128)(4,1)}), s8[3145728]{0:T(1024)(128)(4,1)S(1)}, s32[]{:S(2)}) async-start(s8[7340032]{0:T(1024)(128)(4,1)} %bitcast.19), calls=%async_computation.3 | async-start | bytes 6291456
  9.2 77.6 %collective-permute-start.1 = (bf16[512,7168]{1,0:T(8,128)(2,1)S(1)}, bf16[512,7168]{1,0:T(8,128)(2,1)S(1)}, u32[]{:S(2)}, u32[]{:S(2)}) collective-permute-start(bf16[512,7168]{1,0:T(8,128)(2,1)S(1)} %bitcast.21), channel_id=1, source_target_pairs={{0,1},{1,0},{2,3},{3,2},{4,5},{5,4},{6,7},{7,6},{8,9},{9,8},{10,11... | collective-permute-start | bytes 22020104 | tf_op jit(solution)/shard_map/ppermute | solution.py:40
  9.8 76.9 %collective-permute-start.2 = (bf16[7168,512]{1,0:T(8,128)(2,1)}, bf16[7168,512]{1,0:T(8,128)(2,1)S(1)}, u32[]{:S(2)}, u32[]{:S(2)}) collective-permute-start(bf16[7168,512]{1,0:T(8,128)(2,1)} %bitcast.30), channel_id=1, source_target_pairs={{0,1},{1,0},{2,3},{3,2},{4,5},{5,4},{6,7},{7,6},{8,9},{9,8},{10,11... | collective-permute-start | bytes 22020104 | tf_op jit(solution)/shard_map/ppermute | solution.py:40
  9.9 76.9 %collective-permute-start.3 = (bf16[7168,512]{1,0:T(8,128)(2,1)}, bf16[7168,512]{1,0:T(8,128)(2,1)S(1)}, u32[]{:S(2)}, u32[]{:S(2)}) collective-permute-start(bf16[7168,512]{1,0:T(8,128)(2,1)} %bitcast.35), channel_id=1, source_target_pairs={{0,1},{1,0},{2,3},{3,2},{4,5},{5,4},{6,7},{7,6},{8,9},{9,8},{10,11... | collective-permute-start | bytes 22020104 | tf_op jit(solution)/shard_map/ppermute | solution.py:40
  90.8 5.4 %collective-permute-start.4 = (f32[768,512]{1,0:T(8,128)S(1)}, f32[768,512]{1,0:T(8,128)S(1)}, u32[]{:S(2)}, u32[]{:S(2)}) collective-permute-start(f32[768,512]{1,0:T(8,128)S(1)} %get-tuple-element.27), channel_id=1, source_target_pairs={{0,1},{1,0},{2,3},{3,2},{4,5},{5,4},{6,7},{7,6},{8,9},{9,8},{10,11... | collective-permute-start | bytes 4718600 | tf_op jit(solution)/shard_map/ppermute | solution.py:40
  92.8 3.4 %copy-start.3 = (bf16[1,768,512]{2,1,0:T(8,128)(2,1)S(1)}, bf16[1,768,512]{2,1,0:T(8,128)(2,1)}, u32[]{:S(2)}) copy-start(bf16[1,768,512]{2,1,0:T(8,128)(2,1)} %param.11) | copy-start | bytes 2359300
  92.8 3.4 %copy-start.4 = (bf16[1,768,512]{2,1,0:T(8,128)(2,1)S(1)}, bf16[1,768,512]{2,1,0:T(8,128)(2,1)}, u32[]{:S(2)}) copy-start(bf16[1,768,512]{2,1,0:T(8,128)(2,1)} %param.12) | copy-start | bytes 2359300
  97.4 3.8 %collective-permute-start.5 = (bf16[768,1152]{1,0:T(8,128)(2,1)S(1)}, bf16[768,1152]{1,0:T(8,128)(2,1)S(1)}, u32[]{:S(2)}, u32[]{:S(2)}) collective-permute-start(bf16[768,1152]{1,0:T(8,128)(2,1)S(1)} %diffs.1.mine_ref), channel_id=1, source_target_pairs={{0,1},{1,0},{2,3},{3,2},{4,5},{5,4},{6,7},{7,6},{8,9},{9,8},{10,11... | collective-permute-start | bytes 5308424 | tf_op jit(solution)/shard_map/ppermute | solution.py:40
  185.9 4.1 %copy-start.2 = (bf16[512,512]{1,0:T(8,128)(2,1)S(1)}, bf16[512,512]{1,0:T(8,128)(2,1)}, u32[]{:S(2)}) copy-start(bf16[512,512]{1,0:T(8,128)(2,1)} %copy-done.1) | copy-start | bytes 1572868
  185.9 4.1 %copy-start.6 = (s32[256,8]{0,1:T(8,128)S(1)}, s32[256,8]{0,1:T(8,128)}, u32[]{:S(2)}) copy-start(s32[256,8]{0,1:T(8,128)} %param.9) | copy-start | bytes 24580
  187.8 5.4 %collective-permute-start.6 = (bf16[128,3584]{1,0:T(8,128)(2,1)S(1)}, bf16[128,3584]{1,0:T(8,128)(2,1)S(1)}, u32[]{:S(2)}, u32[]{:S(2)}) collective-permute-start(bf16[128,3584]{1,0:T(8,128)(2,1)S(1)} %combine_send.1), channel_id=1, source_target_pairs={{0,1},{1,0},{2,3},{3,2},{4,5},{5,4},{6,7},{7,6},{8,9},{9,8},{10,11... | collective-permute-start | bytes 2752520 | tf_op jit(solution)/shard_map/ppermute | solution.py:40

commit v8 on v7

--- a/solution.py
+++ b/solution.py
@@ -419,7 +419,7 @@
 
 
 def keep_kernel(at_ref, ids_ref, pa_ref, pb_ref, w_ref, back_ref, keep_ref, grad_ref):
-    topk, half = ids_ref.shape
+    topk, half = grad_ref.shape
     rows = back_ref.shape[0]
     experts = rows // MAIN
 
@@ -432,10 +432,10 @@
             value = jnp.where(block, column, 0.0).astype(BF16)
             return lax.dot_general(value, slots, (((0,), (0,)), ((), ())), preferred_element_type=F32)
 
-        table = one(score[:, 0:1], pa_ref[...]) + one(score[:, 1:2], pb_ref[...])
+        table = one(score[:, 0:1], pa_ref[:, :half]) + one(score[:, 1:2], pb_ref[:, :half])
         names = iota((experts, half), 0)
         row = iota((topk, half), 0)
-        ids = ids_ref[...]
+        ids = ids_ref[:, pl.ds(pl.multiple_of(at_ref[0] * half, half), half)]
         result = jnp.zeros((topk, half), F32)
         for k in range(topk):
             hit = names == ids[k : k + 1, :]
@@ -449,21 +449,14 @@
 def combine_keep(at, ids_t, pa, pb, w, back):
     topk, tokens = ids_t.shape
     half = tokens // 2
-    rows, lanes = back.shape
-    tile = (lanes - 128) // 6
+    tile = (back.shape[1] - 128) // 6
     whole = pl.BlockSpec(memory_space=pltpu.VMEM)
     return pl.pallas_call(
         keep_kernel,
         grid_spec=pltpu.PrefetchScalarGridSpec(
             num_scalar_prefetch=1,
             grid=(4,),
-            in_specs=[
-                pl.BlockSpec((topk, half), lambda j, at: (0, at[0])),
-                pl.BlockSpec((rows, half), lambda j, at: (0, 0)),
-                pl.BlockSpec((rows, half), lambda j, at: (0, 0)),
-                whole,
-                whole,
-            ],
+            in_specs=[whole] * 5,
             out_specs=[
                 pl.BlockSpec((half, tile), lambda j, at: (0, 4 * at[0] + j)),
                 pl.BlockSpec((topk, half), lambda j, at: (0, 0)),

time: 195 us -> 194 us (level)
  no operation moved by 1% of the time
where the time goes in v8:
time: 194 us
  blocking collectives  148 us (76%)
  Pallas kernels  34.9 us (18%)
  starting transfers between devices  6.93 us (4%)
  local copies, waits for them, and re-layouts  2.83 us (1%)
    all_to_all x2, blocking collectives, exchange(): lax.all_to_all(value.reshape(groups, MAIN, lanes), 'expert', split_axis=0...  148 us
    pallas_call x1, Pallas kernels, inputs(): pl.pallas_call(inputs_kernel, grid_spec=pltpu.PrefetchScalarGridSpec(num_...  12.8 us
    pallas_call x2, Pallas kernels, hidden(): pl.pallas_call(first_kernel if first else hidden_slots, grid_spec=pltpu.P...  7.41 us
    ppermute x7, starting transfers between devices, swap(): return lax.ppermute(value, 'seq', [(0, 1), (1, 0)])  6.93 us
  transfers between devices with their start and end apart: 7, of which 1 were waited for; matrix products, arithmetic and copies ran while one was open for 0% of the time, Pallas kernels for 6%

profile of v8, /device:TPU:1, one launch (start us, length us, event | category | flops | bytes accessed | tf_op | source)
XLA Modules:
  0.0 194.2 jit_solution(12797704547826770850)
XLA Ops:
  0.6 0.0 copy-start
  0.6 0.0 slice-start
  0.7 1.4 constant_dynamic-slice_fusion
  2.1 1.5 collective-permute-start
  3.6 0.0 copy-start.5
  3.6 0.7 copy-done.5
  4.3 0.0 copy-start.7
  4.3 0.7 copy-done.7
  5.0 0.8 routes.1
  5.8 0.0 copy-start.1
  5.8 0.0 collective-permute-done.other_ref
  5.8 0.0 copy-done
  5.8 0.0 slice-start.1
  5.8 3.3 %dispatch.1 = bf16[512,5376]{1,0:T(8,128)(2,1)S(1)} custom-call(s32[1]{0:T(128)} %bitcast.at_ref, bf16[512,256]{1,0:T(8,128)(2,1)S(1)} %get-tuple-element.17.pa_ref, bf16[512,512]{1,0:T(8,128)(2,1)S(1)} %get-tuple-element.18.pb_ref, bf16[128,7168]{1,0:T(8,128)(2,1)S(1)} %copy-done, bf16[128,3584]{1,0:T(8,128)(2,1)S(1)} %collective-permute-done.other_ref), custom_call_target="tpu_custom_call" | custom-call | flops 2000000000 | bytes 8000000 | tf_op jit(solution)/shard_map/dispatch/pallas_call | solution.py:134
  9.2 0.0 copy-done.1
  9.2 0.0 slice-done
  9.2 0.0 slice-done.1
  9.2 0.6 collective-permute-start.1
  9.8 0.1 collective-permute-start.2
  9.9 0.4 collective-permute-start.3
  10.3 76.4 %all_to_all.10 = bf16[64,8,5376]{2,1,0:T(8,128)(2,1)S(1)} all-to-all(bf16[64,8,5376]{2,1,0:T(8,128)(2,1)S(1)} %bitcast.18), channel_id=1, replica_groups=mesh['expert'=64,'seq'=2] {'expert'}, dimensions={0} | all-to-all | bytes 11010048 | tf_op jit(solution)/shard_map/all_to_all | solution.py:502
  86.8 0.0 collective-permute-done.1.w_ref
  86.8 0.0 collective-permute-done.2.og_ref
  86.8 0.0 collective-permute-done.3.ou_ref
  86.8 4.0 %hidden_other.1 = (f32[768,512]{1,0:T(8,128)S(1)}, bf16[256,3584]{1,0:T(8,128)(2,1)S(1)}) custom-call(s32[1]{0:T(128)} %bitcast.at_ref, bf16[512,5376]{1,0:T(8,128)(2,1)S(1)} %bitcast.15, bf16[512,7168]{1,0:T(8,128)(2,1)S(1)} %collective-permute-done.1.w_ref), custom_call_target="tpu_custom_call" | custom-call | tf_op jit(solution)/shard_map/hidden_other/pallas_call | solution.py:195
  90.8 2.0 %collective-permute-start.4 = (f32[768,512]{1,0:T(8,128)S(1)}, f32[768,512]{1,0:T(8,128)S(1)}, u32[]{:S(2)}, u32[]{:S(2)}) collective-permute-start(f32[768,512]{1,0:T(8,128)S(1)} %get-tuple-element.27), channel_id=1, source_target_pairs={{0,1},{1,0},{2,3},{3,2},{4,5},{5,4},{6,7},{7,6},{8,9},{9,8},{10,11... | collective-permute-start | bytes 4718600 | tf_op jit(solution)/shard_map/ppermute | solution.py:40
  92.8 0.0 copy-start.3
  92.8 0.0 copy-start.4
  92.8 3.4 %hidden_own.1.mine_ref = f32[768,512]{1,0:T(8,128)S(1)} custom-call(s32[1]{0:T(128)} %bitcast.at_ref, bf16[512,5376]{1,0:T(8,128)(2,1)S(1)} %bitcast.16, bf16[256,3584]{1,0:T(8,128)(2,1)S(1)} %get-tuple-element.26.rest_ref, bf16[512,7168]{1,0:T(8,128)(2,1)S(1)} %bitcast.22), custom_call_target="tpu_custom_call" | custom-call | tf_op jit(solution)/shard_map/hidden_own/pallas_call | solution.py:195
  96.2 0.0 collective-permute-done.4.other_ref
  96.2 0.0 copy-done.3
  96.2 0.0 copy-done.4
  96.3 1.2 diffs.1.mine_ref
  97.4 0.1 collective-permute-start.5
  97.6 3.3 %early_inputs.1.early_ref = f32[768,1024]{1,0:T(8,128)S(1)} custom-call(s32[1]{0:T(128)} %bitcast.at_ref, bf16[768,1152]{1,0:T(8,128)(2,1)S(1)} %diffs.1.mine_ref, bf16[7168,512]{1,0:T(8,128)(2,1)} %bitcast.31, bf16[7168,512]{1,0:T(8,128)(2,1)} %bitcast.32, bf16[7168,512]{1,0:T(8,128)(2,1)} %bitcast.36, bf16[7168,512]{1,0:T(8,128)(2,1)} %bitcast.37), custom_call_target="tpu_custom_call" | custom-call | flops 1610612736 | bytes 10000000 | tf_op jit(solution)/shard_map/early_inputs/pallas_call | solution.py:292
  100.9 0.3 collective-permute-done.5.other_ref
  101.2 12.8 %inputs.1 = bf16[512,5504]{1,0:T(8,128)(2,1)S(1)} custom-call(s32[1]{0:T(128)} %bitcast.at_ref, bf16[768,1152]{1,0:T(8,128)(2,1)S(1)} %diffs.1.mine_ref, bf16[768,1152]{1,0:T(8,128)(2,1)S(1)} %collective-permute-done.5.other_ref, f32[768,1024]{1,0:T(8,128)S(1)} %early_inputs.1.early_ref, bf16[7168,512]{1,0:T(8,128)(2,1)} %bitcast.33, ...), custom_call_target="tpu_custom_call" | custom-call | flops 11274289152 | bytes 24000000 | tf_op jit(solution)/shard_map/inputs/pallas_call | solution.py:372
  114.0 71.9 %all_to_all.11 = bf16[64,8,5504]{2,1,0:T(8,128)(2,1)S(1)} all-to-all(bf16[64,8,5504]{2,1,0:T(8,128)(2,1)S(1)} %bitcast.17), channel_id=1, replica_groups=mesh['expert'=64,'seq'=2] {'expert'}, dimensions={0} | all-to-all | bytes 11272192 | tf_op jit(solution)/shard_map/all_to_all | solution.py:502
  185.9 0.0 copy-start.2
  185.9 0.0 copy-start.6
  185.9 1.9 combine_send.1
  187.8 2.2 %collective-permute-start.6 = (bf16[128,3584]{1,0:T(8,128)(2,1)S(1)}, bf16[128,3584]{1,0:T(8,128)(2,1)S(1)}, u32[]{:S(2)}, u32[]{:S(2)}) collective-permute-start(bf16[128,3584]{1,0:T(8,128)(2,1)S(1)} %combine_send.1), channel_id=1, source_target_pairs={{0,1},{1,0},{2,3},{3,2},{4,5},{5,4},{6,7},{7,6},{8,9},{9,8},{10,11... | collective-permute-start | bytes 2752520 | tf_op jit(solution)/shard_map/ppermute | solution.py:40
  190.0 0.0 copy-done.2
  190.0 0.0 copy-done.6
  190.0 3.2 %combine_keep.1 = (bf16[128,7168]{1,0:T(8,128)(2,1)}, bf16[8,128]{1,0:T(8,128)(2,1)}) custom-call(s32[1]{0:T(128)} %bitcast.at_ref, s32[8,256]{1,0:T(8,128)S(1)} %bitcast.27, bf16[512,256]{1,0:T(8,128)(2,1)S(1)} %get-tuple-element.17.pa_ref, bf16[512,512]{1,0:T(8,128)(2,1)S(1)} %copy-done.2, bf16[768,512]{1,0:T(8,128)(2,1)S(1)} %get-tuple-element.19.w_ref, ...), custom_call_target="tpu_custom_call" | custom-call | flops 1000000000 | bytes 7000000 | tf_op jit(solution)/shard_map/combine_keep/pallas_call | solution.py:454
  193.2 0.0 collective-permute-done.6.came_ref
  193.2 1.0 join.1
  (1 shorter events, 0.0 us)
Async XLA Ops:
  0.6 5.2 %copy-start = (bf16[128,7168]{1,0:T(8,128)(2,1)S(1)}, bf16[128,7168]{1,0:T(8,128)(2,1)}, u32[]{:S(2)}) copy-start(bf16[128,7168]{1,0:T(8,128)(2,1)} %own_ref.1) | copy-start | bytes 5505028
  0.6 8.5 %slice-start = ((s8[7340032]{0:T(1024)(128)(4,1)}), s8[4194304]{0:T(1024)(128)(4,1)S(1)}, s32[]{:S(2)}) async-start(s8[7340032]{0:T(1024)(128)(4,1)} %bitcast.19), calls=%async_computation.2 | async-start | bytes 8388608
  2.1 3.8 %collective-permute-start = (bf16[128,3584]{1,0:T(8,128)(2,1)S(1)}, bf16[128,3584]{1,0:T(8,128)(2,1)S(1)}, u32[]{:S(2)}, u32[]{:S(2)}) collective-permute-start(bf16[128,3584]{1,0:T(8,128)(2,1)S(1)} %constant_dynamic-slice_fusion), channel_id=1, source_target_pairs={{0,1},{1,0},{2,3},{3,2},{4,5},{5,4},{6,7},{7,6},{8,9},{9,8},{10,11... | collective-permute-start | bytes 2752520 | tf_op jit(solution)/shard_map/ppermute | solution.py:40
  3.6 0.7 copy-start.5
  4.3 0.7 copy-start.7
  5.8 3.4 %copy-start.1 = (bf16[512,512]{1,0:T(8,128)(2,1)}, bf16[512,512]{1,0:T(8,128)(2,1)S(1)}, u32[]{:S(2)}) copy-start(bf16[512,512]{1,0:T(8,128)(2,1)S(1)} %get-tuple-element.18.pb_ref) | copy-start | bytes 1572868
  5.8 3.4 %slice-start.1 = ((s8[7340032]{0:T(1024)(128)(4,1)}), s8[3145728]{0:T(1024)(128)(4,1)S(1)}, s32[]{:S(2)}) async-start(s8[7340032]{0:T(1024)(128)(4,1)} %bitcast.19), calls=%async_computation.3 | async-start | bytes 6291456
  9.2 77.6 %collective-permute-start.1 = (bf16[512,7168]{1,0:T(8,128)(2,1)S(1)}, bf16[512,7168]{1,0:T(8,128)(2,1)S(1)}, u32[]{:S(2)}, u32[]{:S(2)}) collective-permute-start(bf16[512,7168]{1,0:T(8,128)(2,1)S(1)} %bitcast.21), channel_id=1, source_target_pairs={{0,1},{1,0},{2,3},{3,2},{4,5},{5,4},{6,7},{7,6},{8,9},{9,8},{10,11... | collective-permute-start | bytes 22020104 | tf_op jit(solution)/shard_map/ppermute | solution.py:40
  9.8 76.9 %collective-permute-start.2 = (bf16[7168,512]{1,0:T(8,128)(2,1)}, bf16[7168,512]{1,0:T(8,128)(2,1)S(1)}, u32[]{:S(2)}, u32[]{:S(2)}) collective-permute-start(bf16[7168,512]{1,0:T(8,128)(2,1)} %bitcast.30), channel_id=1, source_target_pairs={{0,1},{1,0},{2,3},{3,2},{4,5},{5,4},{6,7},{7,6},{8,9},{9,8},{10,11... | collective-permute-start | bytes 22020104 | tf_op jit(solution)/shard_map/ppermute | solution.py:40
  9.9 76.9 %collective-permute-start.3 = (bf16[7168,512]{1,0:T(8,128)(2,1)}, bf16[7168,512]{1,0:T(8,128)(2,1)S(1)}, u32[]{:S(2)}, u32[]{:S(2)}) collective-permute-start(bf16[7168,512]{1,0:T(8,128)(2,1)} %bitcast.35), channel_id=1, source_target_pairs={{0,1},{1,0},{2,3},{3,2},{4,5},{5,4},{6,7},{7,6},{8,9},{9,8},{10,11... | collective-permute-start | bytes 22020104 | tf_op jit(solution)/shard_map/ppermute | solution.py:40
  90.8 5.4 %collective-permute-start.4 = (f32[768,512]{1,0:T(8,128)S(1)}, f32[768,512]{1,0:T(8,128)S(1)}, u32[]{:S(2)}, u32[]{:S(2)}) collective-permute-start(f32[768,512]{1,0:T(8,128)S(1)} %get-tuple-element.27), channel_id=1, source_target_pairs={{0,1},{1,0},{2,3},{3,2},{4,5},{5,4},{6,7},{7,6},{8,9},{9,8},{10,11... | collective-permute-start | bytes 4718600 | tf_op jit(solution)/shard_map/ppermute | solution.py:40
  92.8 3.4 %copy-start.3 = (bf16[1,768,512]{2,1,0:T(8,128)(2,1)S(1)}, bf16[1,768,512]{2,1,0:T(8,128)(2,1)}, u32[]{:S(2)}) copy-start(bf16[1,768,512]{2,1,0:T(8,128)(2,1)} %param.11) | copy-start | bytes 2359300
  92.8 3.4 %copy-start.4 = (bf16[1,768,512]{2,1,0:T(8,128)(2,1)S(1)}, bf16[1,768,512]{2,1,0:T(8,128)(2,1)}, u32[]{:S(2)}) copy-start(bf16[1,768,512]{2,1,0:T(8,128)(2,1)} %param.12) | copy-start | bytes 2359300
  97.4 3.8 %collective-permute-start.5 = (bf16[768,1152]{1,0:T(8,128)(2,1)S(1)}, bf16[768,1152]{1,0:T(8,128)(2,1)S(1)}, u32[]{:S(2)}, u32[]{:S(2)}) collective-permute-start(bf16[768,1152]{1,0:T(8,128)(2,1)S(1)} %diffs.1.mine_ref), channel_id=1, source_target_pairs={{0,1},{1,0},{2,3},{3,2},{4,5},{5,4},{6,7},{7,6},{8,9},{9,8},{10,11... | collective-permute-start | bytes 5308424 | tf_op jit(solution)/shard_map/ppermute | solution.py:40
  185.9 4.1 %copy-start.2 = (bf16[512,512]{1,0:T(8,128)(2,1)S(1)}, bf16[512,512]{1,0:T(8,128)(2,1)}, u32[]{:S(2)}) copy-start(bf16[512,512]{1,0:T(8,128)(2,1)} %copy-done.1) | copy-start | bytes 1572868
  185.9 4.1 %copy-start.6 = (s32[256,8]{0,1:T(8,128)S(1)}, s32[256,8]{0,1:T(8,128)}, u32[]{:S(2)}) copy-start(s32[256,8]{0,1:T(8,128)} %param.9) | copy-start | bytes 24580
  187.8 5.3 %collective-permute-start.6 = (bf16[128,3584]{1,0:T(8,128)(2,1)S(1)}, bf16[128,3584]{1,0:T(8,128)(2,1)S(1)}, u32[]{:S(2)}, u32[]{:S(2)}) collective-permute-start(bf16[128,3584]{1,0:T(8,128)(2,1)S(1)} %combine_send.1), channel_id=1, source_target_pairs={{0,1},{1,0},{2,3},{3,2},{4,5},{5,4},{6,7},{7,6},{8,9},{9,8},{10,11... | collective-permute-start | bytes 2752520 | tf_op jit(solution)/shard_map/ppermute | solution.py:40

commit v9 on v7

--- a/solution.py
+++ b/solution.py
@@ -110,7 +110,7 @@
 def dispatch_kernel(at_ref, pa_ref, pb_ref, own_ref, other_ref, out_ref):
     step = pl.program_id(0)
     part = other_ref.shape[1]
-    tile = part // 4
+    tile = part // 2
     cols = pl.ds(pl.multiple_of(step * tile, 128), tile)
 
     def tokens(index):
@@ -118,13 +118,13 @@
         other = pl.ds(pl.multiple_of(index * tile, 128), tile)
         return [own_ref[:, own], other_ref[:, other]]
 
-    @pl.when(step < 4)
+    @pl.when(step < 2)
     def _():
         out_ref[:, cols] = dot(pa_ref[...], jnp.concatenate(tokens(step), axis=0)).astype(BF16)
 
-    @pl.when(step >= 4)
-    def _():
-        both = jnp.concatenate(tokens(step - 4) + tokens(step - 2), axis=0)
+    @pl.when(step == 2)
+    def _():
+        both = jnp.concatenate(tokens(0) + tokens(1), axis=0)
         out_ref[:, cols] = dot(pb_ref[...], both).astype(BF16)
 
 
@@ -135,7 +135,7 @@
         dispatch_kernel,
         grid_spec=pltpu.PrefetchScalarGridSpec(
             num_scalar_prefetch=1,
-            grid=(6,),
+            grid=(3,),
             in_specs=[whole] * 4,
             out_specs=whole,
         ),

time: 195 us -> 194 us (level)
  no operation moved by 1% of the time
where the time goes in v9:
time: 194 us; the launch traced here: 193 us
  blocking collectives  148 us (76%)
  Pallas kernels  34.1 us (18%)
  starting transfers between devices  6.92 us (4%)
  local copies, waits for them, and re-layouts  2.83 us (1%)
    all_to_all x2, blocking collectives, exchange(): lax.all_to_all(value.reshape(groups, MAIN, lanes), 'expert', split_axis=0...  148 us
    pallas_call x1, Pallas kernels, inputs(): pl.pallas_call(inputs_kernel, grid_spec=pltpu.PrefetchScalarGridSpec(num_...  12.8 us
    pallas_call x2, Pallas kernels, hidden(): pl.pallas_call(first_kernel if first else hidden_slots, grid_spec=pltpu.P...  7.41 us
    ppermute x7, starting transfers between devices, swap(): return lax.ppermute(value, 'seq', [(0, 1), (1, 0)])  6.92 us
  transfers between devices with their start and end apart: 7, of which 1 were waited for; matrix products, arithmetic and copies ran while one was open for 0% of the time, Pallas kernels for 6%

profile of v9, /device:TPU:1, one launch (start us, length us, event | category | flops | bytes accessed | tf_op | source)
XLA Modules:
  0.0 193.4 jit_solution(12156796519941671847)
XLA Ops:
  0.6 0.0 copy-start
  0.6 0.0 slice-start
  0.7 1.4 constant_dynamic-slice_fusion
  2.1 1.5 collective-permute-start
  3.6 0.0 copy-start.5
  3.6 0.7 copy-done.5
  4.3 0.0 copy-start.7
  4.3 0.7 copy-done.7
  5.0 0.8 routes.1
  5.8 0.0 copy-start.1
  5.8 0.0 collective-permute-done.other_ref
  5.8 0.0 copy-done
  5.8 0.0 slice-start.1
  5.8 2.5 %dispatch.1 = bf16[512,5376]{1,0:T(8,128)(2,1)S(1)} custom-call(s32[1]{0:T(128)} %bitcast.at_ref, bf16[512,256]{1,0:T(8,128)(2,1)S(1)} %get-tuple-element.17.pa_ref, bf16[512,512]{1,0:T(8,128)(2,1)S(1)} %get-tuple-element.18.pb_ref, bf16[128,7168]{1,0:T(8,128)(2,1)S(1)} %copy-done, bf16[128,3584]{1,0:T(8,128)(2,1)S(1)} %collective-permute-done.other_ref), custom_call_target="tpu_custom_call" | custom-call | flops 2000000000 | bytes 8000000 | tf_op jit(solution)/shard_map/dispatch/pallas_call | solution.py:134
  8.3 0.0 copy-done.1
  8.3 0.0 slice-done
  8.4 0.0 slice-done.1
  8.4 0.6 collective-permute-start.1
  9.0 0.1 collective-permute-start.2
  9.1 0.4 collective-permute-start.3
  9.5 76.4 %all_to_all.10 = bf16[64,8,5376]{2,1,0:T(8,128)(2,1)S(1)} all-to-all(bf16[64,8,5376]{2,1,0:T(8,128)(2,1)S(1)} %bitcast.18), channel_id=1, replica_groups=mesh['expert'=64,'seq'=2] {'expert'}, dimensions={0} | all-to-all | bytes 11010048 | tf_op jit(solution)/shard_map/all_to_all | solution.py:509
  85.9 0.0 collective-permute-done.1.w_ref
  85.9 0.0 collective-permute-done.2.og_ref
  85.9 0.0 collective-permute-done.3.ou_ref
  86.0 4.0 %hidden_other.1 = (f32[768,512]{1,0:T(8,128)S(1)}, bf16[256,3584]{1,0:T(8,128)(2,1)S(1)}) custom-call(s32[1]{0:T(128)} %bitcast.at_ref, bf16[512,5376]{1,0:T(8,128)(2,1)S(1)} %bitcast.15, bf16[512,7168]{1,0:T(8,128)(2,1)S(1)} %collective-permute-done.1.w_ref), custom_call_target="tpu_custom_call" | custom-call | tf_op jit(solution)/shard_map/hidden_other/pallas_call | solution.py:195
  90.0 2.0 %collective-permute-start.4 = (f32[768,512]{1,0:T(8,128)S(1)}, f32[768,512]{1,0:T(8,128)S(1)}, u32[]{:S(2)}, u32[]{:S(2)}) collective-permute-start(f32[768,512]{1,0:T(8,128)S(1)} %get-tuple-element.27), channel_id=1, source_target_pairs={{0,1},{1,0},{2,3},{3,2},{4,5},{5,4},{6,7},{7,6},{8,9},{9,8},{10,11... | collective-permute-start | bytes 4718600 | tf_op jit(solution)/shard_map/ppermute | solution.py:40
  92.0 0.0 copy-start.3
  92.0 0.0 copy-start.4
  92.0 3.4 %hidden_own.1.mine_ref = f32[768,512]{1,0:T(8,128)S(1)} custom-call(s32[1]{0:T(128)} %bitcast.at_ref, bf16[512,5376]{1,0:T(8,128)(2,1)S(1)} %bitcast.16, bf16[256,3584]{1,0:T(8,128)(2,1)S(1)} %get-tuple-element.26.rest_ref, bf16[512,7168]{1,0:T(8,128)(2,1)S(1)} %bitcast.22), custom_call_target="tpu_custom_call" | custom-call | tf_op jit(solution)/shard_map/hidden_own/pallas_call | solution.py:195
  95.4 0.0 collective-permute-done.4.other_ref
  95.4 0.0 copy-done.3
  95.4 0.0 copy-done.4
  95.4 1.2 diffs.1.mine_ref
  96.6 0.1 collective-permute-start.5
  96.7 3.3 %early_inputs.1.early_ref = f32[768,1024]{1,0:T(8,128)S(1)} custom-call(s32[1]{0:T(128)} %bitcast.at_ref, bf16[768,1152]{1,0:T(8,128)(2,1)S(1)} %diffs.1.mine_ref, bf16[7168,512]{1,0:T(8,128)(2,1)} %bitcast.31, bf16[7168,512]{1,0:T(8,128)(2,1)} %bitcast.32, bf16[7168,512]{1,0:T(8,128)(2,1)} %bitcast.36, bf16[7168,512]{1,0:T(8,128)(2,1)} %bitcast.37), custom_call_target="tpu_custom_call" | custom-call | flops 1610612736 | bytes 10000000 | tf_op jit(solution)/shard_map/early_inputs/pallas_call | solution.py:292
  100.0 0.4 collective-permute-done.5.other_ref
  100.4 12.8 %inputs.1 = bf16[512,5504]{1,0:T(8,128)(2,1)S(1)} custom-call(s32[1]{0:T(128)} %bitcast.at_ref, bf16[768,1152]{1,0:T(8,128)(2,1)S(1)} %diffs.1.mine_ref, bf16[768,1152]{1,0:T(8,128)(2,1)S(1)} %collective-permute-done.5.other_ref, f32[768,1024]{1,0:T(8,128)S(1)} %early_inputs.1.early_ref, bf16[7168,512]{1,0:T(8,128)(2,1)} %bitcast.33, ...), custom_call_target="tpu_custom_call" | custom-call | flops 11274289152 | bytes 24000000 | tf_op jit(solution)/shard_map/inputs/pallas_call | solution.py:372
  113.2 71.9 %all_to_all.11 = bf16[64,8,5504]{2,1,0:T(8,128)(2,1)S(1)} all-to-all(bf16[64,8,5504]{2,1,0:T(8,128)(2,1)S(1)} %bitcast.17), channel_id=1, replica_groups=mesh['expert'=64,'seq'=2] {'expert'}, dimensions={0} | all-to-all | bytes 11272192 | tf_op jit(solution)/shard_map/all_to_all | solution.py:509
  185.1 0.0 copy-start.2
  185.1 0.0 copy-start.6
  185.1 1.9 combine_send.1
  187.0 2.2 %collective-permute-start.6 = (bf16[128,3584]{1,0:T(8,128)(2,1)S(1)}, bf16[128,3584]{1,0:T(8,128)(2,1)S(1)}, u32[]{:S(2)}, u32[]{:S(2)}) collective-permute-start(bf16[128,3584]{1,0:T(8,128)(2,1)S(1)} %combine_send.1), channel_id=1, source_target_pairs={{0,1},{1,0},{2,3},{3,2},{4,5},{5,4},{6,7},{7,6},{8,9},{9,8},{10,11... | collective-permute-start | bytes 2752520 | tf_op jit(solution)/shard_map/ppermute | solution.py:40
  189.2 0.0 copy-done.2
  189.2 0.0 copy-done.6
  189.2 3.2 %combine_keep.1 = (bf16[128,7168]{1,0:T(8,128)(2,1)}, bf16[8,128]{1,0:T(8,128)(2,1)}) custom-call(s32[1]{0:T(128)} %bitcast.at_ref, s32[8,256]{1,0:T(8,128)S(1)} %bitcast.27, bf16[512,256]{1,0:T(8,128)(2,1)S(1)} %get-tuple-element.17.pa_ref, bf16[512,512]{1,0:T(8,128)(2,1)S(1)} %copy-done.2, bf16[768,512]{1,0:T(8,128)(2,1)S(1)} %get-tuple-element.19.w_ref, ...), custom_call_target="tpu_custom_call" | custom-call | flops 1000000000 | bytes 7000000 | tf_op jit(solution)/shard_map/combine_keep/pallas_call | solution.py:455
  192.4 0.0 collective-permute-done.6.came_ref
  192.4 1.0 join.1
  (1 shorter events, 0.0 us)
Async XLA Ops:
  0.6 5.2 %copy-start = (bf16[128,7168]{1,0:T(8,128)(2,1)S(1)}, bf16[128,7168]{1,0:T(8,128)(2,1)}, u32[]{:S(2)}) copy-start(bf16[128,7168]{1,0:T(8,128)(2,1)} %own_ref.1) | copy-start | bytes 5505028
  0.6 7.7 %slice-start = ((s8[7340032]{0:T(1024)(128)(4,1)}), s8[4194304]{0:T(1024)(128)(4,1)S(1)}, s32[]{:S(2)}) async-start(s8[7340032]{0:T(1024)(128)(4,1)} %bitcast.19), calls=%async_computation.2 | async-start | bytes 8388608
  2.1 3.8 %collective-permute-start = (bf16[128,3584]{1,0:T(8,128)(2,1)S(1)}, bf16[128,3584]{1,0:T(8,128)(2,1)S(1)}, u32[]{:S(2)}, u32[]{:S(2)}) collective-permute-start(bf16[128,3584]{1,0:T(8,128)(2,1)S(1)} %constant_dynamic-slice_fusion), channel_id=1, source_target_pairs={{0,1},{1,0},{2,3},{3,2},{4,5},{5,4},{6,7},{7,6},{8,9},{9,8},{10,11... | collective-permute-start | bytes 2752520 | tf_op jit(solution)/shard_map/ppermute | solution.py:40
  3.6 0.7 copy-start.5
  4.3 0.7 copy-start.7
  5.8 2.5 %copy-start.1 = (bf16[512,512]{1,0:T(8,128)(2,1)}, bf16[512,512]{1,0:T(8,128)(2,1)S(1)}, u32[]{:S(2)}) copy-start(bf16[512,512]{1,0:T(8,128)(2,1)S(1)} %get-tuple-element.18.pb_ref) | copy-start | bytes 1572868
  5.8 2.5 %slice-start.1 = ((s8[7340032]{0:T(1024)(128)(4,1)}), s8[3145728]{0:T(1024)(128)(4,1)S(1)}, s32[]{:S(2)}) async-start(s8[7340032]{0:T(1024)(128)(4,1)} %bitcast.19), calls=%async_computation.3 | async-start | bytes 6291456
  8.4 77.6 %collective-permute-start.1 = (bf16[512,7168]{1,0:T(8,128)(2,1)S(1)}, bf16[512,7168]{1,0:T(8,128)(2,1)S(1)}, u32[]{:S(2)}, u32[]{:S(2)}) collective-permute-start(bf16[512,7168]{1,0:T(8,128)(2,1)S(1)} %bitcast.21), channel_id=1, source_target_pairs={{0,1},{1,0},{2,3},{3,2},{4,5},{5,4},{6,7},{7,6},{8,9},{9,8},{10,11... | collective-permute-start | bytes 22020104 | tf_op jit(solution)/shard_map/ppermute | solution.py:40
  9.0 76.9 %collective-permute-start.2 = (bf16[7168,512]{1,0:T(8,128)(2,1)}, bf16[7168,512]{1,0:T(8,128)(2,1)S(1)}, u32[]{:S(2)}, u32[]{:S(2)}) collective-permute-start(bf16[7168,512]{1,0:T(8,128)(2,1)} %bitcast.30), channel_id=1, source_target_pairs={{0,1},{1,0},{2,3},{3,2},{4,5},{5,4},{6,7},{7,6},{8,9},{9,8},{10,11... | collective-permute-start | bytes 22020104 | tf_op jit(solution)/shard_map/ppermute | solution.py:40
  9.1 76.9 %collective-permute-start.3 = (bf16[7168,512]{1,0:T(8,128)(2,1)}, bf16[7168,512]{1,0:T(8,128)(2,1)S(1)}, u32[]{:S(2)}, u32[]{:S(2)}) collective-permute-start(bf16[7168,512]{1,0:T(8,128)(2,1)} %bitcast.35), channel_id=1, source_target_pairs={{0,1},{1,0},{2,3},{3,2},{4,5},{5,4},{6,7},{7,6},{8,9},{9,8},{10,11... | collective-permute-start | bytes 22020104 | tf_op jit(solution)/shard_map/ppermute | solution.py:40
  90.0 5.4 %collective-permute-start.4 = (f32[768,512]{1,0:T(8,128)S(1)}, f32[768,512]{1,0:T(8,128)S(1)}, u32[]{:S(2)}, u32[]{:S(2)}) collective-permute-start(f32[768,512]{1,0:T(8,128)S(1)} %get-tuple-element.27), channel_id=1, source_target_pairs={{0,1},{1,0},{2,3},{3,2},{4,5},{5,4},{6,7},{7,6},{8,9},{9,8},{10,11... | collective-permute-start | bytes 4718600 | tf_op jit(solution)/shard_map/ppermute | solution.py:40
  92.0 3.4 %copy-start.3 = (bf16[1,768,512]{2,1,0:T(8,128)(2,1)S(1)}, bf16[1,768,512]{2,1,0:T(8,128)(2,1)}, u32[]{:S(2)}) copy-start(bf16[1,768,512]{2,1,0:T(8,128)(2,1)} %param.11) | copy-start | bytes 2359300
  92.0 3.4 %copy-start.4 = (bf16[1,768,512]{2,1,0:T(8,128)(2,1)S(1)}, bf16[1,768,512]{2,1,0:T(8,128)(2,1)}, u32[]{:S(2)}) copy-start(bf16[1,768,512]{2,1,0:T(8,128)(2,1)} %param.12) | copy-start | bytes 2359300
  96.6 3.8 %collective-permute-start.5 = (bf16[768,1152]{1,0:T(8,128)(2,1)S(1)}, bf16[768,1152]{1,0:T(8,128)(2,1)S(1)}, u32[]{:S(2)}, u32[]{:S(2)}) collective-permute-start(bf16[768,1152]{1,0:T(8,128)(2,1)S(1)} %diffs.1.mine_ref), channel_id=1, source_target_pairs={{0,1},{1,0},{2,3},{3,2},{4,5},{5,4},{6,7},{7,6},{8,9},{9,8},{10,11... | collective-permute-start | bytes 5308424 | tf_op jit(solution)/shard_map/ppermute | solution.py:40
  185.1 4.1 %copy-start.2 = (bf16[512,512]{1,0:T(8,128)(2,1)S(1)}, bf16[512,512]{1,0:T(8,128)(2,1)}, u32[]{:S(2)}) copy-start(bf16[512,512]{1,0:T(8,128)(2,1)} %copy-done.1) | copy-start | bytes 1572868
  185.1 4.1 %copy-start.6 = (s32[256,8]{0,1:T(8,128)S(1)}, s32[256,8]{0,1:T(8,128)}, u32[]{:S(2)}) copy-start(s32[256,8]{0,1:T(8,128)} %param.9) | copy-start | bytes 24580
  187.0 5.4 %collective-permute-start.6 = (bf16[128,3584]{1,0:T(8,128)(2,1)S(1)}, bf16[128,3584]{1,0:T(8,128)(2,1)S(1)}, u32[]{:S(2)}, u32[]{:S(2)}) collective-permute-start(bf16[128,3584]{1,0:T(8,128)(2,1)S(1)} %combine_send.1), channel_id=1, source_target_pairs={{0,1},{1,0},{2,3},{3,2},{4,5},{5,4},{6,7},{7,6},{8,9},{9,8},{10,11... | collective-permute-start | bytes 2752520 | tf_op jit(solution)/shard_map/ppermute | solution.py:40
